TPU v7x, 32 devices: a whole 2x2x4 slice. The times are simulated.
32 devices in a mesh: rep: 2 (over y), node: 4 (over x, core), local: 4 (over z).
Axes of the slice: x: 2, y: 2, z: 4, core: 2. Of those that a mesh axis runs over, the one named last changes fastest.
Arguments:
- grad_out: bfloat16 [1024, 3584], P(('rep', 'node', 'local')), parts along dimension 0, may hold values from -6 to 6
- routes: int32 [1024, 8], P(('rep', 'node', 'local')), parts along dimension 0, may hold values from 0 to 15, as said below
- combine: bfloat16 [1024, 8], P(('rep', 'node', 'local')), parts along dimension 0, may hold values from 0.049804688 to 1
- hidden_cache: bfloat16 [32, 256, 1024], P(('rep', 'node', 'local')), parts along dimension 0, may hold values from -0.1875 to 0.1875
- down_weight: bfloat16 [16, 1024, 3584], P(('node', 'local')), may hold values from -0.09375 to 0.09375
Outputs:
- d_hidden: bfloat16 [32, 256, 1024], P(('rep', 'node', 'local')), parts along dimension 0
- d_combine: float32 [1024, 8], P(('rep', 'node', 'local')), parts along dimension 0
There are 2 independent parts, one for each index of `rep`. A program takes and returns all parts, laid end to end along the dimension named above; an argument that names none is the same for every part. Nothing has to cross between parts.
Inputs may be any that keep to these rules, and one draw needn't show every extreme that they name: `routes`: each token names 8 different experts lying in exactly 4 node groups (expert e lies in node group e // 4), 2 in each group. The tokens of one device name each node group exactly 32 * 4 // 4 times and each expert exactly 16 times.
All inputs are finite; a program needn't handle non-finite values.
Results may differ from a plain program's by a relative error of at most 0.0055.
Values may be sent and summed in bfloat16 or wider, within the bound.
No kernel may reach another device: no remote copies, remote signals or barrier semaphores. Data moves between devices by JAX's collectives and lax.ppermute only.
A program may use at most 64 MiB of HBM per device.

v0:
```python
import jax
import jax.numpy as jnp
from jax import lax
from jax.sharding import PartitionSpec as P

TOPNODES = 4


def slot_tables(routes, combine, experts_all, capacity):
    onehot = (routes[:, :, None] == lax.iota(jnp.int32, experts_all)[None, None, :]).astype(
        jnp.float32
    )
    hit_mask = jnp.sum(onehot, axis=1)
    weight_te = jnp.einsum("tke,tk->te", onehot, combine.astype(jnp.float32))
    slot_rank = jnp.cumsum(hit_mask, axis=0) - hit_mask
    select = hit_mask[:, :, None] * (
        slot_rank[:, :, None] == lax.iota(jnp.float32, capacity)[None, None, :]
    ).astype(jnp.float32)
    return (onehot, hit_mask, select, select * weight_te[:, :, None])


def per_device(grad_out, routes, combine, hidden_cache, down_weight):
    node_count = lax.axis_size("node")
    local_count = lax.axis_size("local")
    experts_all = node_count * local_count
    slots_all = hidden_cache.shape[1]
    capacity = slots_all // experts_all
    tok_rows = grad_out.shape[0]
    width = grad_out.shape[1]
    onehot, hit_mask, select, scaled = slot_tables(routes, combine, experts_all, capacity)
    per_node = tok_rows * TOPNODES // node_count
    node_hit = jnp.max(hit_mask.reshape(tok_rows, node_count, local_count), axis=2)
    node_rank = jnp.cumsum(node_hit, axis=0) - node_hit
    placement = node_hit[:, :, None] * (
        node_rank[:, :, None] == lax.iota(jnp.float32, per_node)[None, None, :]
    ).astype(jnp.float32)
    node_rows = jnp.einsum(
        "tnm,td->nmd", placement.astype(jnp.bfloat16), grad_out, preferred_element_type=jnp.float32
    ).astype(jnp.bfloat16)
    weight_table = jnp.einsum(
        "tnm,tnq->nmq", placement, scaled.reshape(tok_rows, node_count, local_count * capacity)
    ).astype(jnp.bfloat16)
    node_rows, weight_table = (
        lax.all_to_all(node_rows, "node", split_axis=0, concat_axis=0, tiled=True),
        lax.all_to_all(weight_table, "node", split_axis=0, concat_axis=0, tiled=True),
    )
    fan_mask = (weight_table != 0).astype(jnp.bfloat16)
    row_block = jnp.einsum(
        "nmq,nmd->nqd", fan_mask, node_rows, preferred_element_type=jnp.float32
    ).astype(jnp.bfloat16)
    weights = jnp.sum(weight_table.astype(jnp.float32), axis=1).astype(jnp.bfloat16)
    row_block = row_block.reshape(node_count, local_count, capacity, width)
    weights = weights.reshape(node_count, local_count, capacity)
    row_block, weights = (
        lax.all_to_all(row_block, "local", split_axis=1, concat_axis=1, tiled=True),
        lax.all_to_all(weights, "local", split_axis=1, concat_axis=1, tiled=True),
    )
    flat_rows = row_block.reshape(slots_all, width)
    products = lax.dot_general(
        flat_rows, down_weight[0], (((1,), (1,)), ((), ())), preferred_element_type=jnp.float32
    )
    d_hidden = (weights.reshape(slots_all, 1).astype(jnp.float32) * products).astype(jnp.bfloat16)[
        None
    ]
    slot_terms = jnp.sum(products * hidden_cache[0].astype(jnp.float32), axis=1)
    slot_terms = slot_terms.reshape(node_count, local_count, capacity)
    returned = lax.all_to_all(
        lax.all_to_all(slot_terms, "node", split_axis=0, concat_axis=0, tiled=True),
        "local",
        split_axis=1,
        concat_axis=1,
        tiled=True,
    )
    returned = returned.reshape(experts_all, capacity)
    per_expert = jnp.einsum("tec,ec->te", select, returned)
    d_combine = jnp.einsum("tke,te->tk", onehot, per_expert)
    return (d_hidden, d_combine)


def solution(mesh):
    placed = (
        P(("rep", "node", "local"), None),
        P(("rep", "node", "local"), None),
        P(("rep", "node", "local"), None),
        P(("rep", "node", "local"), None, None),
        P(("node", "local"), None, None),
    )
    return jax.shard_map(
        per_device,
        mesh=mesh,
        in_specs=placed,
        out_specs=(P(("rep", "node", "local"), None, None), P(("rep", "node", "local"), None)),
        check_vma=False,
    )
```

profile of v0, /device:TPU:0, one launch (start us, length us, event | category | flops | bytes accessed | tf_op | source)
XLA Modules:
  0.0 105.3 jit_solution(5660182493972155483)
XLA Ops:
  0.6 0.0 copy-start
  0.7 0.1 eq.59
  0.7 0.7 convert.7
  1.5 0.7 select_reduce_fusion.1
  2.2 0.1 copy.43
  2.3 0.1 copy.40
  2.4 0.1 reduce_window_sum.23
  2.4 0.1 copy.45
  2.5 0.1 reduce_window_sum.22
  2.5 0.1 copy.42
  2.7 0.1 bitcast_multiply_fusion
  2.8 0.1 convolution_convert_fusion.2
  2.9 0.7 reshape.77
  3.6 4.2 %all-to-all-start = ((bf16[4,2,1024]{2,1,0:T(2,128)(2,1)}), bf16[4,2,1024]{2,1,0:T(2,128)(2,1)S(1)}, u32[]{:S(2)}, u32[]{:S(2)}) async-start(bf16[4,2,1024]{2,1,0:T(2,128)(2,1)} %reshape.77), calls=%async_computation | async-start | bytes 32768 | tf_op jit(solution)/shard_map/all_to_all | solution.py:45
  7.9 0.0 copy-done
  7.9 1.3 %convolution_convert_fusion.1 = bf16[4,32,3584]{2,1,0:T(8,128)(2,1)} fusion(bf16[32,3584]{1,0:T(8,128)(2,1)S(1)} %copy-done, f32[32,4]{0,1:T(4,128)S(1)} %reduce_max.9, f32[32,4]{0,1:T(4,128)S(1)} %copy.42), kind=kOutput, calls=%fused_computation.3 | convolution fusion | flops 29827072 | bytes 1147904 | tf_op jit(solution)/shard_map/tnm,td->nmd/dot_general | solution.py:37
  9.2 2.5 %all-to-all-done = bf16[4,2,1024]{2,1,0:T(2,128)(2,1)S(1)} async-done(((bf16[4,2,1024]{2,1,0:T(2,128)(2,1)}), bf16[4,2,1024]{2,1,0:T(2,128)(2,1)S(1)}, u32[]{:S(2)}, u32[]{:S(2)}) %all-to-all-start) | async-done | bytes 16416 | tf_op jit(solution)/shard_map/all_to_all | solution.py:45
  11.7 3.5 %all-to-all-start.2 = ((bf16[4,32,3584]{2,1,0:T(8,128)(2,1)}), bf16[4,32,3584]{2,1,0:T(8,128)(2,1)S(1)}, u32[]{:S(2)}, u32[]{:S(2)}) async-start(bf16[4,32,3584]{2,1,0:T(8,128)(2,1)} %convolution_convert_fusion.1), calls=%async_computation.2 | async-start | bytes 1835008 | tf_op jit(solution)/shard_map/all_to_all | solution.py:44
  15.2 0.1 reshape.78
  15.3 0.1 reshape.63
  15.4 0.6 copy.47
  16.0 12.2 %all-to-all-done.2 = bf16[4,32,3584]{2,1,0:T(8,128)(2,1)S(1)} async-done(((bf16[4,32,3584]{2,1,0:T(8,128)(2,1)}), bf16[4,32,3584]{2,1,0:T(8,128)(2,1)S(1)}, u32[]{:S(2)}, u32[]{:S(2)}) %all-to-all-start.2) | async-done | bytes 917536 | tf_op jit(solution)/shard_map/all_to_all | solution.py:44
  28.2 5.3 %all-to-all-start.1 = ((bf16[4,4,16]{2,0,1:T(4,128)(2,1)}), bf16[4,4,16]{2,0,1:T(4,128)(2,1)S(1)}, u32[]{:S(2)}, u32[]{:S(2)}) async-start(bf16[4,4,16]{2,0,1:T(4,128)(2,1)} %copy.47), calls=%async_computation.1 | async-start | bytes 8192 | tf_op jit(solution)/shard_map/all_to_all | solution.py:56
  33.6 0.7 convolution_convert_fusion
  34.3 1.4 %copy.49 = bf16[4,4,16,3584]{3,2,0,1:T(8,128)(2,1)} copy(bf16[4,4,16,3584]{3,2,1,0:T(8,128)(2,1)S(1)} %bitcast.46) | data formatting | bytes 3670016 | tf_op jit(solution)/shard_map/reshape | solution.py:52
  35.7 3.5 %all-to-all-done.1 = bf16[4,4,16]{2,0,1:T(4,128)(2,1)S(1)} async-done(((bf16[4,4,16]{2,0,1:T(4,128)(2,1)}), bf16[4,4,16]{2,0,1:T(4,128)(2,1)S(1)}, u32[]{:S(2)}, u32[]{:S(2)}) %all-to-all-start.1) | async-done | bytes 544 | tf_op jit(solution)/shard_map/all_to_all | solution.py:56
  39.2 3.6 %all-to-all-start.3 = ((bf16[4,4,16,3584]{3,2,0,1:T(8,128)(2,1)}), bf16[4,4,16,3584]{3,2,0,1:T(8,128)(2,1)S(1)}, u32[]{:S(2)}, u32[]{:S(2)}) async-start(bf16[4,4,16,3584]{3,2,0,1:T(8,128)(2,1)} %copy.49), calls=%async_computation.3 | async-start | bytes 3670016 | tf_op jit(solution)/shard_map/all_to_all | solution.py:55
  42.8 0.1 reshape.68
  42.8 0.0 copy-start.2
  42.9 41.1 %all-to-all-done.3 = bf16[4,4,16,3584]{3,2,0,1:T(8,128)(2,1)S(1)} async-done(((bf16[4,4,16,3584]{3,2,0,1:T(8,128)(2,1)}), bf16[4,4,16,3584]{3,2,0,1:T(8,128)(2,1)S(1)}, u32[]{:S(2)}, u32[]{:S(2)}) %all-to-all-start.3) | async-done | bytes 1835040 | tf_op jit(solution)/shard_map/all_to_all | solution.py:55
  83.9 0.1 copy.50
  84.1 0.0 copy-done.2
  84.1 0.0 copy-start.1
  84.1 6.1 %fusion.2 = (f32[256]{0:T(256)S(1)}, bf16[1,256,1024]{2,1,0:T(8,128)(2,1)}) fusion(bf16[1,256,1024]{2,1,0:T(8,128)(2,1)S(1)} %copy-done.2, f32[256]{0:T(256)S(1)} %reshape.68, bf16[256,3584]{1,0:T(8,128)(2,1)S(1)} %bitcast.47, bf16[1,1024,3584]{2,1,0:T(8,128)(2,1)} %param.9), kind=kOutput, calls=%fused_computation.6 | convolution fusion | flops 1880358656 | bytes 10225664 | tf_op jit(solution)/shard_map/dot_general | solution.py:59
  90.2 0.1 reshape.66
  90.3 6.1 %all_to_all.30 = f32[4,4,16]{2,1,0:T(4,128)S(1)} all-to-all(f32[4,4,16]{2,1,0:T(4,128)S(1)} %reshape.66), channel_id=1, replica_groups=mesh['rep'=2,'node'=4,'local'=4] {'node'}, dimensions={0} | all-to-all | bytes 2048 | tf_op jit(solution)/shard_map/all_to_all | solution.py:68
  96.4 8.1 %all_to_all.31 = f32[4,4,16]{2,0,1:T(4,128)S(1)} all-to-all(f32[4,4,16]{2,0,1:T(4,128)S(1)} %copy.51), channel_id=1, replica_groups=mesh['rep'=2,'node'=4,'local'=4] {'local'}, dimensions={1} | all-to-all | bytes 2048 | tf_op jit(solution)/shard_map/all_to_all | solution.py:67
  104.5 0.1 fusion.5
  104.7 0.0 copy-done.1
  104.7 0.6 select_reduce_fusion
  (11 shorter events, 0.1 us)
Async XLA Ops:
  0.6 7.2 %copy-start = (bf16[32,3584]{1,0:T(8,128)(2,1)S(1)}, bf16[32,3584]{1,0:T(8,128)(2,1)}, u32[]{:S(2)}) copy-start(bf16[32,3584]{1,0:T(8,128)(2,1)} %param.5) | copy-start | bytes 688132
  3.6 8.1 %all-to-all-start = ((bf16[4,2,1024]{2,1,0:T(2,128)(2,1)}), bf16[4,2,1024]{2,1,0:T(2,128)(2,1)S(1)}, u32[]{:S(2)}, u32[]{:S(2)}) async-start(bf16[4,2,1024]{2,1,0:T(2,128)(2,1)} %reshape.77), calls=%async_computation | async-start | bytes 32768 | tf_op jit(solution)/shard_map/all_to_all | solution.py:45
  11.7 16.5 %all-to-all-start.2 = ((bf16[4,32,3584]{2,1,0:T(8,128)(2,1)}), bf16[4,32,3584]{2,1,0:T(8,128)(2,1)S(1)}, u32[]{:S(2)}, u32[]{:S(2)}) async-start(bf16[4,32,3584]{2,1,0:T(8,128)(2,1)} %convolution_convert_fusion.1), calls=%async_computation.2 | async-start | bytes 1835008 | tf_op jit(solution)/shard_map/all_to_all | solution.py:44
  28.2 10.9 %all-to-all-start.1 = ((bf16[4,4,16]{2,0,1:T(4,128)(2,1)}), bf16[4,4,16]{2,0,1:T(4,128)(2,1)S(1)}, u32[]{:S(2)}, u32[]{:S(2)}) async-start(bf16[4,4,16]{2,0,1:T(4,128)(2,1)} %copy.47), calls=%async_computation.1 | async-start | bytes 8192 | tf_op jit(solution)/shard_map/all_to_all | solution.py:56
  39.2 44.8 %all-to-all-start.3 = ((bf16[4,4,16,3584]{3,2,0,1:T(8,128)(2,1)}), bf16[4,4,16,3584]{3,2,0,1:T(8,128)(2,1)S(1)}, u32[]{:S(2)}, u32[]{:S(2)}) async-start(bf16[4,4,16,3584]{3,2,0,1:T(8,128)(2,1)} %copy.49), calls=%async_computation.3 | async-start | bytes 3670016 | tf_op jit(solution)/shard_map/all_to_all | solution.py:55
  42.8 41.2 %copy-start.2 = (bf16[1,256,1024]{2,1,0:T(8,128)(2,1)S(1)}, bf16[1,256,1024]{2,1,0:T(8,128)(2,1)}, u32[]{:S(2)}) copy-start(bf16[1,256,1024]{2,1,0:T(8,128)(2,1)} %param.8) | copy-start | bytes 1572868
  84.1 20.6 %copy-start.1 = (s32[32,8]{0,1:T(8,128)S(1)}, s32[32,8]{0,1:T(8,128)}, u32[]{:S(2)}) copy-start(s32[32,8]{0,1:T(8,128)} %param.6) | copy-start | bytes 3076
where the time goes:
time: 106 us; the launch traced here: 105 us
  waiting for transfers between devices  59.4 us (56%)
  starting transfers between devices  16.6 us (16%)
  blocking collectives  14.3 us (13%)
  matrix products  8.36 us (8%)
  local copies, waits for them, and re-layouts  3.65 us (3%)
  other arithmetic  2.3 us (2%)
    all_to_all x1, waiting for transfers between devices, per_device(): lax.all_to_all(row_block, 'local', split_axis=1, concat_axis=1, tiled=True)  41.1 us
    all_to_all x1, waiting for transfers between devices, per_device(): lax.all_to_all(node_rows, 'node', split_axis=0, concat_axis=0, tiled=True)  12.2 us
    all_to_all x1, blocking collectives, per_device(): lax.all_to_all(lax.all_to_all(slot_terms, 'node', split_axis=0, concat_ax...  8.11 us
    all_to_all x1, blocking collectives, per_device(): lax.all_to_all(slot_terms, 'node', split_axis=0, concat_axis=0, tiled=True)  6.14 us
    dot_general x1, matrix products, per_device(): lax.dot_general(flat_rows, down_weight[0], (((1,), (1,)), ((), ())), pref...  6.09 us
    all_to_all x1, starting transfers between devices, per_device(): lax.all_to_all(weights, 'local', split_axis=1, concat_axis=1, tiled=True)  5.34 us
    all_to_all x1, starting transfers between devices, per_device(): lax.all_to_all(weight_table, 'node', split_axis=0, concat_axis=0, tiled=T...  4.21 us
    all_to_all x1, starting transfers between devices, per_device(): lax.all_to_all(row_block, 'local', split_axis=1, concat_axis=1, tiled=True)  3.58 us
  transfers between devices with their start and end apart: 4, of which 4 were waited for; matrix products, arithmetic and copies ran while one was open for 4% of the time, Pallas kernels for 0%

commit v1 on v0

--- a/solution.py
+++ b/solution.py
@@ -1,6 +1,10 @@
+import functools
+
 import jax
 import jax.numpy as jnp
 from jax import lax
+from jax.experimental import pallas as pl
+from jax.experimental.pallas import tpu as pltpu
 from jax.sharding import PartitionSpec as P
 
 TOPNODES = 4
@@ -19,7 +23,7 @@
     return (onehot, hit_mask, select, select * weight_te[:, :, None])
 
 
-def per_device(grad_out, routes, combine, hidden_cache, down_weight):
+def routed(grad_out, routes, combine, hidden_cache, down_weight):
     node_count = lax.axis_size("node")
     local_count = lax.axis_size("local")
     experts_all = node_count * local_count
@@ -77,6 +81,213 @@
     return (d_hidden, d_combine)
 
 
+LANES = 128
+HIGH = 64 * 1024 * 1024
+
+
+def xor_pairs(nodes, locals_, node_mask, local_mask):
+    return [
+        (n * locals_ + l, (n ^ node_mask) * locals_ + (l ^ local_mask))
+        for n in range(nodes)
+        for l in range(locals_)
+    ]
+
+
+def pack_kernel(rows_ref, routes_ref, combine_ref, out_ref):
+    width = rows_ref.shape[1]
+    top, tokens = routes_ref.shape
+    copies = LANES // tokens
+    table = jnp.concatenate(
+        [routes_ref[...].astype(jnp.float32), combine_ref[...].astype(jnp.float32)], axis=0
+    )
+    table = jnp.concatenate([table] * copies, axis=1)
+    fill = jnp.zeros((rows_ref.shape[0] - 2 * top, LANES), jnp.float32)
+    out_ref[:, :width] = rows_ref[...]
+    out_ref[:, width:] = jnp.concatenate([table, fill], axis=0).astype(out_ref.dtype)
+
+
+def expert_kernel(groups, members, place_ref, *refs):
+    count = groups * members
+    blocks = refs[:count]
+    weight_ref, cache_ref, out_ref = refs[count : count + 3]
+    term_refs = refs[count + 3 : count + 3 + groups]
+    picked, inner, cache_rows = refs[count + 3 + groups :]
+    width = weight_ref.shape[1]
+    hidden = weight_ref.shape[0]
+    tokens = blocks[0].shape[0]
+    top = tokens // 4
+    capacity = cache_ref.shape[0] // count
+    expert = place_ref[0].astype(jnp.float32)
+    span = members * tokens
+    lane = lax.broadcasted_iota(jnp.int32, (1, span), 1)
+    owner = lane // tokens
+    earlier = lax.broadcasted_iota(jnp.int32, (span, span), 0)
+    later = lax.broadcasted_iota(jnp.int32, (span, span), 1)
+    before = ((earlier < later) & (earlier // tokens == later // tokens)).astype(jnp.bfloat16)
+    slot_of = lax.broadcasted_iota(jnp.int32, (members * capacity, span), 0).astype(jnp.float32)
+    chosen = []
+    scales = []
+    for j in range(groups):
+        mine = blocks[j * members : (j + 1) * members]
+        table = jnp.zeros((2 * top, span), jnp.float32)
+        for i in range(members):
+            part = mine[i][: 2 * top, width:].astype(jnp.float32)
+            table = jnp.where(owner == i, part, table)
+        match = (table[:top] == expert).astype(jnp.float32)
+        hit = jnp.sum(match, axis=0, keepdims=True)
+        scale = jnp.sum(match * table[top:], axis=0, keepdims=True)
+        rank = jnp.dot(
+            jnp.broadcast_to(hit, (top, span)).astype(jnp.bfloat16),
+            before,
+            preferred_element_type=jnp.float32,
+        )[:1]
+        target = rank + (owner * capacity).astype(jnp.float32)
+        choose = jnp.where((slot_of == target) & (hit > 0), jnp.float32(1), jnp.float32(0))
+        chosen.append(choose)
+        scales.append(jnp.sum(choose * scale, axis=1, keepdims=True))
+        source_rows = jnp.concatenate([mine[i][:, :width] for i in range(members)], axis=0)
+        at = j * members * capacity
+        picked[at : at + members * capacity, :] = jnp.dot(
+            choose.astype(jnp.bfloat16), source_rows, preferred_element_type=jnp.float32
+        ).astype(jnp.bfloat16)
+        for i in range(members):
+            start = pl.multiple_of(place_ref[1 + j * members + i], capacity)
+            cache_rows[at + i * capacity : at + (i + 1) * capacity, :] = cache_ref[
+                pl.ds(start, capacity), :
+            ]
+    step = 256
+    for f in range(0, hidden, step):
+        inner[:, f : f + step] = lax.dot_general(
+            picked[...],
+            weight_ref[f : f + step, :],
+            (((1,), (1,)), ((), ())),
+            preferred_element_type=jnp.float32,
+        )
+    for j in range(groups):
+        at = j * members * capacity
+        products = inner[at : at + members * capacity, :]
+        terms = jnp.sum(
+            products * cache_rows[at : at + members * capacity, :].astype(jnp.float32),
+            axis=1,
+            keepdims=True,
+        )
+        term_refs[j][...] = jnp.sum(chosen[j] * terms, axis=0, keepdims=True)
+        scaled = (scales[j] * products).astype(out_ref.dtype)
+        for i in range(members):
+            start = pl.multiple_of(place_ref[1 + j * members + i], capacity)
+            out_ref[pl.ds(start, capacity), :] = scaled[i * capacity : (i + 1) * capacity]
+
+
+def finish_kernel(place_ref, routes_ref, *refs):
+    out_ref = refs[-1]
+    returned = refs[:-1]
+    top, tokens = routes_ref.shape
+    groups = returned[0].shape[0]
+    total = jnp.zeros((top, tokens), jnp.float32)
+    routes = routes_ref[...]
+    for i in range(len(returned)):
+        mine = returned[i][:, i * tokens : (i + 1) * tokens]
+        for j in range(groups):
+            expert = place_ref[i * groups + j]
+            total = total + jnp.where(routes == expert, mine[j : j + 1, :], jnp.float32(0))
+    out_ref[...] = total
+
+
+def exchanged(grad_out, routes, combine, hidden_cache, down_weight):
+    nodes = lax.axis_size("node")
+    locals_ = lax.axis_size("local")
+    sources = nodes * locals_
+    tokens, width = grad_out.shape
+    hidden = down_weight.shape[1]
+    slots = hidden_cache.shape[1]
+    capacity = slots // sources
+    axes = ("node", "local")
+    node = lax.axis_index("node")
+    local = lax.axis_index("local")
+    vmem = pl.BlockSpec(memory_space=pltpu.VMEM)
+    smem = pl.BlockSpec(memory_space=pltpu.SMEM)
+    params = pltpu.CompilerParams(vmem_limit_bytes=HIGH * 3 // 4)
+
+    def move(x, node_mask, local_mask):
+        return lax.ppermute(x, axes, xor_pairs(nodes, locals_, node_mask, local_mask))
+
+    routes_t = routes.T
+    block = pl.pallas_call(
+        pack_kernel,
+        out_shape=jax.ShapeDtypeStruct((tokens, width + LANES), grad_out.dtype),
+        in_specs=[vmem] * 3,
+        out_specs=vmem,
+    )(grad_out, routes_t, combine.T)
+
+    far = [block] + [move(block, 0, j) for j in range(1, locals_)]
+    blocks = []
+    for j in range(locals_):
+        held = [far[j]]
+        bit = nodes // 2
+        found = {0: far[j]}
+        while bit:
+            for at in list(found):
+                found[at ^ bit] = move(found[at], bit, 0)
+            bit //= 2
+        blocks += [found[i] for i in range(nodes)]
+
+    starts = [
+        ((node ^ i) * locals_ + (local ^ j)) * capacity for j in range(locals_) for i in range(nodes)
+    ]
+    place = jnp.stack([node * locals_ + local] + starts).astype(jnp.int32)
+    results = pl.pallas_call(
+        functools.partial(expert_kernel, locals_, nodes),
+        out_shape=[jax.ShapeDtypeStruct((slots, hidden), jnp.bfloat16)]
+        + [jax.ShapeDtypeStruct((1, nodes * tokens), jnp.float32)] * locals_,
+        in_specs=[smem] + [vmem] * (sources + 2),
+        out_specs=[vmem] * (1 + locals_),
+        scratch_shapes=[
+            pltpu.VMEM((slots, width), jnp.bfloat16),
+            pltpu.VMEM((slots, hidden), jnp.float32),
+            pltpu.VMEM((slots, hidden), jnp.bfloat16),
+        ],
+        compiler_params=params,
+        cost_estimate=pl.CostEstimate(
+            flops=2 * slots * width * hidden * 2, bytes_accessed=2 * hidden * width, transcendentals=0
+        ),
+    )(place, *blocks, down_weight[0], hidden_cache[0])
+    d_hidden, terms = results[0], results[1:]
+    back = jnp.concatenate(
+        [terms[0]] + [move(terms[j], 0, j) for j in range(1, locals_)], axis=0
+    )
+    returned = [back] + [move(back, i, 0) for i in range(1, nodes)]
+    experts = [
+        (node ^ i) * locals_ + (local ^ j) for i in range(nodes) for j in range(locals_)
+    ]
+    d_combine_t = pl.pallas_call(
+        finish_kernel,
+        out_shape=jax.ShapeDtypeStruct(routes_t.shape, jnp.float32),
+        in_specs=[smem] + [vmem] * (1 + nodes),
+        out_specs=vmem,
+    )(jnp.stack(experts).astype(jnp.int32), routes_t, *returned)
+    return d_hidden[None], d_combine_t.T
+
+
+def power_of_two(n):
+    return n & (n - 1) == 0
+
+
+def per_device(grad_out, routes, combine, hidden_cache, down_weight):
+    nodes = lax.axis_size("node")
+    locals_ = lax.axis_size("local")
+    tokens, top = routes.shape
+    if (
+        nodes == TOPNODES
+        and power_of_two(nodes)
+        and power_of_two(locals_)
+        and nodes * tokens == LANES
+        and tokens == 4 * top
+        and locals_ <= 8
+    ):
+        return exchanged(grad_out, routes, combine, hidden_cache, down_weight)
+    return routed(grad_out, routes, combine, hidden_cache, down_weight)
+
+
 def solution(mesh):
     placed = (
         P(("rep", "node", "local"), None),

time: 106 us -> 67.1 us (0.63)
  waiting for transfers between devices: 59.4 us -> 33 us
  blocking collectives: 14.3 us -> 0 us
  Pallas kernels: 0 us -> 10.5 us
  matrix products: 8.36 us -> 0 us
  other arithmetic: 2.3 us -> 0.01 us
  starting transfers between devices: 16.6 us -> 18.6 us
    all_to_all x4 -> x0, waiting for transfers between devices: 59.4 us -> none  [the longest x1 41.1 us: per_device(): lax.all_to_all(row_block, 'local', split_axis=1, concat_axis=1, tiled=True)]
    ppermute x0 -> x21, waiting for transfers between devices: none -> 33 us  [move(): lax.ppermute(x, axes, xor_pairs(nodes, locals_, node_mask, local_mask))]
    ppermute x0 -> x21, starting transfers between devices: none -> 18.6 us  [move(): lax.ppermute(x, axes, xor_pairs(nodes, locals_, node_mask, local_mask))]
    all_to_all x4 -> x0, starting transfers between devices: 16.6 us -> none  [the longest x1 5.34 us: per_device(): lax.all_to_all(weights, 'local', split_axis=1, concat_axis=1, tiled=True)]
    all_to_all x2 -> x0, blocking collectives: 14.3 us -> none  [the longest x1 8.11 us: per_device(): lax.all_to_all(lax.all_to_all(slot_terms, 'node', split_axis=0, concat_ax...]
    pallas_call x0 -> x3, Pallas kernels: none -> 10.5 us  [the longest x1 7.32 us: exchanged(): pl.pallas_call(functools.partial(expert_kernel, locals_, nodes), out_shap...]
    dot_general x5 -> x0, matrix products: 8.36 us -> none  [the longest x1 6.09 us: per_device(): lax.dot_general(flat_rows, down_weight[0], (((1,), (1,)), ((), ())), pref...]
    unnamed x8 -> x12, local copies, waits for them, and re-layouts: 0.84 us -> 3.14 us
  transfers between devices with their start and end apart: 4 -> 21, of which waited for: 4 -> 9; matrix products, arithmetic and copies ran while one was open for 4% -> 1% of each run, Pallas kernels for 0% -> 0%
where the time goes in v1:
time: 67.1 us; the launch traced here: 66.8 us
  waiting for transfers between devices  33 us (49%)
  starting transfers between devices  18.6 us (28%)
  Pallas kernels  10.5 us (16%)
  local copies, waits for them, and re-layouts  3.92 us (6%)
  between operations  0.72 us (1%)
    ppermute x21, waiting for transfers between devices, move(): lax.ppermute(x, axes, xor_pairs(nodes, locals_, node_mask, local_mask))  33 us
    ppermute x21, starting transfers between devices, move(): lax.ppermute(x, axes, xor_pairs(nodes, locals_, node_mask, local_mask))  18.6 us
    pallas_call x1, Pallas kernels, exchanged(): pl.pallas_call(functools.partial(expert_kernel, locals_, nodes), out_shap...  7.32 us
    unnamed x12, local copies, waits for them, and re-layouts  3.14 us
    pallas_call x1, Pallas kernels, exchanged(): pl.pallas_call(pack_kernel, out_shape=jax.ShapeDtypeStruct((tokens, width...  1.72 us
    pallas_call x1, Pallas kernels, exchanged(): pl.pallas_call(finish_kernel, out_shape=jax.ShapeDtypeStruct(routes_t.sha...  1.48 us
  transfers between devices with their start and end apart: 21, of which 9 were waited for; matrix products, arithmetic and copies ran while one was open for 1% of the time, Pallas kernels for 0%

profile of v1, /device:TPU:0, one launch (start us, length us, event | category | flops | bytes accessed | tf_op | source)
XLA Modules:
  0.0 66.8 jit_solution(166888859964457342)
XLA Ops:
  0.6 1.7 %shard_map.68.refs_0_ = bf16[32,3712]{1,0:T(8,128)(2,1)} custom-call(bf16[32,3584]{1,0:T(8,128)(2,1)} %rows_ref.1, s32[8,32]{1,0:T(8,128)} %bitcast.39, bf16[8,32]{1,0:T(8,128)(2,1)} %bitcast.42), custom_call_target="tpu_custom_call" | custom-call | tf_op jit(solution)/shard_map/pallas_call | solution.py:215
  2.4 5.0 %collective-permute-start.11 = (bf16[32,3712]{1,0:T(8,128)(2,1)}, bf16[32,3712]{1,0:T(8,128)(2,1)S(1)}, u32[]{:S(2)}, u32[]{:S(2)}) collective-permute-start(bf16[32,3712]{1,0:T(8,128)(2,1)} %shard_map.68.refs_0_), channel_id=1, source_target_pairs={{0,3},{1,2},{2,1},{3,0},{4,7},{5,6},{6,5},{7,4},{8,11},{9,10},{10,... | collective-permute-start | bytes 712712 | tf_op jit(solution)/shard_map/ppermute | solution.py:212
  7.4 0.0 collective-permute-start.7
  7.4 0.6 collective-permute-start.3
  8.0 1.7 %collective-permute-start.1 = (bf16[32,3712]{1,0:T(8,128)(2,1)}, bf16[32,3712]{1,0:T(8,128)(2,1)S(1)}, u32[]{:S(2)}, u32[]{:S(2)}) collective-permute-start(bf16[32,3712]{1,0:T(8,128)(2,1)} %shard_map.68.refs_0_), channel_id=1, source_target_pairs={{0,8},{1,9},{2,10},{3,11},{4,12},{5,13},{6,14},{7,15},{8,0},{9,1},... | collective-permute-start | bytes 712712 | tf_op jit(solution)/shard_map/ppermute | solution.py:212
  9.7 0.0 collective-permute-start
  9.7 4.7 %collective-permute-done.11.refs_12_ = bf16[32,3712]{1,0:T(8,128)(2,1)S(1)} collective-permute-done((bf16[32,3712]{1,0:T(8,128)(2,1)}, bf16[32,3712]{1,0:T(8,128)(2,1)S(1)}, u32[]{:S(2)}, u32[]{:S(2)}) %collective-permute-start.11) | collective-permute-done | bytes 237600 | tf_op jit(solution)/shard_map/ppermute | solution.py:212
  14.4 1.7 %collective-permute-start.13 = (bf16[32,3712]{1,0:T(8,128)(2,1)S(1)}, bf16[32,3712]{1,0:T(8,128)(2,1)S(1)}, u32[]{:S(2)}, u32[]{:S(2)}) collective-permute-start(bf16[32,3712]{1,0:T(8,128)(2,1)S(1)} %collective-permute-done.11.refs_12_), channel_id=1, source_target_pairs={{0,8},{1,9},{2,10},{3,11},{4,12},{5,13},{6,14},{7,15},{8,0},{9,1},... | collective-permute-start | bytes 712712 | tf_op jit(solution)/shard_map/ppermute | solution.py:212
  16.1 11.8 %collective-permute-done.7.refs_8_ = bf16[32,3712]{1,0:T(8,128)(2,1)S(1)} collective-permute-done((bf16[32,3712]{1,0:T(8,128)(2,1)}, bf16[32,3712]{1,0:T(8,128)(2,1)S(1)}, u32[]{:S(2)}, u32[]{:S(2)}) %collective-permute-start.7) | collective-permute-done | bytes 237600 | tf_op jit(solution)/shard_map/ppermute | solution.py:212
  27.8 0.0 collective-permute-start.12
  27.8 0.0 collective-permute-done.3.refs_4_
  27.8 1.5 %collective-permute-start.9 = (bf16[32,3712]{1,0:T(8,128)(2,1)S(1)}, bf16[32,3712]{1,0:T(8,128)(2,1)S(1)}, u32[]{:S(2)}, u32[]{:S(2)}) collective-permute-start(bf16[32,3712]{1,0:T(8,128)(2,1)S(1)} %collective-permute-done.7.refs_8_), channel_id=1, source_target_pairs={{0,8},{1,9},{2,10},{3,11},{4,12},{5,13},{6,14},{7,15},{8,0},{9,1},... | collective-permute-start | bytes 712712 | tf_op jit(solution)/shard_map/ppermute | solution.py:212
  29.3 0.0 collective-permute-done.1.refs_2_
  29.3 0.2 collective-permute-start.8
  29.5 0.0 collective-permute-done.refs_1_
  29.5 0.5 collective-permute-start.5
  30.1 0.0 collective-permute-done.13.refs_14_
  30.1 0.0 collective-permute-start.4
  30.1 0.0 collective-permute-done.12.refs_13_
  30.1 0.5 collective-permute-start.2
  30.6 5.8 %collective-permute-done.9.refs_10_ = bf16[32,3712]{1,0:T(8,128)(2,1)S(1)} collective-permute-done((bf16[32,3712]{1,0:T(8,128)(2,1)S(1)}, bf16[32,3712]{1,0:T(8,128)(2,1)S(1)}, u32[]{:S(2)}, u32[]{:S(2)}) %collective-permute-start.9) | collective-permute-done | bytes 237600 | tf_op jit(solution)/shard_map/ppermute | solution.py:212
  36.4 0.0 collective-permute-start.14
  36.4 0.0 collective-permute-done.8.refs_9_
  36.4 0.5 collective-permute-start.10
  36.9 4.2 %collective-permute-done.5.refs_6_ = bf16[32,3712]{1,0:T(8,128)(2,1)S(1)} collective-permute-done((bf16[32,3712]{1,0:T(8,128)(2,1)S(1)}, bf16[32,3712]{1,0:T(8,128)(2,1)S(1)}, u32[]{:S(2)}, u32[]{:S(2)}) %collective-permute-start.5) | collective-permute-done | bytes 237600 | tf_op jit(solution)/shard_map/ppermute | solution.py:212
  41.1 0.0 collective-permute-start.6
  41.1 0.1 stack.120.place_ref
  41.2 0.0 collective-permute-done.2.refs_3_
  41.2 0.0 collective-permute-done.14.refs_15_
  41.2 1.5 %collective-permute-done.6.refs_7_ = bf16[32,3712]{1,0:T(8,128)(2,1)} collective-permute-done((bf16[32,3712]{1,0:T(8,128)(2,1)S(1)}, bf16[32,3712]{1,0:T(8,128)(2,1)}, u32[]{:S(2)}, u32[]{:S(2)}) %collective-permute-start.6) | collective-permute-done | bytes 237600 | tf_op jit(solution)/shard_map/ppermute | solution.py:212
  42.7 0.9 %copy-done = bf16[32,3712]{1,0:T(8,128)(2,1)S(1)} copy-done((bf16[32,3712]{1,0:T(8,128)(2,1)S(1)}, bf16[32,3712]{1,0:T(8,128)(2,1)}, u32[]{:S(2)}) %copy-start) | copy-done | bytes 237592
  43.7 1.0 %copy-done.1 = bf16[1,256,1024]{2,1,0:T(8,128)(2,1)S(1)} copy-done((bf16[1,256,1024]{2,1,0:T(8,128)(2,1)S(1)}, bf16[1,256,1024]{2,1,0:T(8,128)(2,1)}, u32[]{:S(2)}) %copy-start.1) | copy-done | bytes 524312
  44.7 7.3 %shard_map.69 = (bf16[256,1024]{1,0:T(8,128)(2,1)}, f32[1,128]{1,0:T(1,128)S(1)}, f32[1,128]{1,0:T(1,128)S(1)}, f32[1,128]{1,0:T(1,128)S(1)}, f32[1,128]{1,0:T(1,128)S(1)}) custom-call(s32[17]{0:T(128)S(1)} %stack.120.place_ref, bf16[32,3712]{1,0:T(8,128)(2,1)S(1)} %copy-done, bf16[32,3712]{1,0:T(8,128)(2,1)S(1)} %collective-permute-done.refs_1_, ...), custom_call_target="tpu_custom_call" | custom-call | flops 3758096384 | bytes 7340032 | tf_op jit(solution)/shard_map/pallas_call | solution.py:238
  52.0 0.0 collective-permute-start.15
  52.0 3.0 %collective-permute-start.16 = (f32[1,128]{1,0:T(1,128)S(1)}, f32[1,128]{1,0:T(1,128)S(1)}, u32[]{:S(2)}, u32[]{:S(2)}) collective-permute-start(f32[1,128]{1,0:T(1,128)S(1)} %get-tuple-element.10), channel_id=1, source_target_pairs={{0,2},{1,3},{2,0},{3,1},{4,6},{5,7},{6,4},{7,5},{8,10},{9,11},{10,... | collective-permute-start | bytes 1544 | tf_op jit(solution)/shard_map/ppermute | solution.py:212
  55.1 1.4 %collective-permute-start.17 = (f32[1,128]{1,0:T(1,128)S(1)}, f32[1,128]{1,0:T(1,128)S(1)}, u32[]{:S(2)}, u32[]{:S(2)}) collective-permute-start(f32[1,128]{1,0:T(1,128)S(1)} %get-tuple-element.11), channel_id=1, source_target_pairs={{0,3},{1,2},{2,1},{3,0},{4,7},{5,6},{6,5},{7,4},{8,11},{9,10},{10,... | collective-permute-start | bytes 1544 | tf_op jit(solution)/shard_map/ppermute | solution.py:212
  56.4 0.0 collective-permute-done.15
  56.4 0.2 collective-permute-done.16
  56.6 3.8 %collective-permute-done.17 = f32[1,128]{1,0:T(1,128)S(1)} collective-permute-done((f32[1,128]{1,0:T(1,128)S(1)}, f32[1,128]{1,0:T(1,128)S(1)}, u32[]{:S(2)}, u32[]{:S(2)}) %collective-permute-start.17) | collective-permute-done | bytes 544 | tf_op jit(solution)/shard_map/ppermute | solution.py:212
  60.4 0.1 collective-permute-start.20
  60.5 1.6 %collective-permute-start.19 = (f32[4,128]{1,0:T(4,128)S(1)}, f32[4,128]{1,0:T(4,128)S(1)}, u32[]{:S(2)}, u32[]{:S(2)}) collective-permute-start(f32[4,128]{1,0:T(4,128)S(1)} %pad_maximum_fusion.refs_0_), channel_id=1, source_target_pairs={{0,8},{1,9},{2,10},{3,11},{4,12},{5,13},{6,14},{7,15},{8,0},{9,1},... | collective-permute-start | bytes 6152 | tf_op jit(solution)/shard_map/ppermute | solution.py:212
  62.1 0.3 collective-permute-start.18
  62.4 0.7 %stack.136.place_ref = s32[16]{0:T(128)} concatenate(s32[1]{0:T(128)} %bitcast, s32[1]{0:T(128)} %bitcast.22, s32[1]{0:T(128)} %bitcast.23, s32[1]{0:T(128)} %bitcast.24, s32[1]{0:T(128)} %bitcast.25, s32[1]{0:T(128)} %bitcast.26, s32[1]{0:T(128)} %bitcast.27, s32[1]{0:T(128)} %bitcast.28, s32[1]{0:T(128)} %bitcast.29, s32[1]{0:T(128)} %bitcast.30, s32[1]{0:T(128)} %bitcast.31, ...), dimensions={0} | concatenate | bytes 128 | tf_op jit(solution)/shard_map/stack | solution.py:267
  63.1 0.5 collective-permute-done.20.refs_3_
  63.5 0.7 collective-permute-done.19.refs_2_
  64.2 0.6 copy-done.4
  64.7 0.6 copy-done.5
  65.3 1.5 %shard_map.70 = f32[8,32]{1,0:T(8,128)} custom-call(s32[16]{0:T(128)} %stack.136.place_ref, s32[8,32]{1,0:T(8,128)} %bitcast.40, f32[4,128]{1,0:T(4,128)} %copy-done.2, f32[4,128]{1,0:T(4,128)} %copy-done.5, f32[4,128]{1,0:T(4,128)} %copy-done.4, f32[4,128]{1,0:T(4,128)} %copy-done.3), custom_call_target="tpu_custom_call" | custom-call | tf_op jit(solution)/shard_map/pallas_call | solution.py:262
  (12 shorter events, 0.0 us)
Async XLA Ops:
  2.4 12.0 %collective-permute-start.11 = (bf16[32,3712]{1,0:T(8,128)(2,1)}, bf16[32,3712]{1,0:T(8,128)(2,1)S(1)}, u32[]{:S(2)}, u32[]{:S(2)}) collective-permute-start(bf16[32,3712]{1,0:T(8,128)(2,1)} %shard_map.68.refs_0_), channel_id=1, source_target_pairs={{0,3},{1,2},{2,1},{3,0},{4,7},{5,6},{6,5},{7,4},{8,11},{9,10},{10,... | collective-permute-start | bytes 712712 | tf_op jit(solution)/shard_map/ppermute | solution.py:212
  7.4 20.4 %collective-permute-start.7 = (bf16[32,3712]{1,0:T(8,128)(2,1)}, bf16[32,3712]{1,0:T(8,128)(2,1)S(1)}, u32[]{:S(2)}, u32[]{:S(2)}) collective-permute-start(bf16[32,3712]{1,0:T(8,128)(2,1)} %shard_map.68.refs_0_), channel_id=1, source_target_pairs={{0,2},{1,3},{2,0},{3,1},{4,6},{5,7},{6,4},{7,5},{8,10},{9,11},{10,... | collective-permute-start | bytes 712712 | tf_op jit(solution)/shard_map/ppermute | solution.py:212
  7.4 20.4 %collective-permute-start.3 = (bf16[32,3712]{1,0:T(8,128)(2,1)}, bf16[32,3712]{1,0:T(8,128)(2,1)S(1)}, u32[]{:S(2)}, u32[]{:S(2)}) collective-permute-start(bf16[32,3712]{1,0:T(8,128)(2,1)} %shard_map.68.refs_0_), channel_id=1, source_target_pairs={{0,1},{1,0},{2,3},{3,2},{4,5},{5,4},{6,7},{7,6},{8,9},{9,8},{10,11... | collective-permute-start | bytes 712712 | tf_op jit(solution)/shard_map/ppermute | solution.py:212
  8.0 21.3 %collective-permute-start.1 = (bf16[32,3712]{1,0:T(8,128)(2,1)}, bf16[32,3712]{1,0:T(8,128)(2,1)S(1)}, u32[]{:S(2)}, u32[]{:S(2)}) collective-permute-start(bf16[32,3712]{1,0:T(8,128)(2,1)} %shard_map.68.refs_0_), channel_id=1, source_target_pairs={{0,8},{1,9},{2,10},{3,11},{4,12},{5,13},{6,14},{7,15},{8,0},{9,1},... | collective-permute-start | bytes 712712 | tf_op jit(solution)/shard_map/ppermute | solution.py:212
  9.7 19.9 %collective-permute-start = (bf16[32,3712]{1,0:T(8,128)(2,1)}, bf16[32,3712]{1,0:T(8,128)(2,1)S(1)}, u32[]{:S(2)}, u32[]{:S(2)}) collective-permute-start(bf16[32,3712]{1,0:T(8,128)(2,1)} %shard_map.68.refs_0_), channel_id=1, source_target_pairs={{0,4},{1,5},{2,6},{3,7},{4,0},{5,1},{6,2},{7,3},{8,12},{9,13},{10,... | collective-permute-start | bytes 712712 | tf_op jit(solution)/shard_map/ppermute | solution.py:212
  14.4 15.7 %collective-permute-start.13 = (bf16[32,3712]{1,0:T(8,128)(2,1)S(1)}, bf16[32,3712]{1,0:T(8,128)(2,1)S(1)}, u32[]{:S(2)}, u32[]{:S(2)}) collective-permute-start(bf16[32,3712]{1,0:T(8,128)(2,1)S(1)} %collective-permute-done.11.refs_12_), channel_id=1, source_target_pairs={{0,8},{1,9},{2,10},{3,11},{4,12},{5,13},{6,14},{7,15},{8,0},{9,1},... | collective-permute-start | bytes 712712 | tf_op jit(solution)/shard_map/ppermute | solution.py:212
  27.8 2.3 %collective-permute-start.12 = (bf16[32,3712]{1,0:T(8,128)(2,1)S(1)}, bf16[32,3712]{1,0:T(8,128)(2,1)S(1)}, u32[]{:S(2)}, u32[]{:S(2)}) collective-permute-start(bf16[32,3712]{1,0:T(8,128)(2,1)S(1)} %collective-permute-done.11.refs_12_), channel_id=1, source_target_pairs={{0,4},{1,5},{2,6},{3,7},{4,0},{5,1},{6,2},{7,3},{8,12},{9,13},{10,... | collective-permute-start | bytes 712712 | tf_op jit(solution)/shard_map/ppermute | solution.py:212
  27.8 8.6 %collective-permute-start.9 = (bf16[32,3712]{1,0:T(8,128)(2,1)S(1)}, bf16[32,3712]{1,0:T(8,128)(2,1)S(1)}, u32[]{:S(2)}, u32[]{:S(2)}) collective-permute-start(bf16[32,3712]{1,0:T(8,128)(2,1)S(1)} %collective-permute-done.7.refs_8_), channel_id=1, source_target_pairs={{0,8},{1,9},{2,10},{3,11},{4,12},{5,13},{6,14},{7,15},{8,0},{9,1},... | collective-permute-start | bytes 712712 | tf_op jit(solution)/shard_map/ppermute | solution.py:212
  29.3 7.1 %collective-permute-start.8 = (bf16[32,3712]{1,0:T(8,128)(2,1)S(1)}, bf16[32,3712]{1,0:T(8,128)(2,1)S(1)}, u32[]{:S(2)}, u32[]{:S(2)}) collective-permute-start(bf16[32,3712]{1,0:T(8,128)(2,1)S(1)} %collective-permute-done.7.refs_8_), channel_id=1, source_target_pairs={{0,4},{1,5},{2,6},{3,7},{4,0},{5,1},{6,2},{7,3},{8,12},{9,13},{10,... | collective-permute-start | bytes 712712 | tf_op jit(solution)/shard_map/ppermute | solution.py:212
  29.5 11.6 %collective-permute-start.5 = (bf16[32,3712]{1,0:T(8,128)(2,1)S(1)}, bf16[32,3712]{1,0:T(8,128)(2,1)S(1)}, u32[]{:S(2)}, u32[]{:S(2)}) collective-permute-start(bf16[32,3712]{1,0:T(8,128)(2,1)S(1)} %collective-permute-done.3.refs_4_), channel_id=1, source_target_pairs={{0,8},{1,9},{2,10},{3,11},{4,12},{5,13},{6,14},{7,15},{8,0},{9,1},... | collective-permute-start | bytes 712712 | tf_op jit(solution)/shard_map/ppermute | solution.py:212
  30.1 11.1 %collective-permute-start.4 = (bf16[32,3712]{1,0:T(8,128)(2,1)S(1)}, bf16[32,3712]{1,0:T(8,128)(2,1)S(1)}, u32[]{:S(2)}, u32[]{:S(2)}) collective-permute-start(bf16[32,3712]{1,0:T(8,128)(2,1)S(1)} %collective-permute-done.3.refs_4_), channel_id=1, source_target_pairs={{0,4},{1,5},{2,6},{3,7},{4,0},{5,1},{6,2},{7,3},{8,12},{9,13},{10,... | collective-permute-start | bytes 712712 | tf_op jit(solution)/shard_map/ppermute | solution.py:212
  30.1 11.1 %collective-permute-start.2 = (bf16[32,3712]{1,0:T(8,128)(2,1)S(1)}, bf16[32,3712]{1,0:T(8,128)(2,1)S(1)}, u32[]{:S(2)}, u32[]{:S(2)}) collective-permute-start(bf16[32,3712]{1,0:T(8,128)(2,1)S(1)} %collective-permute-done.1.refs_2_), channel_id=1, source_target_pairs={{0,4},{1,5},{2,6},{3,7},{4,0},{5,1},{6,2},{7,3},{8,12},{9,13},{10,... | collective-permute-start | bytes 712712 | tf_op jit(solution)/shard_map/ppermute | solution.py:212
  36.4 4.8 %collective-permute-start.14 = (bf16[32,3712]{1,0:T(8,128)(2,1)S(1)}, bf16[32,3712]{1,0:T(8,128)(2,1)S(1)}, u32[]{:S(2)}, u32[]{:S(2)}) collective-permute-start(bf16[32,3712]{1,0:T(8,128)(2,1)S(1)} %collective-permute-done.13.refs_14_), channel_id=1, source_target_pairs={{0,4},{1,5},{2,6},{3,7},{4,0},{5,1},{6,2},{7,3},{8,12},{9,13},{10,... | collective-permute-start | bytes 712712 | tf_op jit(solution)/shard_map/ppermute | solution.py:212
  36.4 4.8 %collective-permute-start.10 = (bf16[32,3712]{1,0:T(8,128)(2,1)S(1)}, bf16[32,3712]{1,0:T(8,128)(2,1)S(1)}, u32[]{:S(2)}, u32[]{:S(2)}) collective-permute-start(bf16[32,3712]{1,0:T(8,128)(2,1)S(1)} %collective-permute-done.9.refs_10_), channel_id=1, source_target_pairs={{0,4},{1,5},{2,6},{3,7},{4,0},{5,1},{6,2},{7,3},{8,12},{9,13},{10,... | collective-permute-start | bytes 712712 | tf_op jit(solution)/shard_map/ppermute | solution.py:212
  41.1 1.6 %collective-permute-start.6 = (bf16[32,3712]{1,0:T(8,128)(2,1)S(1)}, bf16[32,3712]{1,0:T(8,128)(2,1)}, u32[]{:S(2)}, u32[]{:S(2)}) collective-permute-start(bf16[32,3712]{1,0:T(8,128)(2,1)S(1)} %collective-permute-done.5.refs_6_), channel_id=1, source_target_pairs={{0,4},{1,5},{2,6},{3,7},{4,0},{5,1},{6,2},{7,3},{8,12},{9,13},{10,... | collective-permute-start | bytes 712712 | tf_op jit(solution)/shard_map/ppermute | solution.py:212
  42.7 0.9 %copy-start = (bf16[32,3712]{1,0:T(8,128)(2,1)S(1)}, bf16[32,3712]{1,0:T(8,128)(2,1)}, u32[]{:S(2)}) copy-start(bf16[32,3712]{1,0:T(8,128)(2,1)} %shard_map.68.refs_0_) | copy-start | bytes 712708
  43.7 1.0 %copy-start.1 = (bf16[1,256,1024]{2,1,0:T(8,128)(2,1)S(1)}, bf16[1,256,1024]{2,1,0:T(8,128)(2,1)}, u32[]{:S(2)}) copy-start(bf16[1,256,1024]{2,1,0:T(8,128)(2,1)} %param.8) | copy-start | bytes 1572868
  52.0 4.4 %collective-permute-start.15 = (f32[1,128]{1,0:T(1,128)S(1)}, f32[1,128]{1,0:T(1,128)S(1)}, u32[]{:S(2)}, u32[]{:S(2)}) collective-permute-start(f32[1,128]{1,0:T(1,128)S(1)} %get-tuple-element.9), channel_id=1, source_target_pairs={{0,1},{1,0},{2,3},{3,2},{4,5},{5,4},{6,7},{7,6},{8,9},{9,8},{10,11... | collective-permute-start | bytes 1544 | tf_op jit(solution)/shard_map/ppermute | solution.py:212
  52.0 4.5 %collective-permute-start.16 = (f32[1,128]{1,0:T(1,128)S(1)}, f32[1,128]{1,0:T(1,128)S(1)}, u32[]{:S(2)}, u32[]{:S(2)}) collective-permute-start(f32[1,128]{1,0:T(1,128)S(1)} %get-tuple-element.10), channel_id=1, source_target_pairs={{0,2},{1,3},{2,0},{3,1},{4,6},{5,7},{6,4},{7,5},{8,10},{9,11},{10,... | collective-permute-start | bytes 1544 | tf_op jit(solution)/shard_map/ppermute | solution.py:212
  55.1 5.3 %collective-permute-start.17 = (f32[1,128]{1,0:T(1,128)S(1)}, f32[1,128]{1,0:T(1,128)S(1)}, u32[]{:S(2)}, u32[]{:S(2)}) collective-permute-start(f32[1,128]{1,0:T(1,128)S(1)} %get-tuple-element.11), channel_id=1, source_target_pairs={{0,3},{1,2},{2,1},{3,0},{4,7},{5,6},{6,5},{7,4},{8,11},{9,10},{10,... | collective-permute-start | bytes 1544 | tf_op jit(solution)/shard_map/ppermute | solution.py:212
  60.4 3.7 %copy-start.2 = (f32[4,128]{1,0:T(4,128)}, f32[4,128]{1,0:T(4,128)S(1)}, u32[]{:S(2)}) copy-start(f32[4,128]{1,0:T(4,128)S(1)} %pad_maximum_fusion.refs_0_) | copy-start | bytes 6148
  60.4 3.1 %collective-permute-start.20 = (f32[4,128]{1,0:T(4,128)S(1)}, f32[4,128]{1,0:T(4,128)S(1)}, u32[]{:S(2)}, u32[]{:S(2)}) collective-permute-start(f32[4,128]{1,0:T(4,128)S(1)} %pad_maximum_fusion.refs_0_), channel_id=1, source_target_pairs={{0,12},{1,13},{2,14},{3,15},{4,8},{5,9},{6,10},{7,11},{8,4},{9,5},... | collective-permute-start | bytes 6152 | tf_op jit(solution)/shard_map/ppermute | solution.py:212
  60.5 3.7 %collective-permute-start.19 = (f32[4,128]{1,0:T(4,128)S(1)}, f32[4,128]{1,0:T(4,128)S(1)}, u32[]{:S(2)}, u32[]{:S(2)}) collective-permute-start(f32[4,128]{1,0:T(4,128)S(1)} %pad_maximum_fusion.refs_0_), channel_id=1, source_target_pairs={{0,8},{1,9},{2,10},{3,11},{4,12},{5,13},{6,14},{7,15},{8,0},{9,1},... | collective-permute-start | bytes 6152 | tf_op jit(solution)/shard_map/ppermute | solution.py:212
  62.1 2.1 %collective-permute-start.18 = (f32[4,128]{1,0:T(4,128)S(1)}, f32[4,128]{1,0:T(4,128)S(1)}, u32[]{:S(2)}, u32[]{:S(2)}) collective-permute-start(f32[4,128]{1,0:T(4,128)S(1)} %pad_maximum_fusion.refs_0_), channel_id=1, source_target_pairs={{0,4},{1,5},{2,6},{3,7},{4,0},{5,1},{6,2},{7,3},{8,12},{9,13},{10,... | collective-permute-start | bytes 6152 | tf_op jit(solution)/shard_map/ppermute | solution.py:212
  63.5 0.7 copy-start.3
  64.2 0.6 copy-start.4
  64.7 0.6 copy-start.5

commit v2 on v0

--- a/solution.py
+++ b/solution.py
@@ -1,6 +1,10 @@
+import functools
+
 import jax
 import jax.numpy as jnp
 from jax import lax
+from jax.experimental import pallas as pl
+from jax.experimental.pallas import tpu as pltpu
 from jax.sharding import PartitionSpec as P
 
 TOPNODES = 4
@@ -19,7 +23,7 @@
     return (onehot, hit_mask, select, select * weight_te[:, :, None])
 
 
-def per_device(grad_out, routes, combine, hidden_cache, down_weight):
+def routed(grad_out, routes, combine, hidden_cache, down_weight):
     node_count = lax.axis_size("node")
     local_count = lax.axis_size("local")
     experts_all = node_count * local_count
@@ -77,6 +81,212 @@
     return (d_hidden, d_combine)
 
 
+LANES = 128
+LINE = 4
+WORK_BYTES = 16 * 1024 * 1024
+CHUNK = 256
+
+
+def pack_kernel(rows_ref, routes_ref, combine_ref, block_ref, kept_ref):
+    top, tokens = routes_ref.shape
+    table = jnp.concatenate(
+        [routes_ref[...].astype(jnp.float32), combine_ref[...].astype(jnp.float32)], axis=0
+    )
+    table = jnp.concatenate([table] * (LANES // tokens), axis=1)
+    fill = jnp.zeros((rows_ref.shape[0] - 2 * top, LANES), jnp.float32)
+    block_ref[:, :LANES] = jnp.concatenate([table, fill], axis=0).astype(rows_ref.dtype)
+    block_ref[:, LANES:] = rows_ref[...]
+    kept_ref[...] = routes_ref[...]
+
+
+def pick_rows(blocks, expert, capacity, picked, at):
+    tokens = blocks[0].shape[0]
+    top = tokens // 4
+    span = len(blocks) * tokens
+    rows = len(blocks) * capacity
+    owner = lax.broadcasted_iota(jnp.int32, (1, span), 1) // tokens
+    earlier = lax.broadcasted_iota(jnp.int32, (span, span), 0)
+    later = lax.broadcasted_iota(jnp.int32, (span, span), 1)
+    before = ((earlier < later) & (earlier // tokens == later // tokens)).astype(jnp.bfloat16)
+    table = jnp.zeros((2 * top, span), jnp.float32)
+    for i, block in enumerate(blocks):
+        table = jnp.where(owner == i, block[: 2 * top, :LANES].astype(jnp.float32), table)
+    match = (table[:top] == expert).astype(jnp.float32)
+    hit = jnp.sum(match, axis=0, keepdims=True)
+    weight = jnp.sum(match * table[top:], axis=0, keepdims=True)
+    rank = jnp.dot(
+        jnp.broadcast_to(hit, (top, span)).astype(jnp.bfloat16),
+        before,
+        preferred_element_type=jnp.float32,
+    )[:1]
+    target = rank + (owner * capacity).astype(jnp.float32)
+    slot_of = lax.broadcasted_iota(jnp.int32, (rows, span), 0).astype(jnp.float32)
+    choose = jnp.where((slot_of == target) & (hit > 0), jnp.float32(1), jnp.float32(0))
+    source_rows = jnp.concatenate([block[:, LANES:] for block in blocks], axis=0)
+    picked[at : at + rows, :] = jnp.dot(
+        choose.astype(jnp.bfloat16), source_rows, preferred_element_type=jnp.float32
+    ).astype(jnp.bfloat16)
+    return choose, jnp.sum(choose * weight, axis=1, keepdims=True)
+
+
+def expert_kernel(masks, members, *refs):
+    count = len(masks) * members
+    blocks = refs[:count]
+    weights, cache, scaled_ref = refs[count : count + 3]
+    term_refs = refs[count + 3 : count + 3 + len(masks)]
+    picked, chosen, scales = refs[count + 3 + len(masks) :]
+    hidden = weights.shape[0]
+    node = lax.axis_index("node")
+    local = lax.axis_index("local")
+    expert = (node * LINE + local).astype(jnp.float32)
+    rows = scaled_ref.shape[0] // len(masks)
+    capacity = rows // members
+
+    def pick(group, at):
+        choose, scale = pick_rows(group, expert, capacity, picked, at)
+        chosen[at : at + rows, :] = choose
+        scales[at : at + rows, :] = jnp.broadcast_to(scale, (rows, LANES))
+
+    for g in range(len(masks)):
+        pick(blocks[g * members : (g + 1) * members], g * rows)
+
+    scale = scales[:, :1]
+    terms = jnp.zeros((scaled_ref.shape[0], 1), jnp.float32)
+    for c in range(0, hidden, CHUNK):
+        part = slice(c, c + CHUNK)
+        products = lax.dot_general(
+            picked[...], weights[part, :], (((1,), (1,)), ((), ())), preferred_element_type=jnp.float32
+        )
+        kept = []
+        for j in masks:
+            for i in range(members):
+                source = (node ^ i) * LINE + (local ^ j)
+                kept.append(cache[pl.ds(pl.multiple_of(source * capacity, capacity), capacity), part])
+        kept = jnp.concatenate(kept, axis=0).astype(jnp.float32)
+        terms = terms + jnp.sum(products * kept, axis=1, keepdims=True)
+        scaled_ref[:, part] = (scale * products).astype(scaled_ref.dtype)
+    spread = chosen[...] * terms
+    for g, term_ref in enumerate(term_refs):
+        term_ref[...] = jnp.sum(spread[g * rows : (g + 1) * rows], axis=0, keepdims=True)
+
+
+def place_kernel(masks, members, first_ref, rest_ref, out_ref):
+    node = lax.axis_index("node")
+    local = lax.axis_index("local")
+    capacity = out_ref.shape[0] // (len(masks) * members)
+    for g, j in enumerate(masks):
+        for i in range(members):
+            source = (node ^ i) * LINE + (local ^ j)
+            start = pl.multiple_of(source * capacity, capacity)
+            at = ((g - 1 if g else 0) * members + i) * capacity
+            group_ref = rest_ref if g else first_ref
+            out_ref[pl.ds(start, capacity), :] = group_ref[at : at + capacity, :]
+
+
+def finish_kernel(masks, members, routes_ref, *refs):
+    *returned, out_ref = refs
+    node = lax.axis_index("node")
+    local = lax.axis_index("local")
+    routes = routes_ref[...]
+    tokens = routes.shape[1]
+    total = jnp.zeros(routes.shape, jnp.float32)
+    for i in range(members):
+        for g, j in enumerate(masks):
+            expert = (node ^ i) * LINE + (local ^ j)
+            mine = returned[i][g : g + 1, i * tokens : (i + 1) * tokens]
+            total = total + jnp.where(routes == expert, mine, jnp.float32(0))
+    out_ref[...] = total
+
+
+def exchanged(grad_out, routes, combine, hidden_cache, down_weight):
+    nodes = lax.axis_size("node")
+    tokens, width = grad_out.shape
+    hidden = down_weight.shape[1]
+    slots = hidden_cache.shape[1]
+    rows = slots // LINE
+    vmem = pl.BlockSpec(memory_space=pltpu.VMEM)
+
+    def move(x, node_mask, local_mask):
+        pairs = [
+            (n * LINE + l, (n ^ node_mask) * LINE + (l ^ local_mask))
+            for n in range(nodes)
+            for l in range(LINE)
+        ]
+        return lax.ppermute(x, ("node", "local"), pairs)
+
+    def after(x, *others):
+        return lax.optimization_barrier((x, *others))[0]
+
+    def over_nodes(x, gates=()):
+        across = move(x, 2, 0)
+        across_beside = move(after(across, *gates), 1, 0)
+        return [x, move(x, 1, 0), across, across_beside]
+
+    def multiply(masks, blocks):
+        total = rows * len(masks)
+        results = pl.pallas_call(
+            functools.partial(expert_kernel, masks, nodes),
+            out_shape=[jax.ShapeDtypeStruct((total, hidden), jnp.bfloat16)]
+            + [jax.ShapeDtypeStruct((1, nodes * tokens), jnp.float32)] * len(masks),
+            in_specs=[vmem] * (len(blocks) + 2),
+            out_specs=[vmem] * (1 + len(masks)),
+            scratch_shapes=[
+                pltpu.VMEM((total, width), jnp.bfloat16),
+                pltpu.VMEM((total, nodes * tokens), jnp.float32),
+                pltpu.VMEM((total, LANES), jnp.float32),
+            ],
+            compiler_params=pltpu.CompilerParams(vmem_limit_bytes=WORK_BYTES),
+            cost_estimate=pl.CostEstimate(flops=1, bytes_accessed=1, transcendentals=0),
+        )(*blocks, down_weight[0], hidden_cache[0])
+        return results[0], results[1:]
+
+    routes_t = routes.T
+    block, kept = pl.pallas_call(
+        pack_kernel,
+        out_shape=[
+            jax.ShapeDtypeStruct((tokens, LANES + width), grad_out.dtype),
+            jax.ShapeDtypeStruct(routes_t.shape, routes_t.dtype),
+        ],
+        in_specs=[vmem] * 3,
+        out_specs=[vmem] * 2,
+    )(grad_out, routes_t, combine.T)
+
+    masks = (0, 1, 3, 2)
+    far = {j: move(block, 0, j) for j in masks[1:]}
+    first_rows, first_terms = multiply(masks[:1], over_nodes(block))
+    blocks = []
+    for j in masks[1:]:
+        blocks += over_nodes(far[j], first_terms if j == masks[-1] else ())
+    rest_rows, rest_terms = multiply(masks[1:], blocks)
+
+    d_hidden = pl.pallas_call(
+        functools.partial(place_kernel, masks, nodes),
+        out_shape=jax.ShapeDtypeStruct((slots, hidden), jnp.bfloat16),
+        in_specs=[vmem] * 2,
+        out_specs=vmem,
+    )(first_rows, rest_rows)
+
+    back = list(first_terms) + [move(term, 0, j) for j, term in zip(masks[1:], rest_terms)]
+    back = jnp.concatenate(back, axis=0)
+    returned = [back] + [move(back, i, 0) for i in range(1, nodes)]
+    d_combine_t = pl.pallas_call(
+        functools.partial(finish_kernel, masks, nodes),
+        out_shape=jax.ShapeDtypeStruct(routes_t.shape, jnp.float32),
+        in_specs=[vmem] * (1 + nodes),
+        out_specs=vmem,
+    )(kept, *returned)
+    return d_hidden[None], d_combine_t.T
+
+
+def per_device(grad_out, routes, combine, hidden_cache, down_weight):
+    nodes = lax.axis_size("node")
+    locals_ = lax.axis_size("local")
+    tokens, top = routes.shape
+    if nodes == TOPNODES == 4 and locals_ == LINE and nodes * tokens == LANES and tokens == 4 * top:
+        return exchanged(grad_out, routes, combine, hidden_cache, down_weight)
+    return routed(grad_out, routes, combine, hidden_cache, down_weight)
+
+
 def solution(mesh):
     placed = (
         P(("rep", "node", "local"), None),

time: 106 us -> 58.9 us (0.56)
  waiting for transfers between devices: 59.4 us -> 24.6 us
  blocking collectives: 14.3 us -> 0 us
  Pallas kernels: 0 us -> 11.2 us
  matrix products: 8.36 us -> 0 us
  local copies, waits for them, and re-layouts: 3.65 us -> 6.4 us
  other arithmetic: 2.3 us -> 0.01 us
    all_to_all x4 -> x0, waiting for transfers between devices: 59.4 us -> none  [the longest x1 41.1 us: per_device(): lax.all_to_all(row_block, 'local', split_axis=1, concat_axis=1, tiled=True)]
    ppermute x0 -> x21, waiting for transfers between devices: none -> 24.6 us  [move(): return lax.ppermute(x, ('node', 'local'), pairs)]
    all_to_all x4 -> x0, starting transfers between devices: 16.6 us -> none  [the longest x1 5.34 us: per_device(): lax.all_to_all(weights, 'local', split_axis=1, concat_axis=1, tiled=True)]
    ppermute x0 -> x21, starting transfers between devices: none -> 15.7 us  [move(): return lax.ppermute(x, ('node', 'local'), pairs)]
    all_to_all x2 -> x0, blocking collectives: 14.3 us -> none  [the longest x1 8.11 us: per_device(): lax.all_to_all(lax.all_to_all(slot_terms, 'node', split_axis=0, concat_ax...]
    pallas_call x0 -> x5, Pallas kernels: none -> 11.2 us  [the longest x2 6.14 us: multiply(): pl.pallas_call(functools.partial(expert_kernel, masks, nodes), out_shape=...]
    dot_general x5 -> x0, matrix products: 8.36 us -> none  [the longest x1 6.09 us: per_device(): lax.dot_general(flat_rows, down_weight[0], (((1,), (1,)), ((), ())), pref...]
    unnamed x8 -> x22, local copies, waits for them, and re-layouts: 0.84 us -> 6.4 us
  transfers between devices with their start and end apart: 4 -> 21, of which waited for: 4 -> 12; matrix products, arithmetic and copies ran while one was open for 4% -> 0% of each run, Pallas kernels for 0% -> 8%
where the time goes in v2:
time: 58.9 us; the launch traced here: 58.6 us
  waiting for transfers between devices  24.6 us (42%)
  starting transfers between devices  15.7 us (27%)
  Pallas kernels  11.2 us (19%)
  local copies, waits for them, and re-layouts  6.4 us (11%)
  between operations  0.74 us (1%)
    ppermute x21, waiting for transfers between devices, move(): return lax.ppermute(x, ('node', 'local'), pairs)  24.6 us
    ppermute x21, starting transfers between devices, move(): return lax.ppermute(x, ('node', 'local'), pairs)  15.7 us
    unnamed x22, local copies, waits for them, and re-layouts  6.4 us
    pallas_call x2, Pallas kernels, multiply(): pl.pallas_call(functools.partial(expert_kernel, masks, nodes), out_shape=...  6.14 us
    pallas_call x1, Pallas kernels, exchanged(): pl.pallas_call(functools.partial(place_kernel, masks, nodes), out_shape=j...  1.91 us
    pallas_call x1, Pallas kernels, exchanged(): pl.pallas_call(pack_kernel, out_shape=[jax.ShapeDtypeStruct((tokens, LANE...  1.73 us
    pallas_call x1, Pallas kernels, exchanged(): pl.pallas_call(functools.partial(finish_kernel, masks, nodes), out_shape=...  1.39 us
  transfers between devices with their start and end apart: 21, of which 12 were waited for; matrix products, arithmetic and copies ran while one was open for 0% of the time, Pallas kernels for 8%

profile of v2, /device:TPU:0, one launch (start us, length us, event | category | flops | bytes accessed | tf_op | source)
XLA Modules:
  0.0 58.6 jit_solution(2787278165880316677)
XLA Ops:
  0.6 1.7 %shard_map.68 = (bf16[32,3712]{1,0:T(8,128)(2,1)}, s32[8,32]{1,0:T(8,128)}) custom-call(bf16[32,3584]{1,0:T(8,128)(2,1)} %rows_ref.1, s32[8,32]{1,0:T(8,128)} %bitcast.11, bf16[8,32]{1,0:T(8,128)(2,1)} %bitcast.13), custom_call_target="tpu_custom_call" | custom-call | tf_op jit(solution)/shard_map/pallas_call | solution.py:244
  2.4 2.9 %collective-permute-start.1 = (bf16[32,3712]{1,0:T(8,128)(2,1)}, bf16[32,3712]{1,0:T(8,128)(2,1)S(1)}, u32[]{:S(2)}, u32[]{:S(2)}) collective-permute-start(bf16[32,3712]{1,0:T(8,128)(2,1)} %get-tuple-element.11.refs_0_), channel_id=1, source_target_pairs={{0,8},{1,9},{2,10},{3,11},{4,12},{5,13},{6,14},{7,15},{8,0},{9,1},... | collective-permute-start | bytes 712712 | tf_op jit(solution)/shard_map/ppermute | solution.py:215
  5.3 1.6 %collective-permute-start.3 = (bf16[32,3712]{1,0:T(8,128)(2,1)}, bf16[32,3712]{1,0:T(8,128)(2,1)S(1)}, u32[]{:S(2)}, u32[]{:S(2)}) collective-permute-start(bf16[32,3712]{1,0:T(8,128)(2,1)} %get-tuple-element.11.refs_0_), channel_id=1, source_target_pairs={{0,1},{1,0},{2,3},{3,2},{4,5},{5,4},{6,7},{7,6},{8,9},{9,8},{10,11... | collective-permute-start | bytes 712712 | tf_op jit(solution)/shard_map/ppermute | solution.py:215
  6.9 2.5 %collective-permute-start.7 = (bf16[32,3712]{1,0:T(8,128)(2,1)}, bf16[32,3712]{1,0:T(8,128)(2,1)S(1)}, u32[]{:S(2)}, u32[]{:S(2)}) collective-permute-start(bf16[32,3712]{1,0:T(8,128)(2,1)} %get-tuple-element.11.refs_0_), channel_id=1, source_target_pairs={{0,3},{1,2},{2,1},{3,0},{4,7},{5,6},{6,5},{7,4},{8,11},{9,10},{10,... | collective-permute-start | bytes 712712 | tf_op jit(solution)/shard_map/ppermute | solution.py:215
  9.3 0.1 collective-permute-start.11
  9.5 0.0 collective-permute-start
  9.5 1.8 %collective-permute-done.1.refs_2_ = bf16[32,3712]{1,0:T(8,128)(2,1)S(1)} collective-permute-done((bf16[32,3712]{1,0:T(8,128)(2,1)}, bf16[32,3712]{1,0:T(8,128)(2,1)S(1)}, u32[]{:S(2)}, u32[]{:S(2)}) %collective-permute-start.1) | collective-permute-done | bytes 237600 | tf_op jit(solution)/shard_map/ppermute | solution.py:215
  11.3 0.0 collective-permute-start.2
  11.3 2.1 %collective-permute-done.3.refs_0_ = bf16[32,3712]{1,0:T(8,128)(2,1)S(1)} collective-permute-done((bf16[32,3712]{1,0:T(8,128)(2,1)}, bf16[32,3712]{1,0:T(8,128)(2,1)S(1)}, u32[]{:S(2)}, u32[]{:S(2)}) %collective-permute-start.3) | collective-permute-done | bytes 237600 | tf_op jit(solution)/shard_map/ppermute | solution.py:215
  13.4 0.5 collective-permute-start.5
  13.9 7.5 %collective-permute-done.7.refs_4_ = bf16[32,3712]{1,0:T(8,128)(2,1)S(1)} collective-permute-done((bf16[32,3712]{1,0:T(8,128)(2,1)}, bf16[32,3712]{1,0:T(8,128)(2,1)S(1)}, u32[]{:S(2)}, u32[]{:S(2)}) %collective-permute-start.7) | collective-permute-done | bytes 237600 | tf_op jit(solution)/shard_map/ppermute | solution.py:215
  21.4 0.5 collective-permute-start.9
  22.0 8.2 %collective-permute-done.11.refs_8_ = bf16[32,3712]{1,0:T(8,128)(2,1)S(1)} collective-permute-done((bf16[32,3712]{1,0:T(8,128)(2,1)}, bf16[32,3712]{1,0:T(8,128)(2,1)S(1)}, u32[]{:S(2)}, u32[]{:S(2)}) %collective-permute-start.11) | collective-permute-done | bytes 237600 | tf_op jit(solution)/shard_map/ppermute | solution.py:215
  30.2 0.5 collective-permute-start.13
  30.7 0.0 collective-permute-start.4
  30.7 0.0 collective-permute-done.2.refs_3_
  30.7 0.5 collective-permute-start.8
  31.2 3.1 %copy-done = bf16[1,1024,3584]{2,1,0:T(8,128)(2,1)S(1)} copy-done((bf16[1,1024,3584]{2,1,0:T(8,128)(2,1)S(1)}, bf16[1,1024,3584]{2,1,0:T(8,128)(2,1)}, u32[]{:S(2)}) %copy-start) | copy-done | bytes 7340056
  34.3 1.0 %copy-done.2 = bf16[1,256,1024]{2,1,0:T(8,128)(2,1)S(1)} copy-done((bf16[1,256,1024]{2,1,0:T(8,128)(2,1)S(1)}, bf16[1,256,1024]{2,1,0:T(8,128)(2,1)}, u32[]{:S(2)}) %copy-start.2) | copy-done | bytes 524312
  35.4 0.9 %copy-done.5 = bf16[32,3712]{1,0:T(8,128)(2,1)S(1)} copy-done((bf16[32,3712]{1,0:T(8,128)(2,1)S(1)}, bf16[32,3712]{1,0:T(8,128)(2,1)}, u32[]{:S(2)}) %copy-start.5) | copy-done | bytes 237592
  36.3 2.7 %shard_map.69 = (bf16[64,1024]{1,0:T(8,128)(2,1)S(1)}, f32[1,128]{1,0:T(1,128)S(1)}) custom-call(bf16[32,3712]{1,0:T(8,128)(2,1)S(1)} %copy-done.5, bf16[32,3712]{1,0:T(8,128)(2,1)S(1)} %collective-permute-done.refs_1_, bf16[32,3712]{1,0:T(8,128)(2,1)S(1)} %collective-permute-done.1.refs_2_, bf16[32,3712]{1,0:T(8,128)(2,1)S(1)} %collective-permute-done.2.refs_3_, ...), custom_call_target="tpu_custom_call" | custom-call | flops 1 | bytes 1 | tf_op jit(solution)/shard_map/pallas_call | solution.py:227
  39.0 0.0 collective-permute-done.5.refs_2_
  39.0 0.1 collective-permute-start.12
  39.2 0.4 collective-permute-start.6
  39.6 0.0 collective-permute-done.13.refs_10_
  39.6 0.1 collective-permute-start.10
  39.7 0.0 collective-permute-done.4.refs_1_
  39.7 0.4 collective-permute-start.14
  40.1 0.0 collective-permute-done.8.refs_5_
  40.1 0.5 collective-permute-done.12.refs_9_
  40.6 0.3 collective-permute-done.6.refs_3_
  40.9 0.3 collective-permute-done.10.refs_7_
  41.3 0.3 collective-permute-done.14.refs_11_
  41.6 3.4 %shard_map.70 = (bf16[192,1024]{1,0:T(8,128)(2,1)S(1)}, f32[1,128]{1,0:T(1,128)S(1)}, f32[1,128]{1,0:T(1,128)S(1)}, f32[1,128]{1,0:T(1,128)S(1)}) custom-call(bf16[32,3712]{1,0:T(8,128)(2,1)S(1)} %collective-permute-done.3.refs_0_, bf16[32,3712]{1,0:T(8,128)(2,1)S(1)} %collective-permute-done.4.refs_1_, bf16[32,3712]{1,0:T(8,128)(2,1)S(1)} %collective-permute-done.5.refs_2_, ...), custom_call_target="tpu_custom_call" | custom-call | flops 1 | bytes 1 | tf_op jit(solution)/shard_map/pallas_call | solution.py:227
  45.1 0.7 %copy-done.4 = bf16[192,1024]{1,0:T(8,128)(2,1)} copy-done((bf16[192,1024]{1,0:T(8,128)(2,1)}, bf16[192,1024]{1,0:T(8,128)(2,1)S(1)}, u32[]{:S(2)}) %copy-start.4) | copy-done | bytes 393240
  45.8 0.0 collective-permute-start.17
  45.8 2.6 %collective-permute-start.16 = (f32[1,128]{1,0:T(1,128)S(1)}, f32[1,128]{1,0:T(1,128)S(1)}, u32[]{:S(2)}, u32[]{:S(2)}) collective-permute-start(f32[1,128]{1,0:T(1,128)S(1)} %get-tuple-element.18), channel_id=1, source_target_pairs={{0,3},{1,2},{2,1},{3,0},{4,7},{5,6},{6,5},{7,4},{8,11},{9,10},{10,... | collective-permute-start | bytes 1544 | tf_op jit(solution)/shard_map/ppermute | solution.py:215
  48.5 0.9 %collective-permute-start.15 = (f32[1,128]{1,0:T(1,128)S(1)}, f32[1,128]{1,0:T(1,128)S(1)}, u32[]{:S(2)}, u32[]{:S(2)}) collective-permute-start(f32[1,128]{1,0:T(1,128)S(1)} %get-tuple-element.17), channel_id=1, source_target_pairs={{0,1},{1,0},{2,3},{3,2},{4,5},{5,4},{6,7},{7,6},{8,9},{9,8},{10,11... | collective-permute-start | bytes 1544 | tf_op jit(solution)/shard_map/ppermute | solution.py:215
  49.3 0.9 %collective-permute-done.17 = f32[1,128]{1,0:T(1,128)S(1)} collective-permute-done((f32[1,128]{1,0:T(1,128)S(1)}, f32[1,128]{1,0:T(1,128)S(1)}, u32[]{:S(2)}, u32[]{:S(2)}) %collective-permute-start.17) | collective-permute-done | bytes 544 | tf_op jit(solution)/shard_map/ppermute | solution.py:215
  50.3 0.9 %collective-permute-done.16 = f32[1,128]{1,0:T(1,128)S(1)} collective-permute-done((f32[1,128]{1,0:T(1,128)S(1)}, f32[1,128]{1,0:T(1,128)S(1)}, u32[]{:S(2)}, u32[]{:S(2)}) %collective-permute-start.16) | collective-permute-done | bytes 544 | tf_op jit(solution)/shard_map/ppermute | solution.py:215
  51.2 0.8 %collective-permute-done.15 = f32[1,128]{1,0:T(1,128)S(1)} collective-permute-done((f32[1,128]{1,0:T(1,128)S(1)}, f32[1,128]{1,0:T(1,128)S(1)}, u32[]{:S(2)}, u32[]{:S(2)}) %collective-permute-start.15) | collective-permute-done | bytes 544 | tf_op jit(solution)/shard_map/ppermute | solution.py:215
  52.0 0.1 collective-permute-start.18
  52.1 1.5 %collective-permute-start.19 = (f32[4,128]{1,0:T(4,128)S(1)}, f32[4,128]{1,0:T(4,128)S(1)}, u32[]{:S(2)}, u32[]{:S(2)}) collective-permute-start(f32[4,128]{1,0:T(4,128)S(1)} %pad_maximum_fusion.refs_0_), channel_id=1, source_target_pairs={{0,8},{1,9},{2,10},{3,11},{4,12},{5,13},{6,14},{7,15},{8,0},{9,1},... | collective-permute-start | bytes 6152 | tf_op jit(solution)/shard_map/ppermute | solution.py:215
  53.6 0.3 collective-permute-start.20
  54.0 1.9 %shard_map.71 = bf16[256,1024]{1,0:T(8,128)(2,1)} custom-call(bf16[64,1024]{1,0:T(8,128)(2,1)} %copy-done.6, bf16[192,1024]{1,0:T(8,128)(2,1)} %copy-done.4), custom_call_target="tpu_custom_call" | custom-call | tf_op jit(solution)/shard_map/pallas_call | solution.py:262
  55.9 0.8 %collective-permute-done.20.refs_3_ = f32[4,128]{1,0:T(4,128)S(1)} collective-permute-done((f32[4,128]{1,0:T(4,128)S(1)}, f32[4,128]{1,0:T(4,128)S(1)}, u32[]{:S(2)}, u32[]{:S(2)}) %collective-permute-start.20) | collective-permute-done | bytes 2080 | tf_op jit(solution)/shard_map/ppermute | solution.py:215
  56.7 0.6 copy-done.10
  57.2 1.4 %shard_map.72 = f32[8,32]{1,0:T(8,128)} custom-call(s32[8,32]{1,0:T(8,128)} %get-tuple-element.16.routes_ref, f32[4,128]{1,0:T(4,128)} %copy-done.7, f32[4,128]{1,0:T(4,128)} %copy-done.8, f32[4,128]{1,0:T(4,128)} %copy-done.9, f32[4,128]{1,0:T(4,128)} %copy-done.10), custom_call_target="tpu_custom_call" | custom-call | tf_op jit(solution)/shard_map/pallas_call | solution.py:272
  (22 shorter events, 0.1 us)
Async XLA Ops:
  2.4 8.9 %collective-permute-start.1 = (bf16[32,3712]{1,0:T(8,128)(2,1)}, bf16[32,3712]{1,0:T(8,128)(2,1)S(1)}, u32[]{:S(2)}, u32[]{:S(2)}) collective-permute-start(bf16[32,3712]{1,0:T(8,128)(2,1)} %get-tuple-element.11.refs_0_), channel_id=1, source_target_pairs={{0,8},{1,9},{2,10},{3,11},{4,12},{5,13},{6,14},{7,15},{8,0},{9,1},... | collective-permute-start | bytes 712712 | tf_op jit(solution)/shard_map/ppermute | solution.py:215
  5.3 8.1 %collective-permute-start.3 = (bf16[32,3712]{1,0:T(8,128)(2,1)}, bf16[32,3712]{1,0:T(8,128)(2,1)S(1)}, u32[]{:S(2)}, u32[]{:S(2)}) collective-permute-start(bf16[32,3712]{1,0:T(8,128)(2,1)} %get-tuple-element.11.refs_0_), channel_id=1, source_target_pairs={{0,1},{1,0},{2,3},{3,2},{4,5},{5,4},{6,7},{7,6},{8,9},{9,8},{10,11... | collective-permute-start | bytes 712712 | tf_op jit(solution)/shard_map/ppermute | solution.py:215
  6.9 14.6 %collective-permute-start.7 = (bf16[32,3712]{1,0:T(8,128)(2,1)}, bf16[32,3712]{1,0:T(8,128)(2,1)S(1)}, u32[]{:S(2)}, u32[]{:S(2)}) collective-permute-start(bf16[32,3712]{1,0:T(8,128)(2,1)} %get-tuple-element.11.refs_0_), channel_id=1, source_target_pairs={{0,3},{1,2},{2,1},{3,0},{4,7},{5,6},{6,5},{7,4},{8,11},{9,10},{10,... | collective-permute-start | bytes 712712 | tf_op jit(solution)/shard_map/ppermute | solution.py:215
  9.3 20.8 %collective-permute-start.11 = (bf16[32,3712]{1,0:T(8,128)(2,1)}, bf16[32,3712]{1,0:T(8,128)(2,1)S(1)}, u32[]{:S(2)}, u32[]{:S(2)}) collective-permute-start(bf16[32,3712]{1,0:T(8,128)(2,1)} %get-tuple-element.11.refs_0_), channel_id=1, source_target_pairs={{0,2},{1,3},{2,0},{3,1},{4,6},{5,7},{6,4},{7,5},{8,10},{9,11},{10,... | collective-permute-start | bytes 712712 | tf_op jit(solution)/shard_map/ppermute | solution.py:215
  9.5 21.3 %collective-permute-start = (bf16[32,3712]{1,0:T(8,128)(2,1)}, bf16[32,3712]{1,0:T(8,128)(2,1)S(1)}, u32[]{:S(2)}, u32[]{:S(2)}) collective-permute-start(bf16[32,3712]{1,0:T(8,128)(2,1)} %get-tuple-element.11.refs_0_), channel_id=1, source_target_pairs={{0,4},{1,5},{2,6},{3,7},{4,0},{5,1},{6,2},{7,3},{8,12},{9,13},{10,... | collective-permute-start | bytes 712712 | tf_op jit(solution)/shard_map/ppermute | solution.py:215
  11.3 19.5 %collective-permute-start.2 = (bf16[32,3712]{1,0:T(8,128)(2,1)S(1)}, bf16[32,3712]{1,0:T(8,128)(2,1)S(1)}, u32[]{:S(2)}, u32[]{:S(2)}) collective-permute-start(bf16[32,3712]{1,0:T(8,128)(2,1)S(1)} %collective-permute-done.1.refs_2_), channel_id=1, source_target_pairs={{0,4},{1,5},{2,6},{3,7},{4,0},{5,1},{6,2},{7,3},{8,12},{9,13},{10,... | collective-permute-start | bytes 712712 | tf_op jit(solution)/shard_map/ppermute | solution.py:215
  13.4 25.6 %collective-permute-start.5 = (bf16[32,3712]{1,0:T(8,128)(2,1)S(1)}, bf16[32,3712]{1,0:T(8,128)(2,1)S(1)}, u32[]{:S(2)}, u32[]{:S(2)}) collective-permute-start(bf16[32,3712]{1,0:T(8,128)(2,1)S(1)} %collective-permute-done.3.refs_0_), channel_id=1, source_target_pairs={{0,8},{1,9},{2,10},{3,11},{4,12},{5,13},{6,14},{7,15},{8,0},{9,1},... | collective-permute-start | bytes 712712 | tf_op jit(solution)/shard_map/ppermute | solution.py:215
  21.4 17.8 %collective-permute-start.9 = (bf16[32,3712]{1,0:T(8,128)(2,1)S(1)}, bf16[32,3712]{1,0:T(8,128)(2,1)S(1)}, u32[]{:S(2)}, u32[]{:S(2)}) collective-permute-start(bf16[32,3712]{1,0:T(8,128)(2,1)S(1)} %collective-permute-done.7.refs_4_), channel_id=1, source_target_pairs={{0,8},{1,9},{2,10},{3,11},{4,12},{5,13},{6,14},{7,15},{8,0},{9,1},... | collective-permute-start | bytes 712712 | tf_op jit(solution)/shard_map/ppermute | solution.py:215
  30.2 9.4 %collective-permute-start.13 = (bf16[32,3712]{1,0:T(8,128)(2,1)S(1)}, bf16[32,3712]{1,0:T(8,128)(2,1)S(1)}, u32[]{:S(2)}, u32[]{:S(2)}) collective-permute-start(bf16[32,3712]{1,0:T(8,128)(2,1)S(1)} %collective-permute-done.11.refs_8_), channel_id=1, source_target_pairs={{0,8},{1,9},{2,10},{3,11},{4,12},{5,13},{6,14},{7,15},{8,0},{9,1},... | collective-permute-start | bytes 712712 | tf_op jit(solution)/shard_map/ppermute | solution.py:215
  30.7 9.0 %collective-permute-start.4 = (bf16[32,3712]{1,0:T(8,128)(2,1)S(1)}, bf16[32,3712]{1,0:T(8,128)(2,1)S(1)}, u32[]{:S(2)}, u32[]{:S(2)}) collective-permute-start(bf16[32,3712]{1,0:T(8,128)(2,1)S(1)} %collective-permute-done.3.refs_0_), channel_id=1, source_target_pairs={{0,4},{1,5},{2,6},{3,7},{4,0},{5,1},{6,2},{7,3},{8,12},{9,13},{10,... | collective-permute-start | bytes 712712 | tf_op jit(solution)/shard_map/ppermute | solution.py:215
  30.7 9.4 %collective-permute-start.8 = (bf16[32,3712]{1,0:T(8,128)(2,1)S(1)}, bf16[32,3712]{1,0:T(8,128)(2,1)S(1)}, u32[]{:S(2)}, u32[]{:S(2)}) collective-permute-start(bf16[32,3712]{1,0:T(8,128)(2,1)S(1)} %collective-permute-done.7.refs_4_), channel_id=1, source_target_pairs={{0,4},{1,5},{2,6},{3,7},{4,0},{5,1},{6,2},{7,3},{8,12},{9,13},{10,... | collective-permute-start | bytes 712712 | tf_op jit(solution)/shard_map/ppermute | solution.py:215
  31.2 3.1 %copy-start = (bf16[1,1024,3584]{2,1,0:T(8,128)(2,1)S(1)}, bf16[1,1024,3584]{2,1,0:T(8,128)(2,1)}, u32[]{:S(2)}) copy-start(bf16[1,1024,3584]{2,1,0:T(8,128)(2,1)} %param.9) | copy-start | bytes 22020100
  34.3 1.0 %copy-start.2 = (bf16[1,256,1024]{2,1,0:T(8,128)(2,1)S(1)}, bf16[1,256,1024]{2,1,0:T(8,128)(2,1)}, u32[]{:S(2)}) copy-start(bf16[1,256,1024]{2,1,0:T(8,128)(2,1)} %param.8) | copy-start | bytes 1572868
  35.4 0.9 %copy-start.5 = (bf16[32,3712]{1,0:T(8,128)(2,1)S(1)}, bf16[32,3712]{1,0:T(8,128)(2,1)}, u32[]{:S(2)}) copy-start(bf16[32,3712]{1,0:T(8,128)(2,1)} %get-tuple-element.11.refs_0_) | copy-start | bytes 712708
  36.3 5.3 %copy-start.1 = (bf16[1,1024,3584]{2,1,0:T(8,128)(2,1)S(1)}, bf16[1,1024,3584]{2,1,0:T(8,128)(2,1)}, u32[]{:S(2)}) copy-start(bf16[1,1024,3584]{2,1,0:T(8,128)(2,1)} %param.9) | copy-start | bytes 22020100
  36.3 5.3 %copy-start.3 = (bf16[1,256,1024]{2,1,0:T(8,128)(2,1)S(1)}, bf16[1,256,1024]{2,1,0:T(8,128)(2,1)}, u32[]{:S(2)}) copy-start(bf16[1,256,1024]{2,1,0:T(8,128)(2,1)} %param.8) | copy-start | bytes 1572868
  39.0 6.1 %copy-start.6 = (bf16[64,1024]{1,0:T(8,128)(2,1)}, bf16[64,1024]{1,0:T(8,128)(2,1)S(1)}, u32[]{:S(2)}) copy-start(bf16[64,1024]{1,0:T(8,128)(2,1)S(1)} %get-tuple-element.12.first_ref) | copy-start | bytes 393220
  39.0 1.6 %collective-permute-start.12 = (bf16[32,3712]{1,0:T(8,128)(2,1)S(1)}, bf16[32,3712]{1,0:T(8,128)(2,1)S(1)}, u32[]{:S(2)}, u32[]{:S(2)}) collective-permute-start(bf16[32,3712]{1,0:T(8,128)(2,1)S(1)} %collective-permute-done.11.refs_8_), channel_id=1, source_target_pairs={{0,4},{1,5},{2,6},{3,7},{4,0},{5,1},{6,2},{7,3},{8,12},{9,13},{10,... | collective-permute-start | bytes 712712 | tf_op jit(solution)/shard_map/ppermute | solution.py:215
  39.2 1.8 %collective-permute-start.6 = (bf16[32,3712]{1,0:T(8,128)(2,1)S(1)}, bf16[32,3712]{1,0:T(8,128)(2,1)S(1)}, u32[]{:S(2)}, u32[]{:S(2)}) collective-permute-start(bf16[32,3712]{1,0:T(8,128)(2,1)S(1)} %collective-permute-done.5.refs_2_), channel_id=1, source_target_pairs={{0,4},{1,5},{2,6},{3,7},{4,0},{5,1},{6,2},{7,3},{8,12},{9,13},{10,... | collective-permute-start | bytes 712712 | tf_op jit(solution)/shard_map/ppermute | solution.py:215
  39.6 1.7 %collective-permute-start.10 = (bf16[32,3712]{1,0:T(8,128)(2,1)S(1)}, bf16[32,3712]{1,0:T(8,128)(2,1)S(1)}, u32[]{:S(2)}, u32[]{:S(2)}) collective-permute-start(bf16[32,3712]{1,0:T(8,128)(2,1)S(1)} %collective-permute-done.9.refs_6_), channel_id=1, source_target_pairs={{0,4},{1,5},{2,6},{3,7},{4,0},{5,1},{6,2},{7,3},{8,12},{9,13},{10,... | collective-permute-start | bytes 712712 | tf_op jit(solution)/shard_map/ppermute | solution.py:215
  39.7 1.9 %collective-permute-start.14 = (bf16[32,3712]{1,0:T(8,128)(2,1)S(1)}, bf16[32,3712]{1,0:T(8,128)(2,1)S(1)}, u32[]{:S(2)}, u32[]{:S(2)}) collective-permute-start(bf16[32,3712]{1,0:T(8,128)(2,1)S(1)} %collective-permute-done.13.refs_10_), channel_id=1, source_target_pairs={{0,4},{1,5},{2,6},{3,7},{4,0},{5,1},{6,2},{7,3},{8,12},{9,13},{10,... | collective-permute-start | bytes 712712 | tf_op jit(solution)/shard_map/ppermute | solution.py:215
  45.1 0.7 %copy-start.4 = (bf16[192,1024]{1,0:T(8,128)(2,1)}, bf16[192,1024]{1,0:T(8,128)(2,1)S(1)}, u32[]{:S(2)}) copy-start(bf16[192,1024]{1,0:T(8,128)(2,1)S(1)} %get-tuple-element.15.rest_ref) | copy-start | bytes 1179652
  45.8 4.4 %collective-permute-start.17 = (f32[1,128]{1,0:T(1,128)S(1)}, f32[1,128]{1,0:T(1,128)S(1)}, u32[]{:S(2)}, u32[]{:S(2)}) collective-permute-start(f32[1,128]{1,0:T(1,128)S(1)} %get-tuple-element.19), channel_id=1, source_target_pairs={{0,2},{1,3},{2,0},{3,1},{4,6},{5,7},{6,4},{7,5},{8,10},{9,11},{10,... | collective-permute-start | bytes 1544 | tf_op jit(solution)/shard_map/ppermute | solution.py:215
  45.8 5.3 %collective-permute-start.16 = (f32[1,128]{1,0:T(1,128)S(1)}, f32[1,128]{1,0:T(1,128)S(1)}, u32[]{:S(2)}, u32[]{:S(2)}) collective-permute-start(f32[1,128]{1,0:T(1,128)S(1)} %get-tuple-element.18), channel_id=1, source_target_pairs={{0,3},{1,2},{2,1},{3,0},{4,7},{5,6},{6,5},{7,4},{8,11},{9,10},{10,... | collective-permute-start | bytes 1544 | tf_op jit(solution)/shard_map/ppermute | solution.py:215
  48.5 3.5 %collective-permute-start.15 = (f32[1,128]{1,0:T(1,128)S(1)}, f32[1,128]{1,0:T(1,128)S(1)}, u32[]{:S(2)}, u32[]{:S(2)}) collective-permute-start(f32[1,128]{1,0:T(1,128)S(1)} %get-tuple-element.17), channel_id=1, source_target_pairs={{0,1},{1,0},{2,3},{3,2},{4,5},{5,4},{6,7},{7,6},{8,9},{9,8},{10,11... | collective-permute-start | bytes 1544 | tf_op jit(solution)/shard_map/ppermute | solution.py:215
  52.0 4.6 %copy-start.7 = (f32[4,128]{1,0:T(4,128)}, f32[4,128]{1,0:T(4,128)S(1)}, u32[]{:S(2)}) copy-start(f32[4,128]{1,0:T(4,128)S(1)} %pad_maximum_fusion.refs_0_) | copy-start | bytes 6148
  52.0 3.9 %collective-permute-start.18 = (f32[4,128]{1,0:T(4,128)S(1)}, f32[4,128]{1,0:T(4,128)S(1)}, u32[]{:S(2)}, u32[]{:S(2)}) collective-permute-start(f32[4,128]{1,0:T(4,128)S(1)} %pad_maximum_fusion.refs_0_), channel_id=1, source_target_pairs={{0,4},{1,5},{2,6},{3,7},{4,0},{5,1},{6,2},{7,3},{8,12},{9,13},{10,... | collective-permute-start | bytes 6152 | tf_op jit(solution)/shard_map/ppermute | solution.py:215
  52.1 3.8 %collective-permute-start.19 = (f32[4,128]{1,0:T(4,128)S(1)}, f32[4,128]{1,0:T(4,128)S(1)}, u32[]{:S(2)}, u32[]{:S(2)}) collective-permute-start(f32[4,128]{1,0:T(4,128)S(1)} %pad_maximum_fusion.refs_0_), channel_id=1, source_target_pairs={{0,8},{1,9},{2,10},{3,11},{4,12},{5,13},{6,14},{7,15},{8,0},{9,1},... | collective-permute-start | bytes 6152 | tf_op jit(solution)/shard_map/ppermute | solution.py:215
  53.6 3.0 %collective-permute-start.20 = (f32[4,128]{1,0:T(4,128)S(1)}, f32[4,128]{1,0:T(4,128)S(1)}, u32[]{:S(2)}, u32[]{:S(2)}) collective-permute-start(f32[4,128]{1,0:T(4,128)S(1)} %pad_maximum_fusion.refs_0_), channel_id=1, source_target_pairs={{0,12},{1,13},{2,14},{3,15},{4,8},{5,9},{6,10},{7,11},{8,4},{9,5},... | collective-permute-start | bytes 6152 | tf_op jit(solution)/shard_map/ppermute | solution.py:215
  55.9 0.8 %copy-start.8 = (f32[4,128]{1,0:T(4,128)}, f32[4,128]{1,0:T(4,128)S(1)}, u32[]{:S(2)}) copy-start(f32[4,128]{1,0:T(4,128)S(1)} %collective-permute-done.18.refs_1_) | copy-start | bytes 6148
  55.9 0.8 %copy-start.9 = (f32[4,128]{1,0:T(4,128)}, f32[4,128]{1,0:T(4,128)S(1)}, u32[]{:S(2)}) copy-start(f32[4,128]{1,0:T(4,128)S(1)} %collective-permute-done.19.refs_2_) | copy-start | bytes 6148
  56.7 0.6 %copy-start.10 = (f32[4,128]{1,0:T(4,128)}, f32[4,128]{1,0:T(4,128)S(1)}, u32[]{:S(2)}) copy-start(f32[4,128]{1,0:T(4,128)S(1)} %collective-permute-done.20.refs_3_) | copy-start | bytes 6148

commit v3 on v0

--- a/solution.py
+++ b/solution.py
@@ -1,6 +1,10 @@
+import functools
+
 import jax
 import jax.numpy as jnp
 from jax import lax
+from jax.experimental import pallas as pl
+from jax.experimental.pallas import tpu as pltpu
 from jax.sharding import PartitionSpec as P
 
 TOPNODES = 4
@@ -19,7 +23,7 @@
     return (onehot, hit_mask, select, select * weight_te[:, :, None])
 
 
-def per_device(grad_out, routes, combine, hidden_cache, down_weight):
+def routed(grad_out, routes, combine, hidden_cache, down_weight):
     node_count = lax.axis_size("node")
     local_count = lax.axis_size("local")
     experts_all = node_count * local_count
@@ -77,6 +81,239 @@
     return (d_hidden, d_combine)
 
 
+LANES = 128
+LINE = 4
+WORK_BYTES = 16 * 1024 * 1024
+CHUNK = 256
+
+
+def pack_kernel(rows_hbm, routes_hbm, combine_hbm, block_ref, routes_ref, combine_ref, sems):
+    copies = [
+        pltpu.make_async_copy(routes_hbm, routes_ref, sems.at[0]),
+        pltpu.make_async_copy(combine_hbm, combine_ref, sems.at[1]),
+        pltpu.make_async_copy(rows_hbm, block_ref.at[:, LANES:], sems.at[2]),
+    ]
+    for copy in copies:
+        copy.start()
+    for copy in copies[:2]:
+        copy.wait()
+    top, tokens = routes_ref.shape
+    table = jnp.concatenate(
+        [routes_ref[...].astype(jnp.float32), combine_ref[...].astype(jnp.float32)], axis=0
+    )
+    table = jnp.concatenate([table] * (LANES // tokens), axis=1)
+    fill = jnp.zeros((block_ref.shape[0] - 2 * top, LANES), jnp.float32)
+    block_ref[:, :LANES] = jnp.concatenate([table, fill], axis=0).astype(block_ref.dtype)
+    copies[2].wait()
+
+
+def load_kernel(weight_hbm, cache_hbm, weight_ref, cache_ref, sems):
+    copies = [
+        pltpu.make_async_copy(weight_hbm, weight_ref, sems.at[0]),
+        pltpu.make_async_copy(cache_hbm, cache_ref, sems.at[1]),
+    ]
+    for copy in copies:
+        copy.start()
+    for copy in copies:
+        copy.wait()
+
+
+def pick_rows(blocks, expert, capacity, picked, at):
+    tokens = blocks[0].shape[0]
+    top = tokens // 4
+    span = len(blocks) * tokens
+    rows = len(blocks) * capacity
+    owner = lax.broadcasted_iota(jnp.int32, (1, span), 1) // tokens
+    earlier = lax.broadcasted_iota(jnp.int32, (span, span), 0)
+    later = lax.broadcasted_iota(jnp.int32, (span, span), 1)
+    before = ((earlier < later) & (earlier // tokens == later // tokens)).astype(jnp.bfloat16)
+    table = jnp.zeros((2 * top, span), jnp.float32)
+    for i, block in enumerate(blocks):
+        table = jnp.where(owner == i, block[: 2 * top, :LANES].astype(jnp.float32)[:, :span], table)
+    match = (table[:top] == expert).astype(jnp.float32)
+    hit = jnp.sum(match, axis=0, keepdims=True)
+    weight = jnp.sum(match * table[top:], axis=0, keepdims=True)
+    rank = jnp.dot(
+        jnp.broadcast_to(hit, (top, span)).astype(jnp.bfloat16),
+        before,
+        preferred_element_type=jnp.float32,
+    )[:1]
+    target = rank + (owner * capacity).astype(jnp.float32)
+    slot_of = lax.broadcasted_iota(jnp.int32, (rows, span), 0).astype(jnp.float32)
+    choose = jnp.where((slot_of == target) & (hit > 0), jnp.float32(1), jnp.float32(0))
+    source_rows = jnp.concatenate([block[:, LANES:] for block in blocks], axis=0)
+    picked[at : at + rows, :] = jnp.dot(
+        choose.astype(jnp.bfloat16), source_rows, preferred_element_type=jnp.float32
+    ).astype(jnp.bfloat16)
+    return choose, jnp.sum(choose * weight, axis=1, keepdims=True)
+
+
+def source_start(source, capacity):
+    i, j = source
+    index = (lax.axis_index("node") ^ i) * LINE + (lax.axis_index("local") ^ j)
+    return pl.multiple_of(index * capacity, capacity)
+
+
+def multiply_groups(groups, blocks, weights, cache, picked, rows_ref):
+    hidden = weights.shape[0]
+    capacity = blocks[0].shape[0] // 2
+    expert = (lax.axis_index("node") * LINE + lax.axis_index("local")).astype(jnp.float32)
+    chosen, scales, places = [], [], []
+    for group in groups:
+        at = len(places)
+        choose, scale = pick_rows(
+            blocks[at : at + len(group)], expert, capacity, picked, at * capacity
+        )
+        chosen.append(choose)
+        scales.append(scale)
+        places += [source_start(source, capacity) for source in group]
+    scale = jnp.concatenate(scales, axis=0)
+    terms = jnp.zeros((len(places) * capacity, 1), jnp.float32)
+    for c in range(0, hidden, CHUNK):
+        part = slice(c, c + CHUNK)
+        products = lax.dot_general(
+            picked[...], weights[part, :], (((1,), (1,)), ((), ())), preferred_element_type=jnp.float32
+        )
+        kept = [cache[pl.ds(place, capacity), part] for place in places]
+        kept = jnp.concatenate(kept, axis=0).astype(jnp.float32)
+        terms = terms + jnp.sum(products * kept, axis=1, keepdims=True)
+        rows_ref[:, part] = (scale * products).astype(rows_ref.dtype)
+    results, at = [], 0
+    for choose in chosen:
+        rows = choose.shape[0]
+        results.append(jnp.sum(choose * terms[at : at + rows], axis=0, keepdims=True))
+        at += rows
+    return results
+
+
+def expert_kernel(groups, *refs):
+    count = sum(len(group) for group in groups)
+    blocks = refs[:count]
+    weights, cache, rows_ref, *term_refs, picked = refs[count:]
+    terms = multiply_groups(groups, blocks, weights, cache, picked, rows_ref)
+    for term_ref, term in zip(term_refs, terms):
+        term_ref[...] = term
+
+
+def place_kernel(groups, rows_ref, out_ref):
+    sources = [source for group in groups for source in group]
+    capacity = out_ref.shape[0] // len(sources)
+    for s, source in enumerate(sources):
+        out_ref[pl.ds(source_start(source, capacity), capacity), :] = rows_ref[
+            s * capacity : (s + 1) * capacity, :
+        ]
+
+
+def exchanged(grad_out, routes, combine, hidden_cache, down_weight):
+    nodes = lax.axis_size("node")
+    node = lax.axis_index("node")
+    local = lax.axis_index("local")
+    tokens, width = grad_out.shape
+    hidden = down_weight.shape[1]
+    slots = hidden_cache.shape[1]
+    capacity = slots // (nodes * LINE)
+    vmem = pl.BlockSpec(memory_space=pltpu.VMEM)
+    hbm = pl.BlockSpec(memory_space=pltpu.HBM)
+    params = pltpu.CompilerParams(vmem_limit_bytes=WORK_BYTES)
+    free = pl.CostEstimate(flops=1, bytes_accessed=1, transcendentals=0)
+
+    def move(x, node_mask, local_mask):
+        pairs = [
+            (n * LINE + l, (n ^ node_mask) * LINE + (l ^ local_mask))
+            for n in range(nodes)
+            for l in range(LINE)
+        ]
+        return lax.ppermute(x, ("node", "local"), pairs)
+
+    def after(x, *others):
+        return lax.optimization_barrier((x, *others))[0]
+
+    def over_nodes(x, *gates):
+        across = move(x, 2, 0)
+        across_beside = move(after(across, *gates), 1, 0)
+        return [x, move(x, 1, 0), across, across_beside]
+
+    def pinned(x, space=pltpu.HBM):
+        return pltpu.with_memory_space_constraint(x, space)
+
+    def multiply(groups, blocks):
+        rows = len(blocks) * capacity
+        return pl.pallas_call(
+            functools.partial(expert_kernel, groups),
+            out_shape=[jax.ShapeDtypeStruct((rows, hidden), jnp.bfloat16)]
+            + [jax.ShapeDtypeStruct((1, len(group) * tokens), jnp.float32) for group in groups],
+            in_specs=[vmem] * (len(blocks) + 2),
+            out_specs=[vmem] * (1 + len(groups)),
+            scratch_shapes=[
+                pltpu.VMEM((rows, width), jnp.bfloat16),
+            ],
+            compiler_params=params,
+            cost_estimate=free,
+        )(*blocks, pinned(weights, pltpu.VMEM), pinned(cache, pltpu.VMEM))
+
+    routes_t = routes.T
+    block = pl.pallas_call(
+        pack_kernel,
+        out_shape=pltpu.VMEM((tokens, LANES + width), grad_out.dtype),
+        in_specs=[hbm] * 3,
+        out_specs=vmem,
+        scratch_shapes=[
+            pltpu.VMEM(routes_t.shape, routes.dtype),
+            pltpu.VMEM(routes_t.shape, combine.dtype),
+            pltpu.SemaphoreType.DMA((3,)),
+        ],
+        compiler_params=params,
+    )(pinned(grad_out), pinned(routes_t), pinned(combine.T))
+    weights, cache = pl.pallas_call(
+        load_kernel,
+        out_shape=[
+            pltpu.VMEM((hidden, width), down_weight.dtype),
+            pltpu.VMEM((slots, hidden), hidden_cache.dtype),
+        ],
+        in_specs=[hbm] * 2,
+        out_specs=[vmem] * 2,
+        scratch_shapes=[pltpu.SemaphoreType.DMA((2,))],
+        compiler_params=params,
+        cost_estimate=free,
+    )(pinned(down_weight[0]), pinned(hidden_cache[0]))
+
+    order = (1, 3, 2)
+    groups = [[(i, j) for i in range(nodes)] for j in (0, *order)]
+    far = {j: move(block, 0, j) for j in order}
+    blocks = over_nodes(block)
+    for j in order:
+        blocks += over_nodes(after(far[j], blocks[1]) if j == 1 else far[j], *([cache] if j == 2 else []))
+    all_rows, *terms = multiply(groups, blocks)
+    d_hidden = pl.pallas_call(
+        functools.partial(place_kernel, groups),
+        out_shape=jax.ShapeDtypeStruct((slots, hidden), jnp.bfloat16),
+        in_specs=[vmem],
+        out_specs=vmem,
+        compiler_params=params,
+        cost_estimate=free,
+    )(all_rows)
+
+    back = [terms[0]] + [move(term, 0, j) for j, term in zip(order, terms[1:])]
+    back = jnp.concatenate(back, axis=0)
+    back, routes_t, node, local = lax.optimization_barrier((back, routes_t, node, local))
+    d_combine_t = jnp.zeros(routes_t.shape, jnp.float32)
+    for i in range(nodes):
+        returned = (move(back, i, 0) if i else back)[:, i * tokens : (i + 1) * tokens]
+        for g, j in enumerate((0, *order)):
+            expert = (node ^ i) * LINE + (local ^ j)
+            d_combine_t += jnp.where(routes_t == expert, returned[g], jnp.float32(0))
+    return d_hidden[None], d_combine_t.T
+
+
+def per_device(grad_out, routes, combine, hidden_cache, down_weight):
+    nodes = lax.axis_size("node")
+    locals_ = lax.axis_size("local")
+    tokens, top = routes.shape
+    if nodes == TOPNODES == 4 and locals_ == LINE and nodes * tokens == LANES and tokens == 4 * top:
+        return exchanged(grad_out, routes, combine, hidden_cache, down_weight)
+    return routed(grad_out, routes, combine, hidden_cache, down_weight)
+
+
 def solution(mesh):
     placed = (
         P(("rep", "node", "local"), None),

time: 106 us -> 54.7 us (0.52)
  waiting for transfers between devices: 59.4 us -> 21 us
  blocking collectives: 14.3 us -> 0 us
  matrix products: 8.36 us -> 0 us
  Pallas kernels: 0 us -> 8.27 us
  starting transfers between devices: 16.6 us -> 23.7 us
  local copies, waits for them, and re-layouts: 3.65 us -> 0.23 us
  other arithmetic: 2.3 us -> 0.63 us
    all_to_all x4 -> x0, waiting for transfers between devices: 59.4 us -> none  [the longest x1 41.1 us: per_device(): lax.all_to_all(row_block, 'local', split_axis=1, concat_axis=1, tiled=True)]
    ppermute x0 -> x21, starting transfers between devices: none -> 23.7 us  [move(): return lax.ppermute(x, ('node', 'local'), pairs)]
    ppermute x0 -> x21, waiting for transfers between devices: none -> 21 us  [move(): return lax.ppermute(x, ('node', 'local'), pairs)]
    all_to_all x4 -> x0, starting transfers between devices: 16.6 us -> none  [the longest x1 5.34 us: per_device(): lax.all_to_all(weights, 'local', split_axis=1, concat_axis=1, tiled=True)]
    all_to_all x2 -> x0, blocking collectives: 14.3 us -> none  [the longest x1 8.11 us: per_device(): lax.all_to_all(lax.all_to_all(slot_terms, 'node', split_axis=0, concat_ax...]
    dot_general x5 -> x0, matrix products: 8.36 us -> none  [the longest x1 6.09 us: per_device(): lax.dot_general(flat_rows, down_weight[0], (((1,), (1,)), ((), ())), pref...]
    pallas_call x0 -> x4, Pallas kernels: none -> 8.27 us  [the longest x1 3.29 us: multiply(): pl.pallas_call(functools.partial(expert_kernel, groups), out_shape=[jax.S...]
    reshape x4 -> x0, local copies, waits for them, and re-layouts: 2.16 us -> none  [the longest x1 1.38 us: per_device(): row_block = row_block.reshape(node_count, local_count, capacity, width)]
  transfers between devices with their start and end apart: 4 -> 21, of which waited for: 4 -> 10; matrix products, arithmetic and copies ran while one was open for 4% -> 0% of each run, Pallas kernels for 0% -> 7%
where the time goes in v3:
time: 54.7 us; the launch traced here: 54.6 us
  starting transfers between devices  23.7 us (43%)
  waiting for transfers between devices  21 us (38%)
  Pallas kernels  8.27 us (15%)
  between operations  0.73 us (1%)
  other arithmetic  0.63 us (1%)
    ppermute x21, starting transfers between devices, move(): return lax.ppermute(x, ('node', 'local'), pairs)  23.7 us
    ppermute x21, waiting for transfers between devices, move(): return lax.ppermute(x, ('node', 'local'), pairs)  21 us
    pallas_call x1, Pallas kernels, multiply(): pl.pallas_call(functools.partial(expert_kernel, groups), out_shape=[jax.S...  3.29 us
    pallas_call x1, Pallas kernels, exchanged(): pl.pallas_call(load_kernel, out_shape=[pltpu.VMEM((hidden, width), down_w...  3.15 us
  transfers between devices with their start and end apart: 21, of which 10 were waited for; matrix products, arithmetic and copies ran while one was open for 0% of the time, Pallas kernels for 7%

profile of v3, /device:TPU:0, one launch (start us, length us, event | category | flops | bytes accessed | tf_op | source)
XLA Modules:
  0.0 54.6 jit_solution(6259908842321647105)
XLA Ops:
  0.6 1.0 %shard_map.68.refs_0_ = bf16[32,3712]{1,0:T(8,128)(2,1)S(1)} custom-call(bf16[32,3584]{1,0:T(8,128)(2,1)} %rows_hbm.1, s32[8,32]{1,0:T(8,128)} %bitcast.42, bf16[8,32]{1,0:T(8,128)(2,1)} %bitcast.44), custom_call_target="tpu_custom_call" | custom-call | tf_op jit(solution)/shard_map/pallas_call | solution.py:255
  1.6 4.1 %collective-permute-start.11 = (bf16[32,3712]{1,0:T(8,128)(2,1)S(1)}, bf16[32,3712]{1,0:T(8,128)(2,1)S(1)}, u32[]{:S(2)}, u32[]{:S(2)}) collective-permute-start(bf16[32,3712]{1,0:T(8,128)(2,1)S(1)} %shard_map.68.refs_0_), channel_id=1, source_target_pairs={{0,2},{1,3},{2,0},{3,1},{4,6},{5,7},{6,4},{7,5},{8,10},{9,11},{10,... | collective-permute-start | bytes 712712 | tf_op jit(solution)/shard_map/ppermute | solution.py:226
  5.7 0.0 collective-permute-start
  5.7 1.6 %collective-permute-start.3 = (bf16[32,3712]{1,0:T(8,128)(2,1)S(1)}, bf16[32,3712]{1,0:T(8,128)(2,1)S(1)}, u32[]{:S(2)}, u32[]{:S(2)}) collective-permute-start(bf16[32,3712]{1,0:T(8,128)(2,1)S(1)} %shard_map.68.refs_0_), channel_id=1, source_target_pairs={{0,1},{1,0},{2,3},{3,2},{4,5},{5,4},{6,7},{7,6},{8,9},{9,8},{10,11... | collective-permute-start | bytes 712712 | tf_op jit(solution)/shard_map/ppermute | solution.py:226
  7.3 0.0 collective-permute-start.7
  7.4 1.7 %collective-permute-start.1 = (bf16[32,3712]{1,0:T(8,128)(2,1)S(1)}, bf16[32,3712]{1,0:T(8,128)(2,1)S(1)}, u32[]{:S(2)}, u32[]{:S(2)}) collective-permute-start(bf16[32,3712]{1,0:T(8,128)(2,1)S(1)} %shard_map.68.refs_0_), channel_id=1, source_target_pairs={{0,8},{1,9},{2,10},{3,11},{4,12},{5,13},{6,14},{7,15},{8,0},{9,1},... | collective-permute-start | bytes 712712 | tf_op jit(solution)/shard_map/ppermute | solution.py:226
  9.0 9.3 %collective-permute-done.11.refs_12_ = bf16[32,3712]{1,0:T(8,128)(2,1)S(1)} collective-permute-done((bf16[32,3712]{1,0:T(8,128)(2,1)S(1)}, bf16[32,3712]{1,0:T(8,128)(2,1)S(1)}, u32[]{:S(2)}, u32[]{:S(2)}) %collective-permute-start.11) | collective-permute-done | bytes 237600 | tf_op jit(solution)/shard_map/ppermute | solution.py:226
  18.3 6.1 %collective-permute-start.13 = (bf16[32,3712]{1,0:T(8,128)(2,1)S(1)}, bf16[32,3712]{1,0:T(8,128)(2,1)S(1)}, u32[]{:S(2)}, u32[]{:S(2)}) collective-permute-start(bf16[32,3712]{1,0:T(8,128)(2,1)S(1)} %collective-permute-done.11.refs_12_), channel_id=1, source_target_pairs={{0,8},{1,9},{2,10},{3,11},{4,12},{5,13},{6,14},{7,15},{8,0},{9,1},... | collective-permute-start | bytes 712712 | tf_op jit(solution)/shard_map/ppermute | solution.py:226
  24.5 0.0 collective-permute-done.refs_1_
  24.5 0.0 collective-permute-done.3.refs_4_
  24.5 0.1 collective-permute-start.5
  24.5 0.0 collective-permute-done.7.refs_8_
  24.5 2.0 %collective-permute-start.9 = (bf16[32,3712]{1,0:T(8,128)(2,1)S(1)}, bf16[32,3712]{1,0:T(8,128)(2,1)S(1)}, u32[]{:S(2)}, u32[]{:S(2)}) collective-permute-start(bf16[32,3712]{1,0:T(8,128)(2,1)S(1)} %collective-permute-done.7.refs_8_), channel_id=1, source_target_pairs={{0,8},{1,9},{2,10},{3,11},{4,12},{5,13},{6,14},{7,15},{8,0},{9,1},... | collective-permute-start | bytes 712712 | tf_op jit(solution)/shard_map/ppermute | solution.py:226
  26.5 0.5 collective-permute-start.12
  27.0 3.1 %shard_map.69 = (bf16[1024,3584]{1,0:T(8,128)(2,1)S(1)}, bf16[256,1024]{1,0:T(8,128)(2,1)S(1)}) custom-call(bf16[1024,3584]{1,0:T(8,128)(2,1)} %bitcast.39, bf16[256,1024]{1,0:T(8,128)(2,1)} %bitcast.41), custom_call_target="tpu_custom_call" | custom-call | flops 1 | bytes 1 | tf_op jit(solution)/shard_map/pallas_call | solution.py:267
  30.2 0.0 copy-start
  30.2 0.0 collective-permute-done.13.refs_14_
  30.2 0.1 collective-permute-start.2
  30.3 1.8 %collective-permute-done.5.refs_6_ = bf16[32,3712]{1,0:T(8,128)(2,1)S(1)} collective-permute-done((bf16[32,3712]{1,0:T(8,128)(2,1)S(1)}, bf16[32,3712]{1,0:T(8,128)(2,1)S(1)}, u32[]{:S(2)}, u32[]{:S(2)}) %collective-permute-start.5) | collective-permute-done | bytes 237600 | tf_op jit(solution)/shard_map/ppermute | solution.py:226
  32.1 0.0 collective-permute-start.8
  32.1 2.5 %collective-permute-done.9.refs_10_ = bf16[32,3712]{1,0:T(8,128)(2,1)S(1)} collective-permute-done((bf16[32,3712]{1,0:T(8,128)(2,1)S(1)}, bf16[32,3712]{1,0:T(8,128)(2,1)S(1)}, u32[]{:S(2)}, u32[]{:S(2)}) %collective-permute-start.9) | collective-permute-done | bytes 237600 | tf_op jit(solution)/shard_map/ppermute | solution.py:226
  34.6 0.0 collective-permute-start.6
  34.6 0.0 collective-permute-done.4.refs_5_
  34.6 0.5 collective-permute-start.14
  35.1 0.0 collective-permute-done.12.refs_13_
  35.2 0.1 collective-permute-start.10
  35.2 0.0 collective-permute-done.2.refs_3_
  35.2 0.9 %collective-permute-done.6.refs_7_ = bf16[32,3712]{1,0:T(8,128)(2,1)S(1)} collective-permute-done((bf16[32,3712]{1,0:T(8,128)(2,1)S(1)}, bf16[32,3712]{1,0:T(8,128)(2,1)S(1)}, u32[]{:S(2)}, u32[]{:S(2)}) %collective-permute-start.6) | collective-permute-done | bytes 237600 | tf_op jit(solution)/shard_map/ppermute | solution.py:226
  36.1 0.3 collective-permute-done.14.refs_15_
  36.5 0.3 collective-permute-done.10.refs_11_
  36.8 3.3 %shard_map.70 = (bf16[256,1024]{1,0:T(8,128)(2,1)S(1)}, f32[1,128]{1,0:T(1,128)S(1)}, f32[1,128]{1,0:T(1,128)S(1)}, f32[1,128]{1,0:T(1,128)S(1)}, f32[1,128]{1,0:T(1,128)S(1)}) custom-call(bf16[32,3712]{1,0:T(8,128)(2,1)S(1)} %shard_map.68.refs_0_, bf16[32,3712]{1,0:T(8,128)(2,1)S(1)} %collective-permute-done.refs_1_, ...), custom_call_target="tpu_custom_call" | custom-call | flops 1 | bytes 1 | tf_op jit(solution)/shard_map/pallas_call | solution.py:241
  40.1 1.2 %collective-permute-start.15 = (f32[1,128]{1,0:T(1,128)S(1)}, f32[1,128]{1,0:T(1,128)S(1)}, u32[]{:S(2)}, u32[]{:S(2)}) collective-permute-start(f32[1,128]{1,0:T(1,128)S(1)} %get-tuple-element.21), channel_id=1, source_target_pairs={{0,1},{1,0},{2,3},{3,2},{4,5},{5,4},{6,7},{7,6},{8,9},{9,8},{10,11... | collective-permute-start | bytes 1544 | tf_op jit(solution)/shard_map/ppermute | solution.py:226
  41.3 3.4 %collective-permute-start.16 = (f32[1,128]{1,0:T(1,128)S(1)}, f32[1,128]{1,0:T(1,128)S(1)}, u32[]{:S(2)}, u32[]{:S(2)}) collective-permute-start(f32[1,128]{1,0:T(1,128)S(1)} %get-tuple-element.22), channel_id=1, source_target_pairs={{0,3},{1,2},{2,1},{3,0},{4,7},{5,6},{6,5},{7,4},{8,11},{9,10},{10,... | collective-permute-start | bytes 1544 | tf_op jit(solution)/shard_map/ppermute | solution.py:226
  44.7 0.5 collective-permute-start.17
  45.2 0.8 %shard_map.71 = bf16[256,1024]{1,0:T(8,128)(2,1)} custom-call(bf16[256,1024]{1,0:T(8,128)(2,1)S(1)} %get-tuple-element.19.rows_ref), custom_call_target="tpu_custom_call" | custom-call | flops 1 | bytes 1 | tf_op jit(solution)/shard_map/pallas_call | solution.py:287
  46.1 0.0 collective-permute-done.15
  46.1 0.6 %collective-permute-done.16 = f32[1,128]{1,0:T(1,128)S(1)} collective-permute-done((f32[1,128]{1,0:T(1,128)S(1)}, f32[1,128]{1,0:T(1,128)S(1)}, u32[]{:S(2)}, u32[]{:S(2)}) %collective-permute-start.16) | collective-permute-done | bytes 544 | tf_op jit(solution)/shard_map/ppermute | solution.py:226
  46.7 2.5 %collective-permute-done.17 = f32[1,128]{1,0:T(1,128)S(1)} collective-permute-done((f32[1,128]{1,0:T(1,128)S(1)}, f32[1,128]{1,0:T(1,128)S(1)}, u32[]{:S(2)}, u32[]{:S(2)}) %collective-permute-start.17) | collective-permute-done | bytes 544 | tf_op jit(solution)/shard_map/ppermute | solution.py:226
  49.2 0.1 collective-permute-start.18
  49.3 1.6 %collective-permute-start.19 = (f32[4,128]{1,0:T(4,128)S(1)}, f32[4,128]{1,0:T(4,128)S(1)}, u32[]{:S(2)}, u32[]{:S(2)}) collective-permute-start(f32[4,128]{1,0:T(4,128)S(1)} %pad_maximum_fusion), channel_id=1, source_target_pairs={{0,8},{1,9},{2,10},{3,11},{4,12},{5,13},{6,14},{7,15},{8,0},{9,1},... | collective-permute-start | bytes 6152 | tf_op jit(solution)/shard_map/ppermute | solution.py:226
  50.9 0.3 collective-permute-start.20
  51.1 0.0 collective-permute-done.18
  51.2 0.1 slice_bitcast_fusion.11
  51.2 1.7 %collective-permute-done.19 = f32[4,128]{1,0:T(4,128)S(1)} collective-permute-done((f32[4,128]{1,0:T(4,128)S(1)}, f32[4,128]{1,0:T(4,128)S(1)}, u32[]{:S(2)}, u32[]{:S(2)}) %collective-permute-start.19) | collective-permute-done | bytes 2080 | tf_op jit(solution)/shard_map/ppermute | solution.py:226
  53.0 0.1 slice_bitcast_fusion.7
  53.0 0.8 %collective-permute-done.20 = f32[4,128]{1,0:T(4,128)S(1)} collective-permute-done((f32[4,128]{1,0:T(4,128)S(1)}, f32[4,128]{1,0:T(4,128)S(1)}, u32[]{:S(2)}, u32[]{:S(2)}) %collective-permute-start.20) | collective-permute-done | bytes 2080 | tf_op jit(solution)/shard_map/ppermute | solution.py:226
  53.9 0.1 slice_bitcast_fusion.3
  53.9 0.6 %add_bitcast_fusion = f32[32,8]{0,1:T(8,128)} fusion(s32[8,32]{1,0:T(8,128)S(1)} %bitcast.43, f32[32]{0:T(128)S(1)} %get-tuple-element.41, s32[]{:T(128)S(6)} %add.122, f32[32]{0:T(128)S(1)} %get-tuple-element.42, s32[]{:T(128)S(6)} %add.120, f32[32]{0:T(128)S(1)} %get-tuple-element.43, s32[]{:T(128)S(6)} %add.118, f32[32]{0:T(128)S(1)} %get-tuple-element.40, ...), kind=kLoop, calls=%fused_computation | loop fusion | flops 12032 | bytes 4160 | tf_op jit(solution)/shard_map/transpose | solution.py:305
  (6 shorter events, 0.0 us)
Async XLA Ops:
  1.6 16.7 %collective-permute-start.11 = (bf16[32,3712]{1,0:T(8,128)(2,1)S(1)}, bf16[32,3712]{1,0:T(8,128)(2,1)S(1)}, u32[]{:S(2)}, u32[]{:S(2)}) collective-permute-start(bf16[32,3712]{1,0:T(8,128)(2,1)S(1)} %shard_map.68.refs_0_), channel_id=1, source_target_pairs={{0,2},{1,3},{2,0},{3,1},{4,6},{5,7},{6,4},{7,5},{8,10},{9,11},{10,... | collective-permute-start | bytes 712712 | tf_op jit(solution)/shard_map/ppermute | solution.py:226
  5.7 18.7 %collective-permute-start = (bf16[32,3712]{1,0:T(8,128)(2,1)S(1)}, bf16[32,3712]{1,0:T(8,128)(2,1)S(1)}, u32[]{:S(2)}, u32[]{:S(2)}) collective-permute-start(bf16[32,3712]{1,0:T(8,128)(2,1)S(1)} %shard_map.68.refs_0_), channel_id=1, source_target_pairs={{0,4},{1,5},{2,6},{3,7},{4,0},{5,1},{6,2},{7,3},{8,12},{9,13},{10,... | collective-permute-start | bytes 712712 | tf_op jit(solution)/shard_map/ppermute | solution.py:226
  5.7 18.7 %collective-permute-start.3 = (bf16[32,3712]{1,0:T(8,128)(2,1)S(1)}, bf16[32,3712]{1,0:T(8,128)(2,1)S(1)}, u32[]{:S(2)}, u32[]{:S(2)}) collective-permute-start(bf16[32,3712]{1,0:T(8,128)(2,1)S(1)} %shard_map.68.refs_0_), channel_id=1, source_target_pairs={{0,1},{1,0},{2,3},{3,2},{4,5},{5,4},{6,7},{7,6},{8,9},{9,8},{10,11... | collective-permute-start | bytes 712712 | tf_op jit(solution)/shard_map/ppermute | solution.py:226
  7.3 17.2 %collective-permute-start.7 = (bf16[32,3712]{1,0:T(8,128)(2,1)S(1)}, bf16[32,3712]{1,0:T(8,128)(2,1)S(1)}, u32[]{:S(2)}, u32[]{:S(2)}) collective-permute-start(bf16[32,3712]{1,0:T(8,128)(2,1)S(1)} %shard_map.68.refs_0_), channel_id=1, source_target_pairs={{0,3},{1,2},{2,1},{3,0},{4,7},{5,6},{6,5},{7,4},{8,11},{9,10},{10,... | collective-permute-start | bytes 712712 | tf_op jit(solution)/shard_map/ppermute | solution.py:226
  7.4 19.1 %collective-permute-start.1 = (bf16[32,3712]{1,0:T(8,128)(2,1)S(1)}, bf16[32,3712]{1,0:T(8,128)(2,1)S(1)}, u32[]{:S(2)}, u32[]{:S(2)}) collective-permute-start(bf16[32,3712]{1,0:T(8,128)(2,1)S(1)} %shard_map.68.refs_0_), channel_id=1, source_target_pairs={{0,8},{1,9},{2,10},{3,11},{4,12},{5,13},{6,14},{7,15},{8,0},{9,1},... | collective-permute-start | bytes 712712 | tf_op jit(solution)/shard_map/ppermute | solution.py:226
  18.3 11.8 %collective-permute-start.13 = (bf16[32,3712]{1,0:T(8,128)(2,1)S(1)}, bf16[32,3712]{1,0:T(8,128)(2,1)S(1)}, u32[]{:S(2)}, u32[]{:S(2)}) collective-permute-start(bf16[32,3712]{1,0:T(8,128)(2,1)S(1)} %collective-permute-done.11.refs_12_), channel_id=1, source_target_pairs={{0,8},{1,9},{2,10},{3,11},{4,12},{5,13},{6,14},{7,15},{8,0},{9,1},... | collective-permute-start | bytes 712712 | tf_op jit(solution)/shard_map/ppermute | solution.py:226
  24.5 7.6 %collective-permute-start.5 = (bf16[32,3712]{1,0:T(8,128)(2,1)S(1)}, bf16[32,3712]{1,0:T(8,128)(2,1)S(1)}, u32[]{:S(2)}, u32[]{:S(2)}) collective-permute-start(bf16[32,3712]{1,0:T(8,128)(2,1)S(1)} %collective-permute-done.3.refs_4_), channel_id=1, source_target_pairs={{0,8},{1,9},{2,10},{3,11},{4,12},{5,13},{6,14},{7,15},{8,0},{9,1},... | collective-permute-start | bytes 712712 | tf_op jit(solution)/shard_map/ppermute | solution.py:226
  24.5 10.1 %collective-permute-start.9 = (bf16[32,3712]{1,0:T(8,128)(2,1)S(1)}, bf16[32,3712]{1,0:T(8,128)(2,1)S(1)}, u32[]{:S(2)}, u32[]{:S(2)}) collective-permute-start(bf16[32,3712]{1,0:T(8,128)(2,1)S(1)} %collective-permute-done.7.refs_8_), channel_id=1, source_target_pairs={{0,8},{1,9},{2,10},{3,11},{4,12},{5,13},{6,14},{7,15},{8,0},{9,1},... | collective-permute-start | bytes 712712 | tf_op jit(solution)/shard_map/ppermute | solution.py:226
  26.5 8.1 %collective-permute-start.4 = (bf16[32,3712]{1,0:T(8,128)(2,1)S(1)}, bf16[32,3712]{1,0:T(8,128)(2,1)S(1)}, u32[]{:S(2)}, u32[]{:S(2)}) collective-permute-start(bf16[32,3712]{1,0:T(8,128)(2,1)S(1)} %collective-permute-done.3.refs_4_), channel_id=1, source_target_pairs={{0,4},{1,5},{2,6},{3,7},{4,0},{5,1},{6,2},{7,3},{8,12},{9,13},{10,... | collective-permute-start | bytes 712712 | tf_op jit(solution)/shard_map/ppermute | solution.py:226
  26.5 8.6 %collective-permute-start.12 = (bf16[32,3712]{1,0:T(8,128)(2,1)S(1)}, bf16[32,3712]{1,0:T(8,128)(2,1)S(1)}, u32[]{:S(2)}, u32[]{:S(2)}) collective-permute-start(bf16[32,3712]{1,0:T(8,128)(2,1)S(1)} %collective-permute-done.11.refs_12_), channel_id=1, source_target_pairs={{0,4},{1,5},{2,6},{3,7},{4,0},{5,1},{6,2},{7,3},{8,12},{9,13},{10,... | collective-permute-start | bytes 712712 | tf_op jit(solution)/shard_map/ppermute | solution.py:226
  30.2 23.8 %copy-start = (s32[32,8]{0,1:T(8,128)S(1)}, s32[32,8]{0,1:T(8,128)}, u32[]{:S(2)}) copy-start(s32[32,8]{0,1:T(8,128)} %param.6) | copy-start | bytes 3076
  30.2 5.0 %collective-permute-start.2 = (bf16[32,3712]{1,0:T(8,128)(2,1)S(1)}, bf16[32,3712]{1,0:T(8,128)(2,1)S(1)}, u32[]{:S(2)}, u32[]{:S(2)}) collective-permute-start(bf16[32,3712]{1,0:T(8,128)(2,1)S(1)} %collective-permute-done.1.refs_2_), channel_id=1, source_target_pairs={{0,4},{1,5},{2,6},{3,7},{4,0},{5,1},{6,2},{7,3},{8,12},{9,13},{10,... | collective-permute-start | bytes 712712 | tf_op jit(solution)/shard_map/ppermute | solution.py:226
  32.1 3.1 %collective-permute-start.8 = (bf16[32,3712]{1,0:T(8,128)(2,1)S(1)}, bf16[32,3712]{1,0:T(8,128)(2,1)S(1)}, u32[]{:S(2)}, u32[]{:S(2)}) collective-permute-start(bf16[32,3712]{1,0:T(8,128)(2,1)S(1)} %collective-permute-done.7.refs_8_), channel_id=1, source_target_pairs={{0,4},{1,5},{2,6},{3,7},{4,0},{5,1},{6,2},{7,3},{8,12},{9,13},{10,... | collective-permute-start | bytes 712712 | tf_op jit(solution)/shard_map/ppermute | solution.py:226
  34.6 1.5 %collective-permute-start.6 = (bf16[32,3712]{1,0:T(8,128)(2,1)S(1)}, bf16[32,3712]{1,0:T(8,128)(2,1)S(1)}, u32[]{:S(2)}, u32[]{:S(2)}) collective-permute-start(bf16[32,3712]{1,0:T(8,128)(2,1)S(1)} %collective-permute-done.5.refs_6_), channel_id=1, source_target_pairs={{0,4},{1,5},{2,6},{3,7},{4,0},{5,1},{6,2},{7,3},{8,12},{9,13},{10,... | collective-permute-start | bytes 712712 | tf_op jit(solution)/shard_map/ppermute | solution.py:226
  34.6 1.8 %collective-permute-start.14 = (bf16[32,3712]{1,0:T(8,128)(2,1)S(1)}, bf16[32,3712]{1,0:T(8,128)(2,1)S(1)}, u32[]{:S(2)}, u32[]{:S(2)}) collective-permute-start(bf16[32,3712]{1,0:T(8,128)(2,1)S(1)} %collective-permute-done.13.refs_14_), channel_id=1, source_target_pairs={{0,4},{1,5},{2,6},{3,7},{4,0},{5,1},{6,2},{7,3},{8,12},{9,13},{10,... | collective-permute-start | bytes 712712 | tf_op jit(solution)/shard_map/ppermute | solution.py:226
  35.2 1.7 %collective-permute-start.10 = (bf16[32,3712]{1,0:T(8,128)(2,1)S(1)}, bf16[32,3712]{1,0:T(8,128)(2,1)S(1)}, u32[]{:S(2)}, u32[]{:S(2)}) collective-permute-start(bf16[32,3712]{1,0:T(8,128)(2,1)S(1)} %collective-permute-done.9.refs_10_), channel_id=1, source_target_pairs={{0,4},{1,5},{2,6},{3,7},{4,0},{5,1},{6,2},{7,3},{8,12},{9,13},{10,... | collective-permute-start | bytes 712712 | tf_op jit(solution)/shard_map/ppermute | solution.py:226
  40.1 6.0 %collective-permute-start.15 = (f32[1,128]{1,0:T(1,128)S(1)}, f32[1,128]{1,0:T(1,128)S(1)}, u32[]{:S(2)}, u32[]{:S(2)}) collective-permute-start(f32[1,128]{1,0:T(1,128)S(1)} %get-tuple-element.21), channel_id=1, source_target_pairs={{0,1},{1,0},{2,3},{3,2},{4,5},{5,4},{6,7},{7,6},{8,9},{9,8},{10,11... | collective-permute-start | bytes 1544 | tf_op jit(solution)/shard_map/ppermute | solution.py:226
  41.3 5.3 %collective-permute-start.16 = (f32[1,128]{1,0:T(1,128)S(1)}, f32[1,128]{1,0:T(1,128)S(1)}, u32[]{:S(2)}, u32[]{:S(2)}) collective-permute-start(f32[1,128]{1,0:T(1,128)S(1)} %get-tuple-element.22), channel_id=1, source_target_pairs={{0,3},{1,2},{2,1},{3,0},{4,7},{5,6},{6,5},{7,4},{8,11},{9,10},{10,... | collective-permute-start | bytes 1544 | tf_op jit(solution)/shard_map/ppermute | solution.py:226
  44.7 4.4 %collective-permute-start.17 = (f32[1,128]{1,0:T(1,128)S(1)}, f32[1,128]{1,0:T(1,128)S(1)}, u32[]{:S(2)}, u32[]{:S(2)}) collective-permute-start(f32[1,128]{1,0:T(1,128)S(1)} %get-tuple-element.23), channel_id=1, source_target_pairs={{0,2},{1,3},{2,0},{3,1},{4,6},{5,7},{6,4},{7,5},{8,10},{9,11},{10,... | collective-permute-start | bytes 1544 | tf_op jit(solution)/shard_map/ppermute | solution.py:226
  49.2 2.0 %collective-permute-start.18 = (f32[4,128]{1,0:T(4,128)S(1)}, f32[4,128]{1,0:T(4,128)S(1)}, u32[]{:S(2)}, u32[]{:S(2)}) collective-permute-start(f32[4,128]{1,0:T(4,128)S(1)} %pad_maximum_fusion), channel_id=1, source_target_pairs={{0,4},{1,5},{2,6},{3,7},{4,0},{5,1},{6,2},{7,3},{8,12},{9,13},{10,... | collective-permute-start | bytes 6152 | tf_op jit(solution)/shard_map/ppermute | solution.py:226
  49.3 3.7 %collective-permute-start.19 = (f32[4,128]{1,0:T(4,128)S(1)}, f32[4,128]{1,0:T(4,128)S(1)}, u32[]{:S(2)}, u32[]{:S(2)}) collective-permute-start(f32[4,128]{1,0:T(4,128)S(1)} %pad_maximum_fusion), channel_id=1, source_target_pairs={{0,8},{1,9},{2,10},{3,11},{4,12},{5,13},{6,14},{7,15},{8,0},{9,1},... | collective-permute-start | bytes 6152 | tf_op jit(solution)/shard_map/ppermute | solution.py:226
  50.9 3.0 %collective-permute-start.20 = (f32[4,128]{1,0:T(4,128)S(1)}, f32[4,128]{1,0:T(4,128)S(1)}, u32[]{:S(2)}, u32[]{:S(2)}) collective-permute-start(f32[4,128]{1,0:T(4,128)S(1)} %pad_maximum_fusion), channel_id=1, source_target_pairs={{0,12},{1,13},{2,14},{3,15},{4,8},{5,9},{6,10},{7,11},{8,4},{9,5},... | collective-permute-start | bytes 6152 | tf_op jit(solution)/shard_map/ppermute | solution.py:226

commit v4 on v3

--- a/solution.py
+++ b/solution.py
@@ -277,12 +277,12 @@
         cost_estimate=free,
     )(pinned(down_weight[0]), pinned(hidden_cache[0]))
 
-    order = (1, 3, 2)
+    order = (2, 3, 1)
     groups = [[(i, j) for i in range(nodes)] for j in (0, *order)]
     far = {j: move(block, 0, j) for j in order}
     blocks = over_nodes(block)
     for j in order:
-        blocks += over_nodes(after(far[j], blocks[1]) if j == 1 else far[j], *([cache] if j == 2 else []))
+        blocks += over_nodes(after(far[j], blocks[1]) if j == 1 else far[j], *([cache] if j == 3 else []))
     all_rows, *terms = multiply(groups, blocks)
     d_hidden = pl.pallas_call(
         functools.partial(place_kernel, groups),

time: 54.7 us -> 51.6 us (0.943)
  starting transfers between devices: 23.7 us -> 19.1 us
  waiting for transfers between devices: 21 us -> 22.5 us
    ppermute x21, starting transfers between devices: 23.7 us -> 19.1 us  [move(): return lax.ppermute(x, ('node', 'local'), pairs)]
    ppermute x21, waiting for transfers between devices: 21 us -> 22.5 us  [move(): return lax.ppermute(x, ('node', 'local'), pairs)]
  transfers between devices with their start and end apart: 21 -> 21, of which waited for: 10 -> 11; matrix products, arithmetic and copies ran while one was open for 0% -> 0% of each run, Pallas kernels for 7% -> 8%
where the time goes in v4:
time: 51.6 us; the launch traced here: 51.5 us
  waiting for transfers between devices  22.5 us (44%)
  starting transfers between devices  19.1 us (37%)
  Pallas kernels  8.27 us (16%)
  between operations  0.74 us (1%)
  other arithmetic  0.63 us (1%)
    ppermute x21, waiting for transfers between devices, move(): return lax.ppermute(x, ('node', 'local'), pairs)  22.5 us
    ppermute x21, starting transfers between devices, move(): return lax.ppermute(x, ('node', 'local'), pairs)  19.1 us
    pallas_call x1, Pallas kernels, multiply(): pl.pallas_call(functools.partial(expert_kernel, groups), out_shape=[jax.S...  3.29 us
    pallas_call x1, Pallas kernels, exchanged(): pl.pallas_call(load_kernel, out_shape=[pltpu.VMEM((hidden, width), down_w...  3.15 us
  transfers between devices with their start and end apart: 21, of which 11 were waited for; matrix products, arithmetic and copies ran while one was open for 0% of the time, Pallas kernels for 8%

profile of v4, /device:TPU:0, one launch (start us, length us, event | category | flops | bytes accessed | tf_op | source)
XLA Modules:
  0.0 51.5 jit_solution(5265881918493205896)
XLA Ops:
  0.6 1.0 %shard_map.68.refs_0_ = bf16[32,3712]{1,0:T(8,128)(2,1)S(1)} custom-call(bf16[32,3584]{1,0:T(8,128)(2,1)} %rows_hbm.1, s32[8,32]{1,0:T(8,128)} %bitcast.42, bf16[8,32]{1,0:T(8,128)(2,1)} %bitcast.44), custom_call_target="tpu_custom_call" | custom-call | tf_op jit(solution)/shard_map/pallas_call | solution.py:255
  1.6 5.1 %collective-permute-start.7 = (bf16[32,3712]{1,0:T(8,128)(2,1)S(1)}, bf16[32,3712]{1,0:T(8,128)(2,1)S(1)}, u32[]{:S(2)}, u32[]{:S(2)}) collective-permute-start(bf16[32,3712]{1,0:T(8,128)(2,1)S(1)} %shard_map.68.refs_0_), channel_id=1, source_target_pairs={{0,3},{1,2},{2,1},{3,0},{4,7},{5,6},{6,5},{7,4},{8,11},{9,10},{10,... | collective-permute-start | bytes 712712 | tf_op jit(solution)/shard_map/ppermute | solution.py:226
  6.8 0.0 collective-permute-start
  6.8 0.0 collective-permute-start.11
  6.8 0.7 %collective-permute-start.3 = (bf16[32,3712]{1,0:T(8,128)(2,1)S(1)}, bf16[32,3712]{1,0:T(8,128)(2,1)S(1)}, u32[]{:S(2)}, u32[]{:S(2)}) collective-permute-start(bf16[32,3712]{1,0:T(8,128)(2,1)S(1)} %shard_map.68.refs_0_), channel_id=1, source_target_pairs={{0,2},{1,3},{2,0},{3,1},{4,6},{5,7},{6,4},{7,5},{8,10},{9,11},{10,... | collective-permute-start | bytes 712712 | tf_op jit(solution)/shard_map/ppermute | solution.py:226
  7.5 1.6 %collective-permute-start.1 = (bf16[32,3712]{1,0:T(8,128)(2,1)S(1)}, bf16[32,3712]{1,0:T(8,128)(2,1)S(1)}, u32[]{:S(2)}, u32[]{:S(2)}) collective-permute-start(bf16[32,3712]{1,0:T(8,128)(2,1)S(1)} %shard_map.68.refs_0_), channel_id=1, source_target_pairs={{0,8},{1,9},{2,10},{3,11},{4,12},{5,13},{6,14},{7,15},{8,0},{9,1},... | collective-permute-start | bytes 712712 | tf_op jit(solution)/shard_map/ppermute | solution.py:226
  9.0 4.4 %collective-permute-done.7.refs_8_ = bf16[32,3712]{1,0:T(8,128)(2,1)S(1)} collective-permute-done((bf16[32,3712]{1,0:T(8,128)(2,1)S(1)}, bf16[32,3712]{1,0:T(8,128)(2,1)S(1)}, u32[]{:S(2)}, u32[]{:S(2)}) %collective-permute-start.7) | collective-permute-done | bytes 237600 | tf_op jit(solution)/shard_map/ppermute | solution.py:226
  13.4 1.7 %collective-permute-start.9 = (bf16[32,3712]{1,0:T(8,128)(2,1)S(1)}, bf16[32,3712]{1,0:T(8,128)(2,1)S(1)}, u32[]{:S(2)}, u32[]{:S(2)}) collective-permute-start(bf16[32,3712]{1,0:T(8,128)(2,1)S(1)} %collective-permute-done.7.refs_8_), channel_id=1, source_target_pairs={{0,8},{1,9},{2,10},{3,11},{4,12},{5,13},{6,14},{7,15},{8,0},{9,1},... | collective-permute-start | bytes 712712 | tf_op jit(solution)/shard_map/ppermute | solution.py:226
  15.1 0.0 collective-permute-done.refs_1_
  15.1 3.6 %collective-permute-done.11.refs_12_ = bf16[32,3712]{1,0:T(8,128)(2,1)S(1)} collective-permute-done((bf16[32,3712]{1,0:T(8,128)(2,1)S(1)}, bf16[32,3712]{1,0:T(8,128)(2,1)S(1)}, u32[]{:S(2)}, u32[]{:S(2)}) %collective-permute-start.11) | collective-permute-done | bytes 237600 | tf_op jit(solution)/shard_map/ppermute | solution.py:226
  18.7 1.4 %collective-permute-start.13 = (bf16[32,3712]{1,0:T(8,128)(2,1)S(1)}, bf16[32,3712]{1,0:T(8,128)(2,1)S(1)}, u32[]{:S(2)}, u32[]{:S(2)}) collective-permute-start(bf16[32,3712]{1,0:T(8,128)(2,1)S(1)} %collective-permute-done.11.refs_12_), channel_id=1, source_target_pairs={{0,8},{1,9},{2,10},{3,11},{4,12},{5,13},{6,14},{7,15},{8,0},{9,1},... | collective-permute-start | bytes 712712 | tf_op jit(solution)/shard_map/ppermute | solution.py:226
  20.1 6.8 %collective-permute-done.3.refs_4_ = bf16[32,3712]{1,0:T(8,128)(2,1)S(1)} collective-permute-done((bf16[32,3712]{1,0:T(8,128)(2,1)S(1)}, bf16[32,3712]{1,0:T(8,128)(2,1)S(1)}, u32[]{:S(2)}, u32[]{:S(2)}) %collective-permute-start.3) | collective-permute-done | bytes 237600 | tf_op jit(solution)/shard_map/ppermute | solution.py:226
  27.0 1.5 %collective-permute-start.5 = (bf16[32,3712]{1,0:T(8,128)(2,1)S(1)}, bf16[32,3712]{1,0:T(8,128)(2,1)S(1)}, u32[]{:S(2)}, u32[]{:S(2)}) collective-permute-start(bf16[32,3712]{1,0:T(8,128)(2,1)S(1)} %collective-permute-done.3.refs_4_), channel_id=1, source_target_pairs={{0,8},{1,9},{2,10},{3,11},{4,12},{5,13},{6,14},{7,15},{8,0},{9,1},... | collective-permute-start | bytes 712712 | tf_op jit(solution)/shard_map/ppermute | solution.py:226
  28.4 0.0 collective-permute-start.12
  28.4 0.0 collective-permute-done.1.refs_2_
  28.5 0.5 collective-permute-start.4
  29.0 3.1 %shard_map.69 = (bf16[1024,3584]{1,0:T(8,128)(2,1)S(1)}, bf16[256,1024]{1,0:T(8,128)(2,1)S(1)}) custom-call(bf16[1024,3584]{1,0:T(8,128)(2,1)} %bitcast.39, bf16[256,1024]{1,0:T(8,128)(2,1)} %bitcast.41), custom_call_target="tpu_custom_call" | custom-call | flops 1 | bytes 1 | tf_op jit(solution)/shard_map/pallas_call | solution.py:267
  32.1 0.0 copy-start
  32.1 0.1 collective-permute-start.2
  32.2 0.5 collective-permute-start.8
  32.7 1.1 %collective-permute-done.5.refs_6_ = bf16[32,3712]{1,0:T(8,128)(2,1)S(1)} collective-permute-done((bf16[32,3712]{1,0:T(8,128)(2,1)S(1)}, bf16[32,3712]{1,0:T(8,128)(2,1)S(1)}, u32[]{:S(2)}, u32[]{:S(2)}) %collective-permute-start.5) | collective-permute-done | bytes 237600 | tf_op jit(solution)/shard_map/ppermute | solution.py:226
  33.8 0.0 collective-permute-start.14
  33.8 0.0 collective-permute-done.12.refs_13_
  33.8 0.5 collective-permute-start.10
  34.3 0.0 collective-permute-done.4.refs_5_
  34.3 0.1 collective-permute-start.6
  34.4 0.0 collective-permute-done.2.refs_3_
  34.4 0.9 %collective-permute-done.14.refs_15_ = bf16[32,3712]{1,0:T(8,128)(2,1)S(1)} collective-permute-done((bf16[32,3712]{1,0:T(8,128)(2,1)S(1)}, bf16[32,3712]{1,0:T(8,128)(2,1)S(1)}, u32[]{:S(2)}, u32[]{:S(2)}) %collective-permute-start.14) | collective-permute-done | bytes 237600 | tf_op jit(solution)/shard_map/ppermute | solution.py:226
  35.3 0.3 collective-permute-done.10.refs_11_
  35.6 0.3 collective-permute-done.6.refs_7_
  36.0 3.3 %shard_map.70 = (bf16[256,1024]{1,0:T(8,128)(2,1)S(1)}, f32[1,128]{1,0:T(1,128)S(1)}, f32[1,128]{1,0:T(1,128)S(1)}, f32[1,128]{1,0:T(1,128)S(1)}, f32[1,128]{1,0:T(1,128)S(1)}) custom-call(bf16[32,3712]{1,0:T(8,128)(2,1)S(1)} %shard_map.68.refs_0_, bf16[32,3712]{1,0:T(8,128)(2,1)S(1)} %collective-permute-done.refs_1_, ...), custom_call_target="tpu_custom_call" | custom-call | flops 1 | bytes 1 | tf_op jit(solution)/shard_map/pallas_call | solution.py:241
  39.3 1.5 %collective-permute-start.15 = (f32[1,128]{1,0:T(1,128)S(1)}, f32[1,128]{1,0:T(1,128)S(1)}, u32[]{:S(2)}, u32[]{:S(2)}) collective-permute-start(f32[1,128]{1,0:T(1,128)S(1)} %get-tuple-element.21), channel_id=1, source_target_pairs={{0,2},{1,3},{2,0},{3,1},{4,6},{5,7},{6,4},{7,5},{8,10},{9,11},{10,... | collective-permute-start | bytes 1544 | tf_op jit(solution)/shard_map/ppermute | solution.py:226
  40.7 1.5 %collective-permute-start.16 = (f32[1,128]{1,0:T(1,128)S(1)}, f32[1,128]{1,0:T(1,128)S(1)}, u32[]{:S(2)}, u32[]{:S(2)}) collective-permute-start(f32[1,128]{1,0:T(1,128)S(1)} %get-tuple-element.22), channel_id=1, source_target_pairs={{0,3},{1,2},{2,1},{3,0},{4,7},{5,6},{6,5},{7,4},{8,11},{9,10},{10,... | collective-permute-start | bytes 1544 | tf_op jit(solution)/shard_map/ppermute | solution.py:226
  42.3 0.6 %collective-permute-start.17 = (f32[1,128]{1,0:T(1,128)S(1)}, f32[1,128]{1,0:T(1,128)S(1)}, u32[]{:S(2)}, u32[]{:S(2)}) collective-permute-start(f32[1,128]{1,0:T(1,128)S(1)} %get-tuple-element.23), channel_id=1, source_target_pairs={{0,1},{1,0},{2,3},{3,2},{4,5},{5,4},{6,7},{7,6},{8,9},{9,8},{10,11... | collective-permute-start | bytes 1544 | tf_op jit(solution)/shard_map/ppermute | solution.py:226
  42.8 0.8 %shard_map.71 = bf16[256,1024]{1,0:T(8,128)(2,1)} custom-call(bf16[256,1024]{1,0:T(8,128)(2,1)S(1)} %get-tuple-element.19.rows_ref), custom_call_target="tpu_custom_call" | custom-call | flops 1 | bytes 1 | tf_op jit(solution)/shard_map/pallas_call | solution.py:287
  43.6 0.1 collective-permute-done.15
  43.8 2.3 %collective-permute-done.16 = f32[1,128]{1,0:T(1,128)S(1)} collective-permute-done((f32[1,128]{1,0:T(1,128)S(1)}, f32[1,128]{1,0:T(1,128)S(1)}, u32[]{:S(2)}, u32[]{:S(2)}) %collective-permute-start.16) | collective-permute-done | bytes 544 | tf_op jit(solution)/shard_map/ppermute | solution.py:226
  46.1 0.0 collective-permute-done.17
  46.1 0.1 collective-permute-start.18
  46.2 1.6 %collective-permute-start.19 = (f32[4,128]{1,0:T(4,128)S(1)}, f32[4,128]{1,0:T(4,128)S(1)}, u32[]{:S(2)}, u32[]{:S(2)}) collective-permute-start(f32[4,128]{1,0:T(4,128)S(1)} %pad_maximum_fusion), channel_id=1, source_target_pairs={{0,8},{1,9},{2,10},{3,11},{4,12},{5,13},{6,14},{7,15},{8,0},{9,1},... | collective-permute-start | bytes 6152 | tf_op jit(solution)/shard_map/ppermute | solution.py:226
  47.7 0.3 collective-permute-start.20
  48.0 0.0 collective-permute-done.18
  48.0 0.1 slice_bitcast_fusion.11
  48.1 1.7 %collective-permute-done.19 = f32[4,128]{1,0:T(4,128)S(1)} collective-permute-done((f32[4,128]{1,0:T(4,128)S(1)}, f32[4,128]{1,0:T(4,128)S(1)}, u32[]{:S(2)}, u32[]{:S(2)}) %collective-permute-start.19) | collective-permute-done | bytes 2080 | tf_op jit(solution)/shard_map/ppermute | solution.py:226
  49.8 0.1 slice_bitcast_fusion.7
  49.9 0.8 %collective-permute-done.20 = f32[4,128]{1,0:T(4,128)S(1)} collective-permute-done((f32[4,128]{1,0:T(4,128)S(1)}, f32[4,128]{1,0:T(4,128)S(1)}, u32[]{:S(2)}, u32[]{:S(2)}) %collective-permute-start.20) | collective-permute-done | bytes 2080 | tf_op jit(solution)/shard_map/ppermute | solution.py:226
  50.8 0.1 slice_bitcast_fusion.3
  50.8 0.6 %add_bitcast_fusion = f32[32,8]{0,1:T(8,128)} fusion(s32[8,32]{1,0:T(8,128)S(1)} %bitcast.43, f32[32]{0:T(128)S(1)} %get-tuple-element.41, s32[]{:T(128)S(6)} %add.122, f32[32]{0:T(128)S(1)} %get-tuple-element.42, s32[]{:T(128)S(6)} %add.120, f32[32]{0:T(128)S(1)} %get-tuple-element.43, s32[]{:T(128)S(6)} %add.118, f32[32]{0:T(128)S(1)} %get-tuple-element.40, ...), kind=kLoop, calls=%fused_computation | loop fusion | flops 12032 | bytes 4160 | tf_op jit(solution)/shard_map/transpose | solution.py:305
  (6 shorter events, 0.0 us)
Async XLA Ops:
  1.6 11.8 %collective-permute-start.7 = (bf16[32,3712]{1,0:T(8,128)(2,1)S(1)}, bf16[32,3712]{1,0:T(8,128)(2,1)S(1)}, u32[]{:S(2)}, u32[]{:S(2)}) collective-permute-start(bf16[32,3712]{1,0:T(8,128)(2,1)S(1)} %shard_map.68.refs_0_), channel_id=1, source_target_pairs={{0,3},{1,2},{2,1},{3,0},{4,7},{5,6},{6,5},{7,4},{8,11},{9,10},{10,... | collective-permute-start | bytes 712712 | tf_op jit(solution)/shard_map/ppermute | solution.py:226
  6.8 8.3 %collective-permute-start = (bf16[32,3712]{1,0:T(8,128)(2,1)S(1)}, bf16[32,3712]{1,0:T(8,128)(2,1)S(1)}, u32[]{:S(2)}, u32[]{:S(2)}) collective-permute-start(bf16[32,3712]{1,0:T(8,128)(2,1)S(1)} %shard_map.68.refs_0_), channel_id=1, source_target_pairs={{0,4},{1,5},{2,6},{3,7},{4,0},{5,1},{6,2},{7,3},{8,12},{9,13},{10,... | collective-permute-start | bytes 712712 | tf_op jit(solution)/shard_map/ppermute | solution.py:226
  6.8 12.0 %collective-permute-start.11 = (bf16[32,3712]{1,0:T(8,128)(2,1)S(1)}, bf16[32,3712]{1,0:T(8,128)(2,1)S(1)}, u32[]{:S(2)}, u32[]{:S(2)}) collective-permute-start(bf16[32,3712]{1,0:T(8,128)(2,1)S(1)} %shard_map.68.refs_0_), channel_id=1, source_target_pairs={{0,1},{1,0},{2,3},{3,2},{4,5},{5,4},{6,7},{7,6},{8,9},{9,8},{10,11... | collective-permute-start | bytes 712712 | tf_op jit(solution)/shard_map/ppermute | solution.py:226
  6.8 20.2 %collective-permute-start.3 = (bf16[32,3712]{1,0:T(8,128)(2,1)S(1)}, bf16[32,3712]{1,0:T(8,128)(2,1)S(1)}, u32[]{:S(2)}, u32[]{:S(2)}) collective-permute-start(bf16[32,3712]{1,0:T(8,128)(2,1)S(1)} %shard_map.68.refs_0_), channel_id=1, source_target_pairs={{0,2},{1,3},{2,0},{3,1},{4,6},{5,7},{6,4},{7,5},{8,10},{9,11},{10,... | collective-permute-start | bytes 712712 | tf_op jit(solution)/shard_map/ppermute | solution.py:226
  7.5 21.0 %collective-permute-start.1 = (bf16[32,3712]{1,0:T(8,128)(2,1)S(1)}, bf16[32,3712]{1,0:T(8,128)(2,1)S(1)}, u32[]{:S(2)}, u32[]{:S(2)}) collective-permute-start(bf16[32,3712]{1,0:T(8,128)(2,1)S(1)} %shard_map.68.refs_0_), channel_id=1, source_target_pairs={{0,8},{1,9},{2,10},{3,11},{4,12},{5,13},{6,14},{7,15},{8,0},{9,1},... | collective-permute-start | bytes 712712 | tf_op jit(solution)/shard_map/ppermute | solution.py:226
  13.4 18.7 %collective-permute-start.9 = (bf16[32,3712]{1,0:T(8,128)(2,1)S(1)}, bf16[32,3712]{1,0:T(8,128)(2,1)S(1)}, u32[]{:S(2)}, u32[]{:S(2)}) collective-permute-start(bf16[32,3712]{1,0:T(8,128)(2,1)S(1)} %collective-permute-done.7.refs_8_), channel_id=1, source_target_pairs={{0,8},{1,9},{2,10},{3,11},{4,12},{5,13},{6,14},{7,15},{8,0},{9,1},... | collective-permute-start | bytes 712712 | tf_op jit(solution)/shard_map/ppermute | solution.py:226
  18.7 13.5 %collective-permute-start.13 = (bf16[32,3712]{1,0:T(8,128)(2,1)S(1)}, bf16[32,3712]{1,0:T(8,128)(2,1)S(1)}, u32[]{:S(2)}, u32[]{:S(2)}) collective-permute-start(bf16[32,3712]{1,0:T(8,128)(2,1)S(1)} %collective-permute-done.11.refs_12_), channel_id=1, source_target_pairs={{0,8},{1,9},{2,10},{3,11},{4,12},{5,13},{6,14},{7,15},{8,0},{9,1},... | collective-permute-start | bytes 712712 | tf_op jit(solution)/shard_map/ppermute | solution.py:226
  27.0 6.8 %collective-permute-start.5 = (bf16[32,3712]{1,0:T(8,128)(2,1)S(1)}, bf16[32,3712]{1,0:T(8,128)(2,1)S(1)}, u32[]{:S(2)}, u32[]{:S(2)}) collective-permute-start(bf16[32,3712]{1,0:T(8,128)(2,1)S(1)} %collective-permute-done.3.refs_4_), channel_id=1, source_target_pairs={{0,8},{1,9},{2,10},{3,11},{4,12},{5,13},{6,14},{7,15},{8,0},{9,1},... | collective-permute-start | bytes 712712 | tf_op jit(solution)/shard_map/ppermute | solution.py:226
  28.4 5.3 %collective-permute-start.12 = (bf16[32,3712]{1,0:T(8,128)(2,1)S(1)}, bf16[32,3712]{1,0:T(8,128)(2,1)S(1)}, u32[]{:S(2)}, u32[]{:S(2)}) collective-permute-start(bf16[32,3712]{1,0:T(8,128)(2,1)S(1)} %collective-permute-done.11.refs_12_), channel_id=1, source_target_pairs={{0,4},{1,5},{2,6},{3,7},{4,0},{5,1},{6,2},{7,3},{8,12},{9,13},{10,... | collective-permute-start | bytes 712712 | tf_op jit(solution)/shard_map/ppermute | solution.py:226
  28.5 5.9 %collective-permute-start.4 = (bf16[32,3712]{1,0:T(8,128)(2,1)S(1)}, bf16[32,3712]{1,0:T(8,128)(2,1)S(1)}, u32[]{:S(2)}, u32[]{:S(2)}) collective-permute-start(bf16[32,3712]{1,0:T(8,128)(2,1)S(1)} %collective-permute-done.3.refs_4_), channel_id=1, source_target_pairs={{0,4},{1,5},{2,6},{3,7},{4,0},{5,1},{6,2},{7,3},{8,12},{9,13},{10,... | collective-permute-start | bytes 712712 | tf_op jit(solution)/shard_map/ppermute | solution.py:226
  32.1 18.7 %copy-start = (s32[32,8]{0,1:T(8,128)S(1)}, s32[32,8]{0,1:T(8,128)}, u32[]{:S(2)}) copy-start(s32[32,8]{0,1:T(8,128)} %param.6) | copy-start | bytes 3076
  32.1 2.2 %collective-permute-start.2 = (bf16[32,3712]{1,0:T(8,128)(2,1)S(1)}, bf16[32,3712]{1,0:T(8,128)(2,1)S(1)}, u32[]{:S(2)}, u32[]{:S(2)}) collective-permute-start(bf16[32,3712]{1,0:T(8,128)(2,1)S(1)} %collective-permute-done.1.refs_2_), channel_id=1, source_target_pairs={{0,4},{1,5},{2,6},{3,7},{4,0},{5,1},{6,2},{7,3},{8,12},{9,13},{10,... | collective-permute-start | bytes 712712 | tf_op jit(solution)/shard_map/ppermute | solution.py:226
  32.2 2.2 %collective-permute-start.8 = (bf16[32,3712]{1,0:T(8,128)(2,1)S(1)}, bf16[32,3712]{1,0:T(8,128)(2,1)S(1)}, u32[]{:S(2)}, u32[]{:S(2)}) collective-permute-start(bf16[32,3712]{1,0:T(8,128)(2,1)S(1)} %collective-permute-done.7.refs_8_), channel_id=1, source_target_pairs={{0,4},{1,5},{2,6},{3,7},{4,0},{5,1},{6,2},{7,3},{8,12},{9,13},{10,... | collective-permute-start | bytes 712712 | tf_op jit(solution)/shard_map/ppermute | solution.py:226
  33.8 1.5 %collective-permute-start.14 = (bf16[32,3712]{1,0:T(8,128)(2,1)S(1)}, bf16[32,3712]{1,0:T(8,128)(2,1)S(1)}, u32[]{:S(2)}, u32[]{:S(2)}) collective-permute-start(bf16[32,3712]{1,0:T(8,128)(2,1)S(1)} %collective-permute-done.13.refs_14_), channel_id=1, source_target_pairs={{0,4},{1,5},{2,6},{3,7},{4,0},{5,1},{6,2},{7,3},{8,12},{9,13},{10,... | collective-permute-start | bytes 712712 | tf_op jit(solution)/shard_map/ppermute | solution.py:226
  33.8 1.8 %collective-permute-start.10 = (bf16[32,3712]{1,0:T(8,128)(2,1)S(1)}, bf16[32,3712]{1,0:T(8,128)(2,1)S(1)}, u32[]{:S(2)}, u32[]{:S(2)}) collective-permute-start(bf16[32,3712]{1,0:T(8,128)(2,1)S(1)} %collective-permute-done.9.refs_10_), channel_id=1, source_target_pairs={{0,4},{1,5},{2,6},{3,7},{4,0},{5,1},{6,2},{7,3},{8,12},{9,13},{10,... | collective-permute-start | bytes 712712 | tf_op jit(solution)/shard_map/ppermute | solution.py:226
  34.3 1.7 %collective-permute-start.6 = (bf16[32,3712]{1,0:T(8,128)(2,1)S(1)}, bf16[32,3712]{1,0:T(8,128)(2,1)S(1)}, u32[]{:S(2)}, u32[]{:S(2)}) collective-permute-start(bf16[32,3712]{1,0:T(8,128)(2,1)S(1)} %collective-permute-done.5.refs_6_), channel_id=1, source_target_pairs={{0,4},{1,5},{2,6},{3,7},{4,0},{5,1},{6,2},{7,3},{8,12},{9,13},{10,... | collective-permute-start | bytes 712712 | tf_op jit(solution)/shard_map/ppermute | solution.py:226
  39.3 4.5 %collective-permute-start.15 = (f32[1,128]{1,0:T(1,128)S(1)}, f32[1,128]{1,0:T(1,128)S(1)}, u32[]{:S(2)}, u32[]{:S(2)}) collective-permute-start(f32[1,128]{1,0:T(1,128)S(1)} %get-tuple-element.21), channel_id=1, source_target_pairs={{0,2},{1,3},{2,0},{3,1},{4,6},{5,7},{6,4},{7,5},{8,10},{9,11},{10,... | collective-permute-start | bytes 1544 | tf_op jit(solution)/shard_map/ppermute | solution.py:226
  40.7 5.3 %collective-permute-start.16 = (f32[1,128]{1,0:T(1,128)S(1)}, f32[1,128]{1,0:T(1,128)S(1)}, u32[]{:S(2)}, u32[]{:S(2)}) collective-permute-start(f32[1,128]{1,0:T(1,128)S(1)} %get-tuple-element.22), channel_id=1, source_target_pairs={{0,3},{1,2},{2,1},{3,0},{4,7},{5,6},{6,5},{7,4},{8,11},{9,10},{10,... | collective-permute-start | bytes 1544 | tf_op jit(solution)/shard_map/ppermute | solution.py:226
  42.3 3.8 %collective-permute-start.17 = (f32[1,128]{1,0:T(1,128)S(1)}, f32[1,128]{1,0:T(1,128)S(1)}, u32[]{:S(2)}, u32[]{:S(2)}) collective-permute-start(f32[1,128]{1,0:T(1,128)S(1)} %get-tuple-element.23), channel_id=1, source_target_pairs={{0,1},{1,0},{2,3},{3,2},{4,5},{5,4},{6,7},{7,6},{8,9},{9,8},{10,11... | collective-permute-start | bytes 1544 | tf_op jit(solution)/shard_map/ppermute | solution.py:226
  46.1 2.0 %collective-permute-start.18 = (f32[4,128]{1,0:T(4,128)S(1)}, f32[4,128]{1,0:T(4,128)S(1)}, u32[]{:S(2)}, u32[]{:S(2)}) collective-permute-start(f32[4,128]{1,0:T(4,128)S(1)} %pad_maximum_fusion), channel_id=1, source_target_pairs={{0,4},{1,5},{2,6},{3,7},{4,0},{5,1},{6,2},{7,3},{8,12},{9,13},{10,... | collective-permute-start | bytes 6152 | tf_op jit(solution)/shard_map/ppermute | solution.py:226
  46.2 3.7 %collective-permute-start.19 = (f32[4,128]{1,0:T(4,128)S(1)}, f32[4,128]{1,0:T(4,128)S(1)}, u32[]{:S(2)}, u32[]{:S(2)}) collective-permute-start(f32[4,128]{1,0:T(4,128)S(1)} %pad_maximum_fusion), channel_id=1, source_target_pairs={{0,8},{1,9},{2,10},{3,11},{4,12},{5,13},{6,14},{7,15},{8,0},{9,1},... | collective-permute-start | bytes 6152 | tf_op jit(solution)/shard_map/ppermute | solution.py:226
  47.7 3.0 %collective-permute-start.20 = (f32[4,128]{1,0:T(4,128)S(1)}, f32[4,128]{1,0:T(4,128)S(1)}, u32[]{:S(2)}, u32[]{:S(2)}) collective-permute-start(f32[4,128]{1,0:T(4,128)S(1)} %pad_maximum_fusion), channel_id=1, source_target_pairs={{0,12},{1,13},{2,14},{3,15},{4,8},{5,9},{6,10},{7,11},{8,4},{9,5},... | collective-permute-start | bytes 6152 | tf_op jit(solution)/shard_map/ppermute | solution.py:226

commit v5 on v4

--- a/solution.py
+++ b/solution.py
@@ -154,20 +154,33 @@
     return pl.multiple_of(index * capacity, capacity)
 
 
-def multiply_groups(groups, blocks, weights, cache, picked, rows_ref):
+def pick_kernel(groups, *refs):
+    *blocks, picked, chosen_ref, scale_ref = refs
+    expert = (lax.axis_index("node") * LINE + lax.axis_index("local")).astype(jnp.float32)
+    capacity = blocks[0].shape[0] // 2
+    at = 0
+    for g, group in enumerate(groups):
+        mine = blocks[g * len(group) : (g + 1) * len(group)]
+        choose, scale = pick_rows(mine, expert, capacity, picked, at)
+        rows = choose.shape[0]
+        chosen_ref[at : at + rows, :] = choose
+        scale_ref[at : at + rows, :] = jnp.broadcast_to(scale, (rows, LANES))
+        at += rows
+
+
+def expert_kernel(groups, *refs):
+    members = len(groups[-1])
+    chosen_ref, scale_ref, weights, cache, _ = refs[:5]
+    blocks, rows_ref = refs[5 : 5 + members], refs[5 + members]
+    term_refs, picked = refs[6 + members : -1], refs[-1]
     hidden = weights.shape[0]
     capacity = blocks[0].shape[0] // 2
     expert = (lax.axis_index("node") * LINE + lax.axis_index("local")).astype(jnp.float32)
-    chosen, scales, places = [], [], []
-    for group in groups:
-        at = len(places)
-        choose, scale = pick_rows(
-            blocks[at : at + len(group)], expert, capacity, picked, at * capacity
-        )
-        chosen.append(choose)
-        scales.append(scale)
-        places += [source_start(source, capacity) for source in group]
-    scale = jnp.concatenate(scales, axis=0)
+    early = chosen_ref.shape[0]
+    choose, scale = pick_rows(blocks, expert, capacity, picked, early)
+    scale = jnp.concatenate([scale_ref[:, :1], scale], axis=0)
+    choose = jnp.concatenate([chosen_ref[...], choose], axis=0)
+    places = [source_start(source, capacity) for group in groups for source in group]
     terms = jnp.zeros((len(places) * capacity, 1), jnp.float32)
     for c in range(0, hidden, CHUNK):
         part = slice(c, c + CHUNK)
@@ -178,21 +191,10 @@
         kept = jnp.concatenate(kept, axis=0).astype(jnp.float32)
         terms = terms + jnp.sum(products * kept, axis=1, keepdims=True)
         rows_ref[:, part] = (scale * products).astype(rows_ref.dtype)
-    results, at = [], 0
-    for choose in chosen:
-        rows = choose.shape[0]
-        results.append(jnp.sum(choose * terms[at : at + rows], axis=0, keepdims=True))
-        at += rows
-    return results
-
-
-def expert_kernel(groups, *refs):
-    count = sum(len(group) for group in groups)
-    blocks = refs[:count]
-    weights, cache, rows_ref, *term_refs, picked = refs[count:]
-    terms = multiply_groups(groups, blocks, weights, cache, picked, rows_ref)
-    for term_ref, term in zip(term_refs, terms):
-        term_ref[...] = term
+    spread = choose * terms
+    rows = members * capacity
+    for g, term_ref in enumerate(term_refs):
+        term_ref[...] = jnp.sum(spread[g * rows : (g + 1) * rows], axis=0, keepdims=True)
 
 
 def place_kernel(groups, rows_ref, out_ref):
@@ -236,21 +238,6 @@
     def pinned(x, space=pltpu.HBM):
         return pltpu.with_memory_space_constraint(x, space)
 
-    def multiply(groups, blocks):
-        rows = len(blocks) * capacity
-        return pl.pallas_call(
-            functools.partial(expert_kernel, groups),
-            out_shape=[jax.ShapeDtypeStruct((rows, hidden), jnp.bfloat16)]
-            + [jax.ShapeDtypeStruct((1, len(group) * tokens), jnp.float32) for group in groups],
-            in_specs=[vmem] * (len(blocks) + 2),
-            out_specs=[vmem] * (1 + len(groups)),
-            scratch_shapes=[
-                pltpu.VMEM((rows, width), jnp.bfloat16),
-            ],
-            compiler_params=params,
-            cost_estimate=free,
-        )(*blocks, pinned(weights, pltpu.VMEM), pinned(cache, pltpu.VMEM))
-
     routes_t = routes.T
     block = pl.pallas_call(
         pack_kernel,
@@ -277,13 +264,42 @@
         cost_estimate=free,
     )(pinned(down_weight[0]), pinned(hidden_cache[0]))
 
-    order = (2, 3, 1)
-    groups = [[(i, j) for i in range(nodes)] for j in (0, *order)]
-    far = {j: move(block, 0, j) for j in order}
-    blocks = over_nodes(block)
-    for j in order:
-        blocks += over_nodes(after(far[j], blocks[1]) if j == 1 else far[j], *([cache] if j == 3 else []))
-    all_rows, *terms = multiply(groups, blocks)
+    early, late = (3, 1, 0), 2
+    order = (*[j for j in early if j], late)
+    groups = [[(i, j) for i in range(nodes)] for j in (*early, late)]
+    far = {j: move(block, 0, j) for j in (2, 3, 1)}
+    blocks = []
+    for j in early:
+        blocks += over_nodes(far[j] if j else block, *([cache] if j == early[0] else []))
+    rows = len(blocks) * capacity
+    picked, chosen, scales = pl.pallas_call(
+        functools.partial(pick_kernel, groups[:-1]),
+        out_shape=[
+            pltpu.VMEM((slots, width), jnp.bfloat16),
+            pltpu.VMEM((rows, LANES), jnp.float32),
+            pltpu.VMEM((rows, LANES), jnp.float32),
+        ],
+        in_specs=[vmem] * len(blocks),
+        out_specs=[vmem] * 3,
+        compiler_params=params,
+        cost_estimate=pl.CostEstimate(
+            flops=2 * rows * nodes * tokens * width, bytes_accessed=1 << 22, transcendentals=0
+        ),
+    )(*blocks)
+    blocks = over_nodes(far[late])
+    held = [chosen, scales, weights, cache, picked]
+    all_rows, *terms = pl.pallas_call(
+        functools.partial(expert_kernel, groups),
+        out_shape=[jax.ShapeDtypeStruct((slots, hidden), jnp.bfloat16)]
+        + [jax.ShapeDtypeStruct((1, nodes * tokens), jnp.float32)] * LINE
+        + [pltpu.VMEM(picked.shape, picked.dtype)],
+        in_specs=[vmem] * (nodes + len(held)),
+        out_specs=[vmem] * (2 + LINE),
+        input_output_aliases={len(held) - 1: 1 + LINE},
+        compiler_params=params,
+        cost_estimate=free,
+    )(*[pinned(x, pltpu.VMEM) for x in held], *blocks)
+    terms = dict(zip((*early, late), terms))
     d_hidden = pl.pallas_call(
         functools.partial(place_kernel, groups),
         out_shape=jax.ShapeDtypeStruct((slots, hidden), jnp.bfloat16),
@@ -293,7 +309,7 @@
         cost_estimate=free,
     )(all_rows)
 
-    back = [terms[0]] + [move(term, 0, j) for j, term in zip(order, terms[1:])]
+    back = [move(terms[j], 0, j) if j else terms[j] for j in (0, *order)]
     back = jnp.concatenate(back, axis=0)
     back, routes_t, node, local = lax.optimization_barrier((back, routes_t, node, local))
     d_combine_t = jnp.zeros(routes_t.shape, jnp.float32)
@@ -309,7 +325,8 @@
     nodes = lax.axis_size("node")
     locals_ = lax.axis_size("local")
     tokens, top = routes.shape
-    if nodes == TOPNODES == 4 and locals_ == LINE and nodes * tokens == LANES and tokens == 4 * top:
+    fits = nodes * tokens == LANES and tokens == 4 * top and hidden_cache.shape[1] == 8 * tokens
+    if nodes == TOPNODES == 4 and locals_ == LINE and fits:
         return exchanged(grad_out, routes, combine, hidden_cache, down_weight)
     return routed(grad_out, routes, combine, hidden_cache, down_weight)
 

time: 51.6 us -> 51.1 us (level)
  waiting for transfers between devices: 22.5 us -> 20.9 us
  starting transfers between devices: 19.1 us -> 20 us
    ppermute x21, waiting for transfers between devices: 22.5 us -> 20.9 us  [move(): return lax.ppermute(x, ('node', 'local'), pairs)]
    ppermute x21, starting transfers between devices: 19.1 us -> 20 us  [move(): return lax.ppermute(x, ('node', 'local'), pairs)]
    pallas_call x1 -> x2, Pallas kernels: 3.29 us -> 3.46 us  [the longest x1 2.5 us: exchanged(): pl.pallas_call(functools.partial(expert_kernel, groups), out_shape=[jax.S...]
  transfers between devices with their start and end apart: 21 -> 21, of which waited for: 11 -> 10; matrix products, arithmetic and copies ran while one was open for 0% -> 0% of each run, Pallas kernels for 8% -> 10%
where the time goes in v5:
time: 51.1 us; the launch traced here: 51 us
  waiting for transfers between devices  20.9 us (41%)
  starting transfers between devices  20 us (39%)
  Pallas kernels  8.44 us (17%)
  between operations  0.74 us (1%)
  other arithmetic  0.63 us (1%)
    ppermute x21, waiting for transfers between devices, move(): return lax.ppermute(x, ('node', 'local'), pairs)  20.9 us
    ppermute x21, starting transfers between devices, move(): return lax.ppermute(x, ('node', 'local'), pairs)  20 us
    pallas_call x1, Pallas kernels, exchanged(): pl.pallas_call(load_kernel, out_shape=[pltpu.VMEM((hidden, width), down_w...  3.15 us
    pallas_call x1, Pallas kernels, exchanged(): pl.pallas_call(functools.partial(expert_kernel, groups), out_shape=[jax.S...  2.5 us
  transfers between devices with their start and end apart: 21, of which 10 were waited for; matrix products, arithmetic and copies ran while one was open for 0% of the time, Pallas kernels for 10%

profile of v5, /device:TPU:0, one launch (start us, length us, event | category | flops | bytes accessed | tf_op | source)
XLA Modules:
  0.0 51.0 jit_solution(548034234921371574)
XLA Ops:
  0.6 1.0 %shard_map.68.refs_8_ = bf16[32,3712]{1,0:T(8,128)(2,1)S(1)} custom-call(bf16[32,3584]{1,0:T(8,128)(2,1)} %rows_hbm.1, s32[8,32]{1,0:T(8,128)} %bitcast.42, bf16[8,32]{1,0:T(8,128)(2,1)} %bitcast.44), custom_call_target="tpu_custom_call" | custom-call | tf_op jit(solution)/shard_map/pallas_call | solution.py:242
  1.6 5.1 %collective-permute-start = (bf16[32,3712]{1,0:T(8,128)(2,1)S(1)}, bf16[32,3712]{1,0:T(8,128)(2,1)S(1)}, u32[]{:S(2)}, u32[]{:S(2)}) collective-permute-start(bf16[32,3712]{1,0:T(8,128)(2,1)S(1)} %shard_map.68.refs_8_), channel_id=1, source_target_pairs={{0,3},{1,2},{2,1},{3,0},{4,7},{5,6},{6,5},{7,4},{8,11},{9,10},{10,... | collective-permute-start | bytes 712712 | tf_op jit(solution)/shard_map/ppermute | solution.py:228
  6.8 0.0 collective-permute-start.4
  6.8 0.6 %collective-permute-start.11 = (bf16[32,3712]{1,0:T(8,128)(2,1)S(1)}, bf16[32,3712]{1,0:T(8,128)(2,1)S(1)}, u32[]{:S(2)}, u32[]{:S(2)}) collective-permute-start(bf16[32,3712]{1,0:T(8,128)(2,1)S(1)} %shard_map.68.refs_8_), channel_id=1, source_target_pairs={{0,2},{1,3},{2,0},{3,1},{4,6},{5,7},{6,4},{7,5},{8,10},{9,11},{10,... | collective-permute-start | bytes 712712 | tf_op jit(solution)/shard_map/ppermute | solution.py:228
  7.4 1.6 %collective-permute-start.9 = (bf16[32,3712]{1,0:T(8,128)(2,1)S(1)}, bf16[32,3712]{1,0:T(8,128)(2,1)S(1)}, u32[]{:S(2)}, u32[]{:S(2)}) collective-permute-start(bf16[32,3712]{1,0:T(8,128)(2,1)S(1)} %shard_map.68.refs_8_), channel_id=1, source_target_pairs={{0,8},{1,9},{2,10},{3,11},{4,12},{5,13},{6,14},{7,15},{8,0},{9,1},... | collective-permute-start | bytes 712712 | tf_op jit(solution)/shard_map/ppermute | solution.py:228
  9.0 4.4 %collective-permute-done.refs_0_ = bf16[32,3712]{1,0:T(8,128)(2,1)S(1)} collective-permute-done((bf16[32,3712]{1,0:T(8,128)(2,1)S(1)}, bf16[32,3712]{1,0:T(8,128)(2,1)S(1)}, u32[]{:S(2)}, u32[]{:S(2)}) %collective-permute-start) | collective-permute-done | bytes 237600 | tf_op jit(solution)/shard_map/ppermute | solution.py:228
  13.4 1.7 %collective-permute-start.2 = (bf16[32,3712]{1,0:T(8,128)(2,1)S(1)}, bf16[32,3712]{1,0:T(8,128)(2,1)S(1)}, u32[]{:S(2)}, u32[]{:S(2)}) collective-permute-start(bf16[32,3712]{1,0:T(8,128)(2,1)S(1)} %collective-permute-done.refs_0_), channel_id=1, source_target_pairs={{0,8},{1,9},{2,10},{3,11},{4,12},{5,13},{6,14},{7,15},{8,0},{9,1},... | collective-permute-start | bytes 712712 | tf_op jit(solution)/shard_map/ppermute | solution.py:228
  15.1 3.6 %collective-permute-done.4.refs_4_ = bf16[32,3712]{1,0:T(8,128)(2,1)S(1)} collective-permute-done((bf16[32,3712]{1,0:T(8,128)(2,1)S(1)}, bf16[32,3712]{1,0:T(8,128)(2,1)S(1)}, u32[]{:S(2)}, u32[]{:S(2)}) %collective-permute-start.4) | collective-permute-done | bytes 237600 | tf_op jit(solution)/shard_map/ppermute | solution.py:228
  18.8 1.4 %collective-permute-start.6 = (bf16[32,3712]{1,0:T(8,128)(2,1)S(1)}, bf16[32,3712]{1,0:T(8,128)(2,1)S(1)}, u32[]{:S(2)}, u32[]{:S(2)}) collective-permute-start(bf16[32,3712]{1,0:T(8,128)(2,1)S(1)} %collective-permute-done.4.refs_4_), channel_id=1, source_target_pairs={{0,8},{1,9},{2,10},{3,11},{4,12},{5,13},{6,14},{7,15},{8,0},{9,1},... | collective-permute-start | bytes 712712 | tf_op jit(solution)/shard_map/ppermute | solution.py:228
  20.1 0.0 collective-permute-start.8
  20.1 6.8 %collective-permute-done.11.refs_5_ = bf16[32,3712]{1,0:T(8,128)(2,1)S(1)} collective-permute-done((bf16[32,3712]{1,0:T(8,128)(2,1)S(1)}, bf16[32,3712]{1,0:T(8,128)(2,1)S(1)}, u32[]{:S(2)}, u32[]{:S(2)}) %collective-permute-start.11) | collective-permute-done | bytes 237600 | tf_op jit(solution)/shard_map/ppermute | solution.py:228
  27.0 1.5 %collective-permute-start.13 = (bf16[32,3712]{1,0:T(8,128)(2,1)S(1)}, bf16[32,3712]{1,0:T(8,128)(2,1)S(1)}, u32[]{:S(2)}, u32[]{:S(2)}) collective-permute-start(bf16[32,3712]{1,0:T(8,128)(2,1)S(1)} %collective-permute-done.11.refs_5_), channel_id=1, source_target_pairs={{0,8},{1,9},{2,10},{3,11},{4,12},{5,13},{6,14},{7,15},{8,0},{9,1},... | collective-permute-start | bytes 712712 | tf_op jit(solution)/shard_map/ppermute | solution.py:228
  28.4 0.0 collective-permute-done.9.refs_10_
  28.4 0.0 collective-permute-start.1
  28.5 0.0 collective-permute-done.2.refs_2_
  28.5 0.5 collective-permute-start.5
  29.0 3.1 %shard_map.69 = (bf16[1024,3584]{1,0:T(8,128)(2,1)S(1)}, bf16[256,1024]{1,0:T(8,128)(2,1)S(1)}) custom-call(bf16[1024,3584]{1,0:T(8,128)(2,1)} %bitcast.39, bf16[256,1024]{1,0:T(8,128)(2,1)} %bitcast.41), custom_call_target="tpu_custom_call" | custom-call | flops 1 | bytes 1 | tf_op jit(solution)/shard_map/pallas_call | solution.py:254
  32.1 0.0 collective-permute-done.6.refs_6_
  32.1 0.1 collective-permute-start.10
  32.3 0.0 collective-permute-done.8.refs_9_
  32.3 0.4 collective-permute-start.3
  32.7 1.1 %collective-permute-done.13.refs_7_ = bf16[32,3712]{1,0:T(8,128)(2,1)S(1)} collective-permute-done((bf16[32,3712]{1,0:T(8,128)(2,1)S(1)}, bf16[32,3712]{1,0:T(8,128)(2,1)S(1)}, u32[]{:S(2)}, u32[]{:S(2)}) %collective-permute-start.13) | collective-permute-done | bytes 237600 | tf_op jit(solution)/shard_map/ppermute | solution.py:228
  33.8 0.0 collective-permute-start.7
  33.8 0.0 collective-permute-done.1.refs_1_
  33.8 0.5 collective-permute-start.12
  34.3 0.1 collective-permute-start.14
  34.4 0.0 collective-permute-done.10.refs_11_
  34.4 0.0 collective-permute-done.3.refs_3_
  34.4 0.9 %collective-permute-done.7.refs_7_ = bf16[32,3712]{1,0:T(8,128)(2,1)S(1)} collective-permute-done((bf16[32,3712]{1,0:T(8,128)(2,1)S(1)}, bf16[32,3712]{1,0:T(8,128)(2,1)S(1)}, u32[]{:S(2)}, u32[]{:S(2)}) %collective-permute-start.7) | collective-permute-done | bytes 237600 | tf_op jit(solution)/shard_map/ppermute | solution.py:228
  35.3 1.0 %shard_map.70 = (bf16[256,3584]{1,0:T(8,128)(2,1)S(1)}, f32[192,128]{1,0:T(8,128)S(1)}, f32[192,128]{1,0:T(8,128)S(1)}) custom-call(bf16[32,3712]{1,0:T(8,128)(2,1)S(1)} %collective-permute-done.refs_0_, bf16[32,3712]{1,0:T(8,128)(2,1)S(1)} %collective-permute-done.1.refs_1_, bf16[32,3712]{1,0:T(8,128)(2,1)S(1)} %collective-permute-done.2.refs_2_, ...), custom_call_target="tpu_custom_call" | custom-call | flops 176160768 | bytes 4194304 | tf_op jit(solution)/shard_map/pallas_call | solution.py:275
  36.3 0.0 collective-permute-done.12.refs_6_
  36.3 2.5 %shard_map.71 = (bf16[256,1024]{1,0:T(8,128)(2,1)S(1)}, f32[1,128]{1,0:T(1,128)S(1)}, f32[1,128]{1,0:T(1,128)S(1)}, f32[1,128]{1,0:T(1,128)S(1)}, f32[1,128]{1,0:T(1,128)S(1)}, /*index=5*/bf16[256,3584]{1,0:T(8,128)(2,1)S(1)}) custom-call(f32[192,128]{1,0:T(8,128)S(1)} %get-tuple-element.19.refs_0_, ...), custom_call_target="tpu_custom_call", output_to_operand_aliasing={{5}: (4, {})} | custom-call | flops 1 | bytes 1 | tf_op jit(solution)/shard_map/pallas_call | solution.py:291
  38.8 2.3 %collective-permute-start.15 = (f32[1,128]{1,0:T(1,128)S(1)}, f32[1,128]{1,0:T(1,128)S(1)}, u32[]{:S(2)}, u32[]{:S(2)}) collective-permute-start(f32[1,128]{1,0:T(1,128)S(1)} %get-tuple-element.25), channel_id=1, source_target_pairs={{0,3},{1,2},{2,1},{3,0},{4,7},{5,6},{6,5},{7,4},{8,11},{9,10},{10,... | collective-permute-start | bytes 1544 | tf_op jit(solution)/shard_map/ppermute | solution.py:228
  41.1 0.0 collective-permute-start.16
  41.1 2.1 %collective-permute-start.17 = (f32[1,128]{1,0:T(1,128)S(1)}, f32[1,128]{1,0:T(1,128)S(1)}, u32[]{:S(2)}, u32[]{:S(2)}) collective-permute-start(f32[1,128]{1,0:T(1,128)S(1)} %get-tuple-element.27), channel_id=1, source_target_pairs={{0,2},{1,3},{2,0},{3,1},{4,6},{5,7},{6,4},{7,5},{8,10},{9,11},{10,... | collective-permute-start | bytes 1544 | tf_op jit(solution)/shard_map/ppermute | solution.py:228
  43.2 0.8 %shard_map.72 = bf16[256,1024]{1,0:T(8,128)(2,1)} custom-call(bf16[256,1024]{1,0:T(8,128)(2,1)S(1)} %get-tuple-element.23.rows_ref), custom_call_target="tpu_custom_call" | custom-call | flops 1 | bytes 1 | tf_op jit(solution)/shard_map/pallas_call | solution.py:303
  44.1 0.1 collective-permute-done.15
  44.2 0.5 collective-permute-done.16
  44.7 0.9 %collective-permute-done.17 = f32[1,128]{1,0:T(1,128)S(1)} collective-permute-done((f32[1,128]{1,0:T(1,128)S(1)}, f32[1,128]{1,0:T(1,128)S(1)}, u32[]{:S(2)}, u32[]{:S(2)}) %collective-permute-start.17) | collective-permute-done | bytes 544 | tf_op jit(solution)/shard_map/ppermute | solution.py:228
  45.6 0.1 collective-permute-start.18
  45.7 1.6 %collective-permute-start.19 = (f32[4,128]{1,0:T(4,128)S(1)}, f32[4,128]{1,0:T(4,128)S(1)}, u32[]{:S(2)}, u32[]{:S(2)}) collective-permute-start(f32[4,128]{1,0:T(4,128)S(1)} %pad_maximum_fusion), channel_id=1, source_target_pairs={{0,8},{1,9},{2,10},{3,11},{4,12},{5,13},{6,14},{7,15},{8,0},{9,1},... | collective-permute-start | bytes 6152 | tf_op jit(solution)/shard_map/ppermute | solution.py:228
  47.2 0.3 collective-permute-start.20
  47.5 0.1 slice_bitcast_fusion.11
  47.6 1.7 %collective-permute-done.19 = f32[4,128]{1,0:T(4,128)S(1)} collective-permute-done((f32[4,128]{1,0:T(4,128)S(1)}, f32[4,128]{1,0:T(4,128)S(1)}, u32[]{:S(2)}, u32[]{:S(2)}) %collective-permute-start.19) | collective-permute-done | bytes 2080 | tf_op jit(solution)/shard_map/ppermute | solution.py:228
  49.3 0.1 slice_bitcast_fusion.7
  49.4 0.8 %collective-permute-done.20 = f32[4,128]{1,0:T(4,128)S(1)} collective-permute-done((f32[4,128]{1,0:T(4,128)S(1)}, f32[4,128]{1,0:T(4,128)S(1)}, u32[]{:S(2)}, u32[]{:S(2)}) %collective-permute-start.20) | collective-permute-done | bytes 2080 | tf_op jit(solution)/shard_map/ppermute | solution.py:228
  50.3 0.1 slice_bitcast_fusion.3
  50.3 0.6 %add_bitcast_fusion = f32[32,8]{0,1:T(8,128)} fusion(s32[8,32]{1,0:T(8,128)S(1)} %bitcast.43, f32[32]{0:T(128)S(1)} %get-tuple-element.45, s32[]{:T(128)S(6)} %add.122, f32[32]{0:T(128)S(1)} %get-tuple-element.46, s32[]{:T(128)S(6)} %add.120, f32[32]{0:T(128)S(1)} %get-tuple-element.47, s32[]{:T(128)S(6)} %add.118, f32[32]{0:T(128)S(1)} %get-tuple-element.44, ...), kind=kLoop, calls=%fused_computation | loop fusion | flops 12032 | bytes 4160 | tf_op jit(solution)/shard_map/transpose | solution.py:321
  (7 shorter events, 0.0 us)
Async XLA Ops:
  1.6 11.8 %collective-permute-start = (bf16[32,3712]{1,0:T(8,128)(2,1)S(1)}, bf16[32,3712]{1,0:T(8,128)(2,1)S(1)}, u32[]{:S(2)}, u32[]{:S(2)}) collective-permute-start(bf16[32,3712]{1,0:T(8,128)(2,1)S(1)} %shard_map.68.refs_8_), channel_id=1, source_target_pairs={{0,3},{1,2},{2,1},{3,0},{4,7},{5,6},{6,5},{7,4},{8,11},{9,10},{10,... | collective-permute-start | bytes 712712 | tf_op jit(solution)/shard_map/ppermute | solution.py:228
  6.8 12.0 %collective-permute-start.4 = (bf16[32,3712]{1,0:T(8,128)(2,1)S(1)}, bf16[32,3712]{1,0:T(8,128)(2,1)S(1)}, u32[]{:S(2)}, u32[]{:S(2)}) collective-permute-start(bf16[32,3712]{1,0:T(8,128)(2,1)S(1)} %shard_map.68.refs_8_), channel_id=1, source_target_pairs={{0,1},{1,0},{2,3},{3,2},{4,5},{5,4},{6,7},{7,6},{8,9},{9,8},{10,11... | collective-permute-start | bytes 712712 | tf_op jit(solution)/shard_map/ppermute | solution.py:228
  6.8 20.2 %collective-permute-start.11 = (bf16[32,3712]{1,0:T(8,128)(2,1)S(1)}, bf16[32,3712]{1,0:T(8,128)(2,1)S(1)}, u32[]{:S(2)}, u32[]{:S(2)}) collective-permute-start(bf16[32,3712]{1,0:T(8,128)(2,1)S(1)} %shard_map.68.refs_8_), channel_id=1, source_target_pairs={{0,2},{1,3},{2,0},{3,1},{4,6},{5,7},{6,4},{7,5},{8,10},{9,11},{10,... | collective-permute-start | bytes 712712 | tf_op jit(solution)/shard_map/ppermute | solution.py:228
  7.4 21.1 %collective-permute-start.9 = (bf16[32,3712]{1,0:T(8,128)(2,1)S(1)}, bf16[32,3712]{1,0:T(8,128)(2,1)S(1)}, u32[]{:S(2)}, u32[]{:S(2)}) collective-permute-start(bf16[32,3712]{1,0:T(8,128)(2,1)S(1)} %shard_map.68.refs_8_), channel_id=1, source_target_pairs={{0,8},{1,9},{2,10},{3,11},{4,12},{5,13},{6,14},{7,15},{8,0},{9,1},... | collective-permute-start | bytes 712712 | tf_op jit(solution)/shard_map/ppermute | solution.py:228
  13.4 15.0 %collective-permute-start.2 = (bf16[32,3712]{1,0:T(8,128)(2,1)S(1)}, bf16[32,3712]{1,0:T(8,128)(2,1)S(1)}, u32[]{:S(2)}, u32[]{:S(2)}) collective-permute-start(bf16[32,3712]{1,0:T(8,128)(2,1)S(1)} %collective-permute-done.refs_0_), channel_id=1, source_target_pairs={{0,8},{1,9},{2,10},{3,11},{4,12},{5,13},{6,14},{7,15},{8,0},{9,1},... | collective-permute-start | bytes 712712 | tf_op jit(solution)/shard_map/ppermute | solution.py:228
  18.8 13.4 %collective-permute-start.6 = (bf16[32,3712]{1,0:T(8,128)(2,1)S(1)}, bf16[32,3712]{1,0:T(8,128)(2,1)S(1)}, u32[]{:S(2)}, u32[]{:S(2)}) collective-permute-start(bf16[32,3712]{1,0:T(8,128)(2,1)S(1)} %collective-permute-done.4.refs_4_), channel_id=1, source_target_pairs={{0,8},{1,9},{2,10},{3,11},{4,12},{5,13},{6,14},{7,15},{8,0},{9,1},... | collective-permute-start | bytes 712712 | tf_op jit(solution)/shard_map/ppermute | solution.py:228
  20.1 12.1 %collective-permute-start.8 = (bf16[32,3712]{1,0:T(8,128)(2,1)S(1)}, bf16[32,3712]{1,0:T(8,128)(2,1)S(1)}, u32[]{:S(2)}, u32[]{:S(2)}) collective-permute-start(bf16[32,3712]{1,0:T(8,128)(2,1)S(1)} %shard_map.68.refs_8_), channel_id=1, source_target_pairs={{0,4},{1,5},{2,6},{3,7},{4,0},{5,1},{6,2},{7,3},{8,12},{9,13},{10,... | collective-permute-start | bytes 712712 | tf_op jit(solution)/shard_map/ppermute | solution.py:228
  27.0 6.8 %collective-permute-start.13 = (bf16[32,3712]{1,0:T(8,128)(2,1)S(1)}, bf16[32,3712]{1,0:T(8,128)(2,1)S(1)}, u32[]{:S(2)}, u32[]{:S(2)}) collective-permute-start(bf16[32,3712]{1,0:T(8,128)(2,1)S(1)} %collective-permute-done.11.refs_5_), channel_id=1, source_target_pairs={{0,8},{1,9},{2,10},{3,11},{4,12},{5,13},{6,14},{7,15},{8,0},{9,1},... | collective-permute-start | bytes 712712 | tf_op jit(solution)/shard_map/ppermute | solution.py:228
  28.4 5.3 %collective-permute-start.1 = (bf16[32,3712]{1,0:T(8,128)(2,1)S(1)}, bf16[32,3712]{1,0:T(8,128)(2,1)S(1)}, u32[]{:S(2)}, u32[]{:S(2)}) collective-permute-start(bf16[32,3712]{1,0:T(8,128)(2,1)S(1)} %collective-permute-done.refs_0_), channel_id=1, source_target_pairs={{0,4},{1,5},{2,6},{3,7},{4,0},{5,1},{6,2},{7,3},{8,12},{9,13},{10,... | collective-permute-start | bytes 712712 | tf_op jit(solution)/shard_map/ppermute | solution.py:228
  28.5 5.8 %collective-permute-start.5 = (bf16[32,3712]{1,0:T(8,128)(2,1)S(1)}, bf16[32,3712]{1,0:T(8,128)(2,1)S(1)}, u32[]{:S(2)}, u32[]{:S(2)}) collective-permute-start(bf16[32,3712]{1,0:T(8,128)(2,1)S(1)} %collective-permute-done.4.refs_4_), channel_id=1, source_target_pairs={{0,4},{1,5},{2,6},{3,7},{4,0},{5,1},{6,2},{7,3},{8,12},{9,13},{10,... | collective-permute-start | bytes 712712 | tf_op jit(solution)/shard_map/ppermute | solution.py:228
  32.1 2.3 %collective-permute-start.10 = (bf16[32,3712]{1,0:T(8,128)(2,1)S(1)}, bf16[32,3712]{1,0:T(8,128)(2,1)S(1)}, u32[]{:S(2)}, u32[]{:S(2)}) collective-permute-start(bf16[32,3712]{1,0:T(8,128)(2,1)S(1)} %collective-permute-done.9.refs_10_), channel_id=1, source_target_pairs={{0,4},{1,5},{2,6},{3,7},{4,0},{5,1},{6,2},{7,3},{8,12},{9,13},{10,... | collective-permute-start | bytes 712712 | tf_op jit(solution)/shard_map/ppermute | solution.py:228
  32.3 2.1 %collective-permute-start.3 = (bf16[32,3712]{1,0:T(8,128)(2,1)S(1)}, bf16[32,3712]{1,0:T(8,128)(2,1)S(1)}, u32[]{:S(2)}, u32[]{:S(2)}) collective-permute-start(bf16[32,3712]{1,0:T(8,128)(2,1)S(1)} %collective-permute-done.2.refs_2_), channel_id=1, source_target_pairs={{0,4},{1,5},{2,6},{3,7},{4,0},{5,1},{6,2},{7,3},{8,12},{9,13},{10,... | collective-permute-start | bytes 712712 | tf_op jit(solution)/shard_map/ppermute | solution.py:228
  33.8 1.5 %collective-permute-start.7 = (bf16[32,3712]{1,0:T(8,128)(2,1)S(1)}, bf16[32,3712]{1,0:T(8,128)(2,1)S(1)}, u32[]{:S(2)}, u32[]{:S(2)}) collective-permute-start(bf16[32,3712]{1,0:T(8,128)(2,1)S(1)} %collective-permute-done.6.refs_6_), channel_id=1, source_target_pairs={{0,4},{1,5},{2,6},{3,7},{4,0},{5,1},{6,2},{7,3},{8,12},{9,13},{10,... | collective-permute-start | bytes 712712 | tf_op jit(solution)/shard_map/ppermute | solution.py:228
  33.8 2.5 %collective-permute-start.12 = (bf16[32,3712]{1,0:T(8,128)(2,1)S(1)}, bf16[32,3712]{1,0:T(8,128)(2,1)S(1)}, u32[]{:S(2)}, u32[]{:S(2)}) collective-permute-start(bf16[32,3712]{1,0:T(8,128)(2,1)S(1)} %collective-permute-done.11.refs_5_), channel_id=1, source_target_pairs={{0,4},{1,5},{2,6},{3,7},{4,0},{5,1},{6,2},{7,3},{8,12},{9,13},{10,... | collective-permute-start | bytes 712712 | tf_op jit(solution)/shard_map/ppermute | solution.py:228
  34.3 2.0 %collective-permute-start.14 = (bf16[32,3712]{1,0:T(8,128)(2,1)S(1)}, bf16[32,3712]{1,0:T(8,128)(2,1)S(1)}, u32[]{:S(2)}, u32[]{:S(2)}) collective-permute-start(bf16[32,3712]{1,0:T(8,128)(2,1)S(1)} %collective-permute-done.13.refs_7_), channel_id=1, source_target_pairs={{0,4},{1,5},{2,6},{3,7},{4,0},{5,1},{6,2},{7,3},{8,12},{9,13},{10,... | collective-permute-start | bytes 712712 | tf_op jit(solution)/shard_map/ppermute | solution.py:228
  34.4 16.0 %copy-start = (s32[32,8]{0,1:T(8,128)S(1)}, s32[32,8]{0,1:T(8,128)}, u32[]{:S(2)}) copy-start(s32[32,8]{0,1:T(8,128)} %param.6) | copy-start | bytes 3076
  38.8 5.4 %collective-permute-start.15 = (f32[1,128]{1,0:T(1,128)S(1)}, f32[1,128]{1,0:T(1,128)S(1)}, u32[]{:S(2)}, u32[]{:S(2)}) collective-permute-start(f32[1,128]{1,0:T(1,128)S(1)} %get-tuple-element.25), channel_id=1, source_target_pairs={{0,3},{1,2},{2,1},{3,0},{4,7},{5,6},{6,5},{7,4},{8,11},{9,10},{10,... | collective-permute-start | bytes 1544 | tf_op jit(solution)/shard_map/ppermute | solution.py:228
  41.1 3.5 %collective-permute-start.16 = (f32[1,128]{1,0:T(1,128)S(1)}, f32[1,128]{1,0:T(1,128)S(1)}, u32[]{:S(2)}, u32[]{:S(2)}) collective-permute-start(f32[1,128]{1,0:T(1,128)S(1)} %get-tuple-element.26), channel_id=1, source_target_pairs={{0,1},{1,0},{2,3},{3,2},{4,5},{5,4},{6,7},{7,6},{8,9},{9,8},{10,11... | collective-permute-start | bytes 1544 | tf_op jit(solution)/shard_map/ppermute | solution.py:228
  41.1 4.4 %collective-permute-start.17 = (f32[1,128]{1,0:T(1,128)S(1)}, f32[1,128]{1,0:T(1,128)S(1)}, u32[]{:S(2)}, u32[]{:S(2)}) collective-permute-start(f32[1,128]{1,0:T(1,128)S(1)} %get-tuple-element.27), channel_id=1, source_target_pairs={{0,2},{1,3},{2,0},{3,1},{4,6},{5,7},{6,4},{7,5},{8,10},{9,11},{10,... | collective-permute-start | bytes 1544 | tf_op jit(solution)/shard_map/ppermute | solution.py:228
  45.6 2.0 %collective-permute-start.18 = (f32[4,128]{1,0:T(4,128)S(1)}, f32[4,128]{1,0:T(4,128)S(1)}, u32[]{:S(2)}, u32[]{:S(2)}) collective-permute-start(f32[4,128]{1,0:T(4,128)S(1)} %pad_maximum_fusion), channel_id=1, source_target_pairs={{0,4},{1,5},{2,6},{3,7},{4,0},{5,1},{6,2},{7,3},{8,12},{9,13},{10,... | collective-permute-start | bytes 6152 | tf_op jit(solution)/shard_map/ppermute | solution.py:228
  45.7 3.7 %collective-permute-start.19 = (f32[4,128]{1,0:T(4,128)S(1)}, f32[4,128]{1,0:T(4,128)S(1)}, u32[]{:S(2)}, u32[]{:S(2)}) collective-permute-start(f32[4,128]{1,0:T(4,128)S(1)} %pad_maximum_fusion), channel_id=1, source_target_pairs={{0,8},{1,9},{2,10},{3,11},{4,12},{5,13},{6,14},{7,15},{8,0},{9,1},... | collective-permute-start | bytes 6152 | tf_op jit(solution)/shard_map/ppermute | solution.py:228
  47.2 3.0 %collective-permute-start.20 = (f32[4,128]{1,0:T(4,128)S(1)}, f32[4,128]{1,0:T(4,128)S(1)}, u32[]{:S(2)}, u32[]{:S(2)}) collective-permute-start(f32[4,128]{1,0:T(4,128)S(1)} %pad_maximum_fusion), channel_id=1, source_target_pairs={{0,12},{1,13},{2,14},{3,15},{4,8},{5,9},{6,10},{7,11},{8,4},{9,5},... | collective-permute-start | bytes 6152 | tf_op jit(solution)/shard_map/ppermute | solution.py:228

commit v6 on v5

--- a/solution.py
+++ b/solution.py
@@ -84,7 +84,7 @@
 LANES = 128
 LINE = 4
 WORK_BYTES = 16 * 1024 * 1024
-CHUNK = 256
+CHUNK = 512
 
 
 def pack_kernel(rows_hbm, routes_hbm, combine_hbm, block_ref, routes_ref, combine_ref, sems):
@@ -270,7 +270,7 @@
     far = {j: move(block, 0, j) for j in (2, 3, 1)}
     blocks = []
     for j in early:
-        blocks += over_nodes(far[j] if j else block, *([cache] if j == early[0] else []))
+        blocks += over_nodes(far[j] if j else block, cache)
     rows = len(blocks) * capacity
     picked, chosen, scales = pl.pallas_call(
         functools.partial(pick_kernel, groups[:-1]),
@@ -312,6 +312,7 @@
     back = [move(terms[j], 0, j) if j else terms[j] for j in (0, *order)]
     back = jnp.concatenate(back, axis=0)
     back, routes_t, node, local = lax.optimization_barrier((back, routes_t, node, local))
+    back = after(back, d_hidden)
     d_combine_t = jnp.zeros(routes_t.shape, jnp.float32)
     for i in range(nodes):
         returned = (move(back, i, 0) if i else back)[:, i * tokens : (i + 1) * tokens]

time: 51.1 us -> 51.1 us (level)
  no operation moved by 1% of the time
where the time goes in v6:
time: 51.1 us; the launch traced here: 51 us
  waiting for transfers between devices  21 us (41%)
  starting transfers between devices  20 us (39%)
  Pallas kernels  8.43 us (16%)
  between operations  0.76 us (1%)
  other arithmetic  0.63 us (1%)
    ppermute x21, waiting for transfers between devices, move(): return lax.ppermute(x, ('node', 'local'), pairs)  21 us
    ppermute x21, starting transfers between devices, move(): return lax.ppermute(x, ('node', 'local'), pairs)  20 us
    pallas_call x1, Pallas kernels, exchanged(): pl.pallas_call(load_kernel, out_shape=[pltpu.VMEM((hidden, width), down_w...  3.15 us
    pallas_call x1, Pallas kernels, exchanged(): pl.pallas_call(functools.partial(expert_kernel, groups), out_shape=[jax.S...  2.5 us
  transfers between devices with their start and end apart: 21, of which 10 were waited for; matrix products, arithmetic and copies ran while one was open for 0% of the time, Pallas kernels for 10%

profile of v6, /device:TPU:0, one launch (start us, length us, event | category | flops | bytes accessed | tf_op | source)
XLA Modules:
  0.0 51.0 jit_solution(15029724912534027326)
XLA Ops:
  0.6 1.0 %shard_map.68.refs_8_ = bf16[32,3712]{1,0:T(8,128)(2,1)S(1)} custom-call(bf16[32,3584]{1,0:T(8,128)(2,1)} %rows_hbm.1, s32[8,32]{1,0:T(8,128)} %bitcast.42, bf16[8,32]{1,0:T(8,128)(2,1)} %bitcast.44), custom_call_target="tpu_custom_call" | custom-call | tf_op jit(solution)/shard_map/pallas_call | solution.py:242
  1.6 5.1 %collective-permute-start = (bf16[32,3712]{1,0:T(8,128)(2,1)S(1)}, bf16[32,3712]{1,0:T(8,128)(2,1)S(1)}, u32[]{:S(2)}, u32[]{:S(2)}) collective-permute-start(bf16[32,3712]{1,0:T(8,128)(2,1)S(1)} %shard_map.68.refs_8_), channel_id=1, source_target_pairs={{0,3},{1,2},{2,1},{3,0},{4,7},{5,6},{6,5},{7,4},{8,11},{9,10},{10,... | collective-permute-start | bytes 712712 | tf_op jit(solution)/shard_map/ppermute | solution.py:228
  6.8 0.0 collective-permute-start.4
  6.8 0.6 %collective-permute-start.11 = (bf16[32,3712]{1,0:T(8,128)(2,1)S(1)}, bf16[32,3712]{1,0:T(8,128)(2,1)S(1)}, u32[]{:S(2)}, u32[]{:S(2)}) collective-permute-start(bf16[32,3712]{1,0:T(8,128)(2,1)S(1)} %shard_map.68.refs_8_), channel_id=1, source_target_pairs={{0,2},{1,3},{2,0},{3,1},{4,6},{5,7},{6,4},{7,5},{8,10},{9,11},{10,... | collective-permute-start | bytes 712712 | tf_op jit(solution)/shard_map/ppermute | solution.py:228
  7.4 1.6 %collective-permute-start.9 = (bf16[32,3712]{1,0:T(8,128)(2,1)S(1)}, bf16[32,3712]{1,0:T(8,128)(2,1)S(1)}, u32[]{:S(2)}, u32[]{:S(2)}) collective-permute-start(bf16[32,3712]{1,0:T(8,128)(2,1)S(1)} %shard_map.68.refs_8_), channel_id=1, source_target_pairs={{0,8},{1,9},{2,10},{3,11},{4,12},{5,13},{6,14},{7,15},{8,0},{9,1},... | collective-permute-start | bytes 712712 | tf_op jit(solution)/shard_map/ppermute | solution.py:228
  9.0 4.4 %collective-permute-done.refs_0_ = bf16[32,3712]{1,0:T(8,128)(2,1)S(1)} collective-permute-done((bf16[32,3712]{1,0:T(8,128)(2,1)S(1)}, bf16[32,3712]{1,0:T(8,128)(2,1)S(1)}, u32[]{:S(2)}, u32[]{:S(2)}) %collective-permute-start) | collective-permute-done | bytes 237600 | tf_op jit(solution)/shard_map/ppermute | solution.py:228
  13.4 1.7 %collective-permute-start.2 = (bf16[32,3712]{1,0:T(8,128)(2,1)S(1)}, bf16[32,3712]{1,0:T(8,128)(2,1)S(1)}, u32[]{:S(2)}, u32[]{:S(2)}) collective-permute-start(bf16[32,3712]{1,0:T(8,128)(2,1)S(1)} %collective-permute-done.refs_0_), channel_id=1, source_target_pairs={{0,8},{1,9},{2,10},{3,11},{4,12},{5,13},{6,14},{7,15},{8,0},{9,1},... | collective-permute-start | bytes 712712 | tf_op jit(solution)/shard_map/ppermute | solution.py:228
  15.1 3.6 %collective-permute-done.4.refs_4_ = bf16[32,3712]{1,0:T(8,128)(2,1)S(1)} collective-permute-done((bf16[32,3712]{1,0:T(8,128)(2,1)S(1)}, bf16[32,3712]{1,0:T(8,128)(2,1)S(1)}, u32[]{:S(2)}, u32[]{:S(2)}) %collective-permute-start.4) | collective-permute-done | bytes 237600 | tf_op jit(solution)/shard_map/ppermute | solution.py:228
  18.8 1.4 %collective-permute-start.6 = (bf16[32,3712]{1,0:T(8,128)(2,1)S(1)}, bf16[32,3712]{1,0:T(8,128)(2,1)S(1)}, u32[]{:S(2)}, u32[]{:S(2)}) collective-permute-start(bf16[32,3712]{1,0:T(8,128)(2,1)S(1)} %collective-permute-done.4.refs_4_), channel_id=1, source_target_pairs={{0,8},{1,9},{2,10},{3,11},{4,12},{5,13},{6,14},{7,15},{8,0},{9,1},... | collective-permute-start | bytes 712712 | tf_op jit(solution)/shard_map/ppermute | solution.py:228
  20.1 0.0 collective-permute-start.8
  20.1 6.8 %collective-permute-done.11.refs_5_ = bf16[32,3712]{1,0:T(8,128)(2,1)S(1)} collective-permute-done((bf16[32,3712]{1,0:T(8,128)(2,1)S(1)}, bf16[32,3712]{1,0:T(8,128)(2,1)S(1)}, u32[]{:S(2)}, u32[]{:S(2)}) %collective-permute-start.11) | collective-permute-done | bytes 237600 | tf_op jit(solution)/shard_map/ppermute | solution.py:228
  27.0 1.5 %collective-permute-start.13 = (bf16[32,3712]{1,0:T(8,128)(2,1)S(1)}, bf16[32,3712]{1,0:T(8,128)(2,1)S(1)}, u32[]{:S(2)}, u32[]{:S(2)}) collective-permute-start(bf16[32,3712]{1,0:T(8,128)(2,1)S(1)} %collective-permute-done.11.refs_5_), channel_id=1, source_target_pairs={{0,8},{1,9},{2,10},{3,11},{4,12},{5,13},{6,14},{7,15},{8,0},{9,1},... | collective-permute-start | bytes 712712 | tf_op jit(solution)/shard_map/ppermute | solution.py:228
  28.4 3.1 %shard_map.69 = (bf16[1024,3584]{1,0:T(8,128)(2,1)S(1)}, bf16[256,1024]{1,0:T(8,128)(2,1)S(1)}) custom-call(bf16[1024,3584]{1,0:T(8,128)(2,1)} %bitcast.39, bf16[256,1024]{1,0:T(8,128)(2,1)} %bitcast.41), custom_call_target="tpu_custom_call" | custom-call | flops 1 | bytes 1 | tf_op jit(solution)/shard_map/pallas_call | solution.py:254
  31.6 0.0 collective-permute-done.9.refs_10_
  31.6 0.1 collective-permute-start.10
  31.7 0.0 collective-permute-done.2.refs_2_
  31.7 0.5 collective-permute-start.1
  32.2 0.0 collective-permute-done.6.refs_6_
  32.2 0.1 collective-permute-start.5
  32.3 0.0 collective-permute-done.8.refs_9_
  32.3 0.4 collective-permute-start.3
  32.7 1.1 %collective-permute-done.13.refs_7_ = bf16[32,3712]{1,0:T(8,128)(2,1)S(1)} collective-permute-done((bf16[32,3712]{1,0:T(8,128)(2,1)S(1)}, bf16[32,3712]{1,0:T(8,128)(2,1)S(1)}, u32[]{:S(2)}, u32[]{:S(2)}) %collective-permute-start.13) | collective-permute-done | bytes 237600 | tf_op jit(solution)/shard_map/ppermute | solution.py:228
  33.8 0.0 collective-permute-start.7
  33.8 0.0 collective-permute-done.10.refs_11_
  33.8 0.5 collective-permute-start.12
  34.3 0.0 collective-permute-done.1.refs_1_
  34.3 0.1 collective-permute-start.14
  34.4 0.0 collective-permute-done.5.refs_5_
  34.4 0.9 %collective-permute-done.7.refs_7_ = bf16[32,3712]{1,0:T(8,128)(2,1)S(1)} collective-permute-done((bf16[32,3712]{1,0:T(8,128)(2,1)S(1)}, bf16[32,3712]{1,0:T(8,128)(2,1)S(1)}, u32[]{:S(2)}, u32[]{:S(2)}) %collective-permute-start.7) | collective-permute-done | bytes 237600 | tf_op jit(solution)/shard_map/ppermute | solution.py:228
  35.3 1.0 %shard_map.70 = (bf16[256,3584]{1,0:T(8,128)(2,1)S(1)}, f32[192,128]{1,0:T(8,128)S(1)}, f32[192,128]{1,0:T(8,128)S(1)}) custom-call(bf16[32,3712]{1,0:T(8,128)(2,1)S(1)} %collective-permute-done.refs_0_, bf16[32,3712]{1,0:T(8,128)(2,1)S(1)} %collective-permute-done.1.refs_1_, bf16[32,3712]{1,0:T(8,128)(2,1)S(1)} %collective-permute-done.2.refs_2_, ...), custom_call_target="tpu_custom_call" | custom-call | flops 176160768 | bytes 4194304 | tf_op jit(solution)/shard_map/pallas_call | solution.py:275
  36.3 0.0 collective-permute-done.14.refs_8_
  36.3 2.5 %shard_map.71 = (bf16[256,1024]{1,0:T(8,128)(2,1)S(1)}, f32[1,128]{1,0:T(1,128)S(1)}, f32[1,128]{1,0:T(1,128)S(1)}, f32[1,128]{1,0:T(1,128)S(1)}, f32[1,128]{1,0:T(1,128)S(1)}, /*index=5*/bf16[256,3584]{1,0:T(8,128)(2,1)S(1)}) custom-call(f32[192,128]{1,0:T(8,128)S(1)} %get-tuple-element.24.refs_0_, ...), custom_call_target="tpu_custom_call", output_to_operand_aliasing={{5}: (4, {})} | custom-call | flops 1 | bytes 1 | tf_op jit(solution)/shard_map/pallas_call | solution.py:291
  38.8 2.3 %collective-permute-start.15 = (f32[1,128]{1,0:T(1,128)S(1)}, f32[1,128]{1,0:T(1,128)S(1)}, u32[]{:S(2)}, u32[]{:S(2)}) collective-permute-start(f32[1,128]{1,0:T(1,128)S(1)} %get-tuple-element.30), channel_id=1, source_target_pairs={{0,3},{1,2},{2,1},{3,0},{4,7},{5,6},{6,5},{7,4},{8,11},{9,10},{10,... | collective-permute-start | bytes 1544 | tf_op jit(solution)/shard_map/ppermute | solution.py:228
  41.1 2.1 %collective-permute-start.17 = (f32[1,128]{1,0:T(1,128)S(1)}, f32[1,128]{1,0:T(1,128)S(1)}, u32[]{:S(2)}, u32[]{:S(2)}) collective-permute-start(f32[1,128]{1,0:T(1,128)S(1)} %get-tuple-element.32), channel_id=1, source_target_pairs={{0,2},{1,3},{2,0},{3,1},{4,6},{5,7},{6,4},{7,5},{8,10},{9,11},{10,... | collective-permute-start | bytes 1544 | tf_op jit(solution)/shard_map/ppermute | solution.py:228
  43.2 0.8 %shard_map.72 = bf16[256,1024]{1,0:T(8,128)(2,1)} custom-call(bf16[256,1024]{1,0:T(8,128)(2,1)S(1)} %get-tuple-element.28.rows_ref), custom_call_target="tpu_custom_call" | custom-call | flops 1 | bytes 1 | tf_op jit(solution)/shard_map/pallas_call | solution.py:303
  44.1 0.1 collective-permute-done.15
  44.2 0.5 collective-permute-done.16
  44.7 0.9 %collective-permute-done.17 = f32[1,128]{1,0:T(1,128)S(1)} collective-permute-done((f32[1,128]{1,0:T(1,128)S(1)}, f32[1,128]{1,0:T(1,128)S(1)}, u32[]{:S(2)}, u32[]{:S(2)}) %collective-permute-start.17) | collective-permute-done | bytes 544 | tf_op jit(solution)/shard_map/ppermute | solution.py:228
  45.6 0.1 collective-permute-start.18
  45.7 1.6 %collective-permute-start.19 = (f32[4,128]{1,0:T(4,128)S(1)}, f32[4,128]{1,0:T(4,128)S(1)}, u32[]{:S(2)}, u32[]{:S(2)}) collective-permute-start(f32[4,128]{1,0:T(4,128)S(1)} %pad_maximum_fusion), channel_id=1, source_target_pairs={{0,8},{1,9},{2,10},{3,11},{4,12},{5,13},{6,14},{7,15},{8,0},{9,1},... | collective-permute-start | bytes 6152 | tf_op jit(solution)/shard_map/ppermute | solution.py:228
  47.2 0.3 collective-permute-start.20
  47.5 0.0 collective-permute-done.18
  47.5 0.1 slice_bitcast_fusion.11
  47.6 1.7 %collective-permute-done.19 = f32[4,128]{1,0:T(4,128)S(1)} collective-permute-done((f32[4,128]{1,0:T(4,128)S(1)}, f32[4,128]{1,0:T(4,128)S(1)}, u32[]{:S(2)}, u32[]{:S(2)}) %collective-permute-start.19) | collective-permute-done | bytes 2080 | tf_op jit(solution)/shard_map/ppermute | solution.py:228
  49.3 0.1 slice_bitcast_fusion.7
  49.4 0.8 %collective-permute-done.20 = f32[4,128]{1,0:T(4,128)S(1)} collective-permute-done((f32[4,128]{1,0:T(4,128)S(1)}, f32[4,128]{1,0:T(4,128)S(1)}, u32[]{:S(2)}, u32[]{:S(2)}) %collective-permute-start.20) | collective-permute-done | bytes 2080 | tf_op jit(solution)/shard_map/ppermute | solution.py:228
  50.3 0.1 slice_bitcast_fusion.3
  50.3 0.6 %add_bitcast_fusion = f32[32,8]{0,1:T(8,128)} fusion(s32[8,32]{1,0:T(8,128)S(1)} %bitcast.43, f32[32]{0:T(128)S(1)} %get-tuple-element.51, s32[]{:T(128)S(6)} %add.122, f32[32]{0:T(128)S(1)} %get-tuple-element.52, s32[]{:T(128)S(6)} %add.120, f32[32]{0:T(128)S(1)} %get-tuple-element.53, s32[]{:T(128)S(6)} %add.118, f32[32]{0:T(128)S(1)} %get-tuple-element.50, ...), kind=kLoop, calls=%fused_computation | loop fusion | flops 12032 | bytes 4160 | tf_op jit(solution)/shard_map/transpose | solution.py:322
  (7 shorter events, 0.0 us)
Async XLA Ops:
  1.6 11.8 %collective-permute-start = (bf16[32,3712]{1,0:T(8,128)(2,1)S(1)}, bf16[32,3712]{1,0:T(8,128)(2,1)S(1)}, u32[]{:S(2)}, u32[]{:S(2)}) collective-permute-start(bf16[32,3712]{1,0:T(8,128)(2,1)S(1)} %shard_map.68.refs_8_), channel_id=1, source_target_pairs={{0,3},{1,2},{2,1},{3,0},{4,7},{5,6},{6,5},{7,4},{8,11},{9,10},{10,... | collective-permute-start | bytes 712712 | tf_op jit(solution)/shard_map/ppermute | solution.py:228
  6.8 12.0 %collective-permute-start.4 = (bf16[32,3712]{1,0:T(8,128)(2,1)S(1)}, bf16[32,3712]{1,0:T(8,128)(2,1)S(1)}, u32[]{:S(2)}, u32[]{:S(2)}) collective-permute-start(bf16[32,3712]{1,0:T(8,128)(2,1)S(1)} %shard_map.68.refs_8_), channel_id=1, source_target_pairs={{0,1},{1,0},{2,3},{3,2},{4,5},{5,4},{6,7},{7,6},{8,9},{9,8},{10,11... | collective-permute-start | bytes 712712 | tf_op jit(solution)/shard_map/ppermute | solution.py:228
  6.8 20.2 %collective-permute-start.11 = (bf16[32,3712]{1,0:T(8,128)(2,1)S(1)}, bf16[32,3712]{1,0:T(8,128)(2,1)S(1)}, u32[]{:S(2)}, u32[]{:S(2)}) collective-permute-start(bf16[32,3712]{1,0:T(8,128)(2,1)S(1)} %shard_map.68.refs_8_), channel_id=1, source_target_pairs={{0,2},{1,3},{2,0},{3,1},{4,6},{5,7},{6,4},{7,5},{8,10},{9,11},{10,... | collective-permute-start | bytes 712712 | tf_op jit(solution)/shard_map/ppermute | solution.py:228
  7.4 24.2 %collective-permute-start.9 = (bf16[32,3712]{1,0:T(8,128)(2,1)S(1)}, bf16[32,3712]{1,0:T(8,128)(2,1)S(1)}, u32[]{:S(2)}, u32[]{:S(2)}) collective-permute-start(bf16[32,3712]{1,0:T(8,128)(2,1)S(1)} %shard_map.68.refs_8_), channel_id=1, source_target_pairs={{0,8},{1,9},{2,10},{3,11},{4,12},{5,13},{6,14},{7,15},{8,0},{9,1},... | collective-permute-start | bytes 712712 | tf_op jit(solution)/shard_map/ppermute | solution.py:228
  13.4 18.2 %collective-permute-start.2 = (bf16[32,3712]{1,0:T(8,128)(2,1)S(1)}, bf16[32,3712]{1,0:T(8,128)(2,1)S(1)}, u32[]{:S(2)}, u32[]{:S(2)}) collective-permute-start(bf16[32,3712]{1,0:T(8,128)(2,1)S(1)} %collective-permute-done.refs_0_), channel_id=1, source_target_pairs={{0,8},{1,9},{2,10},{3,11},{4,12},{5,13},{6,14},{7,15},{8,0},{9,1},... | collective-permute-start | bytes 712712 | tf_op jit(solution)/shard_map/ppermute | solution.py:228
  18.8 13.4 %collective-permute-start.6 = (bf16[32,3712]{1,0:T(8,128)(2,1)S(1)}, bf16[32,3712]{1,0:T(8,128)(2,1)S(1)}, u32[]{:S(2)}, u32[]{:S(2)}) collective-permute-start(bf16[32,3712]{1,0:T(8,128)(2,1)S(1)} %collective-permute-done.4.refs_4_), channel_id=1, source_target_pairs={{0,8},{1,9},{2,10},{3,11},{4,12},{5,13},{6,14},{7,15},{8,0},{9,1},... | collective-permute-start | bytes 712712 | tf_op jit(solution)/shard_map/ppermute | solution.py:228
  20.1 12.1 %collective-permute-start.8 = (bf16[32,3712]{1,0:T(8,128)(2,1)S(1)}, bf16[32,3712]{1,0:T(8,128)(2,1)S(1)}, u32[]{:S(2)}, u32[]{:S(2)}) collective-permute-start(bf16[32,3712]{1,0:T(8,128)(2,1)S(1)} %shard_map.68.refs_8_), channel_id=1, source_target_pairs={{0,4},{1,5},{2,6},{3,7},{4,0},{5,1},{6,2},{7,3},{8,12},{9,13},{10,... | collective-permute-start | bytes 712712 | tf_op jit(solution)/shard_map/ppermute | solution.py:228
  27.0 6.8 %collective-permute-start.13 = (bf16[32,3712]{1,0:T(8,128)(2,1)S(1)}, bf16[32,3712]{1,0:T(8,128)(2,1)S(1)}, u32[]{:S(2)}, u32[]{:S(2)}) collective-permute-start(bf16[32,3712]{1,0:T(8,128)(2,1)S(1)} %collective-permute-done.11.refs_5_), channel_id=1, source_target_pairs={{0,8},{1,9},{2,10},{3,11},{4,12},{5,13},{6,14},{7,15},{8,0},{9,1},... | collective-permute-start | bytes 712712 | tf_op jit(solution)/shard_map/ppermute | solution.py:228
  31.6 2.2 %collective-permute-start.10 = (bf16[32,3712]{1,0:T(8,128)(2,1)S(1)}, bf16[32,3712]{1,0:T(8,128)(2,1)S(1)}, u32[]{:S(2)}, u32[]{:S(2)}) collective-permute-start(bf16[32,3712]{1,0:T(8,128)(2,1)S(1)} %collective-permute-done.9.refs_10_), channel_id=1, source_target_pairs={{0,4},{1,5},{2,6},{3,7},{4,0},{5,1},{6,2},{7,3},{8,12},{9,13},{10,... | collective-permute-start | bytes 712712 | tf_op jit(solution)/shard_map/ppermute | solution.py:228
  31.7 2.6 %collective-permute-start.1 = (bf16[32,3712]{1,0:T(8,128)(2,1)S(1)}, bf16[32,3712]{1,0:T(8,128)(2,1)S(1)}, u32[]{:S(2)}, u32[]{:S(2)}) collective-permute-start(bf16[32,3712]{1,0:T(8,128)(2,1)S(1)} %collective-permute-done.refs_0_), channel_id=1, source_target_pairs={{0,4},{1,5},{2,6},{3,7},{4,0},{5,1},{6,2},{7,3},{8,12},{9,13},{10,... | collective-permute-start | bytes 712712 | tf_op jit(solution)/shard_map/ppermute | solution.py:228
  32.2 2.2 %collective-permute-start.5 = (bf16[32,3712]{1,0:T(8,128)(2,1)S(1)}, bf16[32,3712]{1,0:T(8,128)(2,1)S(1)}, u32[]{:S(2)}, u32[]{:S(2)}) collective-permute-start(bf16[32,3712]{1,0:T(8,128)(2,1)S(1)} %collective-permute-done.4.refs_4_), channel_id=1, source_target_pairs={{0,4},{1,5},{2,6},{3,7},{4,0},{5,1},{6,2},{7,3},{8,12},{9,13},{10,... | collective-permute-start | bytes 712712 | tf_op jit(solution)/shard_map/ppermute | solution.py:228
  32.3 2.1 %collective-permute-start.3 = (bf16[32,3712]{1,0:T(8,128)(2,1)S(1)}, bf16[32,3712]{1,0:T(8,128)(2,1)S(1)}, u32[]{:S(2)}, u32[]{:S(2)}) collective-permute-start(bf16[32,3712]{1,0:T(8,128)(2,1)S(1)} %collective-permute-done.2.refs_2_), channel_id=1, source_target_pairs={{0,4},{1,5},{2,6},{3,7},{4,0},{5,1},{6,2},{7,3},{8,12},{9,13},{10,... | collective-permute-start | bytes 712712 | tf_op jit(solution)/shard_map/ppermute | solution.py:228
  33.8 1.5 %collective-permute-start.7 = (bf16[32,3712]{1,0:T(8,128)(2,1)S(1)}, bf16[32,3712]{1,0:T(8,128)(2,1)S(1)}, u32[]{:S(2)}, u32[]{:S(2)}) collective-permute-start(bf16[32,3712]{1,0:T(8,128)(2,1)S(1)} %collective-permute-done.6.refs_6_), channel_id=1, source_target_pairs={{0,4},{1,5},{2,6},{3,7},{4,0},{5,1},{6,2},{7,3},{8,12},{9,13},{10,... | collective-permute-start | bytes 712712 | tf_op jit(solution)/shard_map/ppermute | solution.py:228
  33.8 2.5 %collective-permute-start.12 = (bf16[32,3712]{1,0:T(8,128)(2,1)S(1)}, bf16[32,3712]{1,0:T(8,128)(2,1)S(1)}, u32[]{:S(2)}, u32[]{:S(2)}) collective-permute-start(bf16[32,3712]{1,0:T(8,128)(2,1)S(1)} %collective-permute-done.11.refs_5_), channel_id=1, source_target_pairs={{0,4},{1,5},{2,6},{3,7},{4,0},{5,1},{6,2},{7,3},{8,12},{9,13},{10,... | collective-permute-start | bytes 712712 | tf_op jit(solution)/shard_map/ppermute | solution.py:228
  34.3 2.0 %collective-permute-start.14 = (bf16[32,3712]{1,0:T(8,128)(2,1)S(1)}, bf16[32,3712]{1,0:T(8,128)(2,1)S(1)}, u32[]{:S(2)}, u32[]{:S(2)}) collective-permute-start(bf16[32,3712]{1,0:T(8,128)(2,1)S(1)} %collective-permute-done.13.refs_7_), channel_id=1, source_target_pairs={{0,4},{1,5},{2,6},{3,7},{4,0},{5,1},{6,2},{7,3},{8,12},{9,13},{10,... | collective-permute-start | bytes 712712 | tf_op jit(solution)/shard_map/ppermute | solution.py:228
  34.4 16.0 %copy-start = (s32[32,8]{0,1:T(8,128)S(1)}, s32[32,8]{0,1:T(8,128)}, u32[]{:S(2)}) copy-start(s32[32,8]{0,1:T(8,128)} %param.6) | copy-start | bytes 3076
  38.8 5.4 %collective-permute-start.15 = (f32[1,128]{1,0:T(1,128)S(1)}, f32[1,128]{1,0:T(1,128)S(1)}, u32[]{:S(2)}, u32[]{:S(2)}) collective-permute-start(f32[1,128]{1,0:T(1,128)S(1)} %get-tuple-element.30), channel_id=1, source_target_pairs={{0,3},{1,2},{2,1},{3,0},{4,7},{5,6},{6,5},{7,4},{8,11},{9,10},{10,... | collective-permute-start | bytes 1544 | tf_op jit(solution)/shard_map/ppermute | solution.py:228
  41.1 3.5 %collective-permute-start.16 = (f32[1,128]{1,0:T(1,128)S(1)}, f32[1,128]{1,0:T(1,128)S(1)}, u32[]{:S(2)}, u32[]{:S(2)}) collective-permute-start(f32[1,128]{1,0:T(1,128)S(1)} %get-tuple-element.31), channel_id=1, source_target_pairs={{0,1},{1,0},{2,3},{3,2},{4,5},{5,4},{6,7},{7,6},{8,9},{9,8},{10,11... | collective-permute-start | bytes 1544 | tf_op jit(solution)/shard_map/ppermute | solution.py:228
  41.1 4.4 %collective-permute-start.17 = (f32[1,128]{1,0:T(1,128)S(1)}, f32[1,128]{1,0:T(1,128)S(1)}, u32[]{:S(2)}, u32[]{:S(2)}) collective-permute-start(f32[1,128]{1,0:T(1,128)S(1)} %get-tuple-element.32), channel_id=1, source_target_pairs={{0,2},{1,3},{2,0},{3,1},{4,6},{5,7},{6,4},{7,5},{8,10},{9,11},{10,... | collective-permute-start | bytes 1544 | tf_op jit(solution)/shard_map/ppermute | solution.py:228
  45.6 2.0 %collective-permute-start.18 = (f32[4,128]{1,0:T(4,128)S(1)}, f32[4,128]{1,0:T(4,128)S(1)}, u32[]{:S(2)}, u32[]{:S(2)}) collective-permute-start(f32[4,128]{1,0:T(4,128)S(1)} %pad_maximum_fusion), channel_id=1, source_target_pairs={{0,4},{1,5},{2,6},{3,7},{4,0},{5,1},{6,2},{7,3},{8,12},{9,13},{10,... | collective-permute-start | bytes 6152 | tf_op jit(solution)/shard_map/ppermute | solution.py:228
  45.7 3.7 %collective-permute-start.19 = (f32[4,128]{1,0:T(4,128)S(1)}, f32[4,128]{1,0:T(4,128)S(1)}, u32[]{:S(2)}, u32[]{:S(2)}) collective-permute-start(f32[4,128]{1,0:T(4,128)S(1)} %pad_maximum_fusion), channel_id=1, source_target_pairs={{0,8},{1,9},{2,10},{3,11},{4,12},{5,13},{6,14},{7,15},{8,0},{9,1},... | collective-permute-start | bytes 6152 | tf_op jit(solution)/shard_map/ppermute | solution.py:228
  47.2 3.0 %collective-permute-start.20 = (f32[4,128]{1,0:T(4,128)S(1)}, f32[4,128]{1,0:T(4,128)S(1)}, u32[]{:S(2)}, u32[]{:S(2)}) collective-permute-start(f32[4,128]{1,0:T(4,128)S(1)} %pad_maximum_fusion), channel_id=1, source_target_pairs={{0,12},{1,13},{2,14},{3,15},{4,8},{5,9},{6,10},{7,11},{8,4},{9,5},... | collective-permute-start | bytes 6152 | tf_op jit(solution)/shard_map/ppermute | solution.py:228

commit v7 on v6

--- a/solution.py
+++ b/solution.py
@@ -83,6 +83,7 @@
 
 LANES = 128
 LINE = 4
+PARTS = 4
 WORK_BYTES = 16 * 1024 * 1024
 CHUNK = 512
 
@@ -91,8 +92,12 @@
     copies = [
         pltpu.make_async_copy(routes_hbm, routes_ref, sems.at[0]),
         pltpu.make_async_copy(combine_hbm, combine_ref, sems.at[1]),
-        pltpu.make_async_copy(rows_hbm, block_ref.at[:, LANES:], sems.at[2]),
     ]
+    quarter = rows_hbm.shape[1] // PARTS
+    for p in range(PARTS):
+        part = rows_hbm.at[:, p * quarter : (p + 1) * quarter]
+        place = block_ref.at[:, LANES + p * quarter : LANES + (p + 1) * quarter]
+        copies.append(pltpu.make_async_copy(part, place, sems.at[2 + p]))
     for copy in copies:
         copy.start()
     for copy in copies[:2]:
@@ -104,7 +109,8 @@
     table = jnp.concatenate([table] * (LANES // tokens), axis=1)
     fill = jnp.zeros((block_ref.shape[0] - 2 * top, LANES), jnp.float32)
     block_ref[:, :LANES] = jnp.concatenate([table, fill], axis=0).astype(block_ref.dtype)
-    copies[2].wait()
+    for copy in copies[2:]:
+        copy.wait()
 
 
 def load_kernel(weight_hbm, cache_hbm, weight_ref, cache_ref, sems):
@@ -247,7 +253,7 @@
         scratch_shapes=[
             pltpu.VMEM(routes_t.shape, routes.dtype),
             pltpu.VMEM(routes_t.shape, combine.dtype),
-            pltpu.SemaphoreType.DMA((3,)),
+            pltpu.SemaphoreType.DMA((2 + PARTS,)),
         ],
         compiler_params=params,
     )(pinned(grad_out), pinned(routes_t), pinned(combine.T))

time: 51.1 us -> 51.1 us (level)
  no operation moved by 1% of the time
where the time goes in v7:
time: 51.1 us; the launch traced here: 50.9 us
  waiting for transfers between devices  21 us (41%)
  starting transfers between devices  20 us (39%)
  Pallas kernels  8.42 us (16%)
  between operations  0.76 us (1%)
  other arithmetic  0.63 us (1%)
    ppermute x21, waiting for transfers between devices, move(): return lax.ppermute(x, ('node', 'local'), pairs)  21 us
    ppermute x21, starting transfers between devices, move(): return lax.ppermute(x, ('node', 'local'), pairs)  20 us
    pallas_call x1, Pallas kernels, exchanged(): pl.pallas_call(load_kernel, out_shape=[pltpu.VMEM((hidden, width), down_w...  3.15 us
    pallas_call x1, Pallas kernels, exchanged(): pl.pallas_call(functools.partial(expert_kernel, groups), out_shape=[jax.S...  2.5 us
  transfers between devices with their start and end apart: 21, of which 10 were waited for; matrix products, arithmetic and copies ran while one was open for 0% of the time, Pallas kernels for 10%

profile of v7, /device:TPU:0, one launch (start us, length us, event | category | flops | bytes accessed | tf_op | source)
XLA Modules:
  0.0 50.9 jit_solution(12002517467794730789)
XLA Ops:
  0.6 1.0 %shard_map.68.refs_8_ = bf16[32,3712]{1,0:T(8,128)(2,1)S(1)} custom-call(bf16[32,3584]{1,0:T(8,128)(2,1)} %rows_hbm.1, s32[8,32]{1,0:T(8,128)} %bitcast.42, bf16[8,32]{1,0:T(8,128)(2,1)} %bitcast.44), custom_call_target="tpu_custom_call" | custom-call | tf_op jit(solution)/shard_map/pallas_call | solution.py:248
  1.6 5.1 %collective-permute-start = (bf16[32,3712]{1,0:T(8,128)(2,1)S(1)}, bf16[32,3712]{1,0:T(8,128)(2,1)S(1)}, u32[]{:S(2)}, u32[]{:S(2)}) collective-permute-start(bf16[32,3712]{1,0:T(8,128)(2,1)S(1)} %shard_map.68.refs_8_), channel_id=1, source_target_pairs={{0,3},{1,2},{2,1},{3,0},{4,7},{5,6},{6,5},{7,4},{8,11},{9,10},{10,... | collective-permute-start | bytes 712712 | tf_op jit(solution)/shard_map/ppermute | solution.py:234
  6.7 0.0 collective-permute-start.4
  6.7 0.6 %collective-permute-start.11 = (bf16[32,3712]{1,0:T(8,128)(2,1)S(1)}, bf16[32,3712]{1,0:T(8,128)(2,1)S(1)}, u32[]{:S(2)}, u32[]{:S(2)}) collective-permute-start(bf16[32,3712]{1,0:T(8,128)(2,1)S(1)} %shard_map.68.refs_8_), channel_id=1, source_target_pairs={{0,2},{1,3},{2,0},{3,1},{4,6},{5,7},{6,4},{7,5},{8,10},{9,11},{10,... | collective-permute-start | bytes 712712 | tf_op jit(solution)/shard_map/ppermute | solution.py:234
  7.4 1.6 %collective-permute-start.9 = (bf16[32,3712]{1,0:T(8,128)(2,1)S(1)}, bf16[32,3712]{1,0:T(8,128)(2,1)S(1)}, u32[]{:S(2)}, u32[]{:S(2)}) collective-permute-start(bf16[32,3712]{1,0:T(8,128)(2,1)S(1)} %shard_map.68.refs_8_), channel_id=1, source_target_pairs={{0,8},{1,9},{2,10},{3,11},{4,12},{5,13},{6,14},{7,15},{8,0},{9,1},... | collective-permute-start | bytes 712712 | tf_op jit(solution)/shard_map/ppermute | solution.py:234
  9.0 4.4 %collective-permute-done.refs_0_ = bf16[32,3712]{1,0:T(8,128)(2,1)S(1)} collective-permute-done((bf16[32,3712]{1,0:T(8,128)(2,1)S(1)}, bf16[32,3712]{1,0:T(8,128)(2,1)S(1)}, u32[]{:S(2)}, u32[]{:S(2)}) %collective-permute-start) | collective-permute-done | bytes 237600 | tf_op jit(solution)/shard_map/ppermute | solution.py:234
  13.4 1.7 %collective-permute-start.2 = (bf16[32,3712]{1,0:T(8,128)(2,1)S(1)}, bf16[32,3712]{1,0:T(8,128)(2,1)S(1)}, u32[]{:S(2)}, u32[]{:S(2)}) collective-permute-start(bf16[32,3712]{1,0:T(8,128)(2,1)S(1)} %collective-permute-done.refs_0_), channel_id=1, source_target_pairs={{0,8},{1,9},{2,10},{3,11},{4,12},{5,13},{6,14},{7,15},{8,0},{9,1},... | collective-permute-start | bytes 712712 | tf_op jit(solution)/shard_map/ppermute | solution.py:234
  15.1 3.6 %collective-permute-done.4.refs_4_ = bf16[32,3712]{1,0:T(8,128)(2,1)S(1)} collective-permute-done((bf16[32,3712]{1,0:T(8,128)(2,1)S(1)}, bf16[32,3712]{1,0:T(8,128)(2,1)S(1)}, u32[]{:S(2)}, u32[]{:S(2)}) %collective-permute-start.4) | collective-permute-done | bytes 237600 | tf_op jit(solution)/shard_map/ppermute | solution.py:234
  18.7 1.4 %collective-permute-start.6 = (bf16[32,3712]{1,0:T(8,128)(2,1)S(1)}, bf16[32,3712]{1,0:T(8,128)(2,1)S(1)}, u32[]{:S(2)}, u32[]{:S(2)}) collective-permute-start(bf16[32,3712]{1,0:T(8,128)(2,1)S(1)} %collective-permute-done.4.refs_4_), channel_id=1, source_target_pairs={{0,8},{1,9},{2,10},{3,11},{4,12},{5,13},{6,14},{7,15},{8,0},{9,1},... | collective-permute-start | bytes 712712 | tf_op jit(solution)/shard_map/ppermute | solution.py:234
  20.1 0.0 collective-permute-start.8
  20.1 6.8 %collective-permute-done.11.refs_5_ = bf16[32,3712]{1,0:T(8,128)(2,1)S(1)} collective-permute-done((bf16[32,3712]{1,0:T(8,128)(2,1)S(1)}, bf16[32,3712]{1,0:T(8,128)(2,1)S(1)}, u32[]{:S(2)}, u32[]{:S(2)}) %collective-permute-start.11) | collective-permute-done | bytes 237600 | tf_op jit(solution)/shard_map/ppermute | solution.py:234
  26.9 1.5 %collective-permute-start.13 = (bf16[32,3712]{1,0:T(8,128)(2,1)S(1)}, bf16[32,3712]{1,0:T(8,128)(2,1)S(1)}, u32[]{:S(2)}, u32[]{:S(2)}) collective-permute-start(bf16[32,3712]{1,0:T(8,128)(2,1)S(1)} %collective-permute-done.11.refs_5_), channel_id=1, source_target_pairs={{0,8},{1,9},{2,10},{3,11},{4,12},{5,13},{6,14},{7,15},{8,0},{9,1},... | collective-permute-start | bytes 712712 | tf_op jit(solution)/shard_map/ppermute | solution.py:234
  28.4 3.1 %shard_map.69 = (bf16[1024,3584]{1,0:T(8,128)(2,1)S(1)}, bf16[256,1024]{1,0:T(8,128)(2,1)S(1)}) custom-call(bf16[1024,3584]{1,0:T(8,128)(2,1)} %bitcast.39, bf16[256,1024]{1,0:T(8,128)(2,1)} %bitcast.41), custom_call_target="tpu_custom_call" | custom-call | flops 1 | bytes 1 | tf_op jit(solution)/shard_map/pallas_call | solution.py:260
  31.6 0.0 collective-permute-done.9.refs_10_
  31.6 0.1 collective-permute-start.10
  31.7 0.0 collective-permute-done.2.refs_2_
  31.7 0.5 collective-permute-start.1
  32.2 0.0 collective-permute-done.6.refs_6_
  32.2 0.1 collective-permute-start.5
  32.3 0.0 collective-permute-done.8.refs_9_
  32.3 0.4 collective-permute-start.3
  32.7 1.1 %collective-permute-done.13.refs_7_ = bf16[32,3712]{1,0:T(8,128)(2,1)S(1)} collective-permute-done((bf16[32,3712]{1,0:T(8,128)(2,1)S(1)}, bf16[32,3712]{1,0:T(8,128)(2,1)S(1)}, u32[]{:S(2)}, u32[]{:S(2)}) %collective-permute-start.13) | collective-permute-done | bytes 237600 | tf_op jit(solution)/shard_map/ppermute | solution.py:234
  33.8 0.0 collective-permute-start.7
  33.8 0.5 collective-permute-start.12
  34.3 0.1 collective-permute-start.14
  34.4 0.0 collective-permute-done.5.refs_5_
  34.4 0.0 collective-permute-done.3.refs_3_
  34.4 0.9 %collective-permute-done.7.refs_7_ = bf16[32,3712]{1,0:T(8,128)(2,1)S(1)} collective-permute-done((bf16[32,3712]{1,0:T(8,128)(2,1)S(1)}, bf16[32,3712]{1,0:T(8,128)(2,1)S(1)}, u32[]{:S(2)}, u32[]{:S(2)}) %collective-permute-start.7) | collective-permute-done | bytes 237600 | tf_op jit(solution)/shard_map/ppermute | solution.py:234
  35.3 0.9 %shard_map.70 = (bf16[256,3584]{1,0:T(8,128)(2,1)S(1)}, f32[192,128]{1,0:T(8,128)S(1)}, f32[192,128]{1,0:T(8,128)S(1)}) custom-call(bf16[32,3712]{1,0:T(8,128)(2,1)S(1)} %collective-permute-done.refs_0_, bf16[32,3712]{1,0:T(8,128)(2,1)S(1)} %collective-permute-done.1.refs_1_, bf16[32,3712]{1,0:T(8,128)(2,1)S(1)} %collective-permute-done.2.refs_2_, ...), custom_call_target="tpu_custom_call" | custom-call | flops 176160768 | bytes 4194304 | tf_op jit(solution)/shard_map/pallas_call | solution.py:281
  36.2 0.0 collective-permute-done.12.refs_6_
  36.2 0.0 collective-permute-done.14.refs_8_
  36.3 2.5 %shard_map.71 = (bf16[256,1024]{1,0:T(8,128)(2,1)S(1)}, f32[1,128]{1,0:T(1,128)S(1)}, f32[1,128]{1,0:T(1,128)S(1)}, f32[1,128]{1,0:T(1,128)S(1)}, f32[1,128]{1,0:T(1,128)S(1)}, /*index=5*/bf16[256,3584]{1,0:T(8,128)(2,1)S(1)}) custom-call(f32[192,128]{1,0:T(8,128)S(1)} %get-tuple-element.24.refs_0_, ...), custom_call_target="tpu_custom_call", output_to_operand_aliasing={{5}: (4, {})} | custom-call | flops 1 | bytes 1 | tf_op jit(solution)/shard_map/pallas_call | solution.py:297
  38.8 2.3 %collective-permute-start.15 = (f32[1,128]{1,0:T(1,128)S(1)}, f32[1,128]{1,0:T(1,128)S(1)}, u32[]{:S(2)}, u32[]{:S(2)}) collective-permute-start(f32[1,128]{1,0:T(1,128)S(1)} %get-tuple-element.30), channel_id=1, source_target_pairs={{0,3},{1,2},{2,1},{3,0},{4,7},{5,6},{6,5},{7,4},{8,11},{9,10},{10,... | collective-permute-start | bytes 1544 | tf_op jit(solution)/shard_map/ppermute | solution.py:234
  41.1 0.0 collective-permute-start.16
  41.1 2.1 %collective-permute-start.17 = (f32[1,128]{1,0:T(1,128)S(1)}, f32[1,128]{1,0:T(1,128)S(1)}, u32[]{:S(2)}, u32[]{:S(2)}) collective-permute-start(f32[1,128]{1,0:T(1,128)S(1)} %get-tuple-element.32), channel_id=1, source_target_pairs={{0,2},{1,3},{2,0},{3,1},{4,6},{5,7},{6,4},{7,5},{8,10},{9,11},{10,... | collective-permute-start | bytes 1544 | tf_op jit(solution)/shard_map/ppermute | solution.py:234
  43.2 0.8 %shard_map.72 = bf16[256,1024]{1,0:T(8,128)(2,1)} custom-call(bf16[256,1024]{1,0:T(8,128)(2,1)S(1)} %get-tuple-element.28.rows_ref), custom_call_target="tpu_custom_call" | custom-call | flops 1 | bytes 1 | tf_op jit(solution)/shard_map/pallas_call | solution.py:309
  44.1 0.1 collective-permute-done.15
  44.2 0.5 collective-permute-done.16
  44.6 0.9 %collective-permute-done.17 = f32[1,128]{1,0:T(1,128)S(1)} collective-permute-done((f32[1,128]{1,0:T(1,128)S(1)}, f32[1,128]{1,0:T(1,128)S(1)}, u32[]{:S(2)}, u32[]{:S(2)}) %collective-permute-start.17) | collective-permute-done | bytes 544 | tf_op jit(solution)/shard_map/ppermute | solution.py:234
  45.6 0.1 collective-permute-start.18
  45.7 1.6 %collective-permute-start.19 = (f32[4,128]{1,0:T(4,128)S(1)}, f32[4,128]{1,0:T(4,128)S(1)}, u32[]{:S(2)}, u32[]{:S(2)}) collective-permute-start(f32[4,128]{1,0:T(4,128)S(1)} %pad_maximum_fusion), channel_id=1, source_target_pairs={{0,8},{1,9},{2,10},{3,11},{4,12},{5,13},{6,14},{7,15},{8,0},{9,1},... | collective-permute-start | bytes 6152 | tf_op jit(solution)/shard_map/ppermute | solution.py:234
  47.2 0.3 collective-permute-start.20
  47.5 0.1 slice_bitcast_fusion.11
  47.6 1.7 %collective-permute-done.19 = f32[4,128]{1,0:T(4,128)S(1)} collective-permute-done((f32[4,128]{1,0:T(4,128)S(1)}, f32[4,128]{1,0:T(4,128)S(1)}, u32[]{:S(2)}, u32[]{:S(2)}) %collective-permute-start.19) | collective-permute-done | bytes 2080 | tf_op jit(solution)/shard_map/ppermute | solution.py:234
  49.3 0.1 slice_bitcast_fusion.7
  49.4 0.9 %collective-permute-done.20 = f32[4,128]{1,0:T(4,128)S(1)} collective-permute-done((f32[4,128]{1,0:T(4,128)S(1)}, f32[4,128]{1,0:T(4,128)S(1)}, u32[]{:S(2)}, u32[]{:S(2)}) %collective-permute-start.20) | collective-permute-done | bytes 2080 | tf_op jit(solution)/shard_map/ppermute | solution.py:234
  50.2 0.1 slice_bitcast_fusion.3
  50.3 0.6 %add_bitcast_fusion = f32[32,8]{0,1:T(8,128)} fusion(s32[8,32]{1,0:T(8,128)S(1)} %bitcast.43, f32[32]{0:T(128)S(1)} %get-tuple-element.51, s32[]{:T(128)S(6)} %add.122, f32[32]{0:T(128)S(1)} %get-tuple-element.52, s32[]{:T(128)S(6)} %add.120, f32[32]{0:T(128)S(1)} %get-tuple-element.53, s32[]{:T(128)S(6)} %add.118, f32[32]{0:T(128)S(1)} %get-tuple-element.50, ...), kind=kLoop, calls=%fused_computation | loop fusion | flops 12032 | bytes 4160 | tf_op jit(solution)/shard_map/transpose | solution.py:328
  (7 shorter events, 0.0 us)
Async XLA Ops:
  1.6 11.8 %collective-permute-start = (bf16[32,3712]{1,0:T(8,128)(2,1)S(1)}, bf16[32,3712]{1,0:T(8,128)(2,1)S(1)}, u32[]{:S(2)}, u32[]{:S(2)}) collective-permute-start(bf16[32,3712]{1,0:T(8,128)(2,1)S(1)} %shard_map.68.refs_8_), channel_id=1, source_target_pairs={{0,3},{1,2},{2,1},{3,0},{4,7},{5,6},{6,5},{7,4},{8,11},{9,10},{10,... | collective-permute-start | bytes 712712 | tf_op jit(solution)/shard_map/ppermute | solution.py:234
  6.7 12.0 %collective-permute-start.4 = (bf16[32,3712]{1,0:T(8,128)(2,1)S(1)}, bf16[32,3712]{1,0:T(8,128)(2,1)S(1)}, u32[]{:S(2)}, u32[]{:S(2)}) collective-permute-start(bf16[32,3712]{1,0:T(8,128)(2,1)S(1)} %shard_map.68.refs_8_), channel_id=1, source_target_pairs={{0,1},{1,0},{2,3},{3,2},{4,5},{5,4},{6,7},{7,6},{8,9},{9,8},{10,11... | collective-permute-start | bytes 712712 | tf_op jit(solution)/shard_map/ppermute | solution.py:234
  6.7 20.2 %collective-permute-start.11 = (bf16[32,3712]{1,0:T(8,128)(2,1)S(1)}, bf16[32,3712]{1,0:T(8,128)(2,1)S(1)}, u32[]{:S(2)}, u32[]{:S(2)}) collective-permute-start(bf16[32,3712]{1,0:T(8,128)(2,1)S(1)} %shard_map.68.refs_8_), channel_id=1, source_target_pairs={{0,2},{1,3},{2,0},{3,1},{4,6},{5,7},{6,4},{7,5},{8,10},{9,11},{10,... | collective-permute-start | bytes 712712 | tf_op jit(solution)/shard_map/ppermute | solution.py:234
  7.4 24.2 %collective-permute-start.9 = (bf16[32,3712]{1,0:T(8,128)(2,1)S(1)}, bf16[32,3712]{1,0:T(8,128)(2,1)S(1)}, u32[]{:S(2)}, u32[]{:S(2)}) collective-permute-start(bf16[32,3712]{1,0:T(8,128)(2,1)S(1)} %shard_map.68.refs_8_), channel_id=1, source_target_pairs={{0,8},{1,9},{2,10},{3,11},{4,12},{5,13},{6,14},{7,15},{8,0},{9,1},... | collective-permute-start | bytes 712712 | tf_op jit(solution)/shard_map/ppermute | solution.py:234
  13.4 18.2 %collective-permute-start.2 = (bf16[32,3712]{1,0:T(8,128)(2,1)S(1)}, bf16[32,3712]{1,0:T(8,128)(2,1)S(1)}, u32[]{:S(2)}, u32[]{:S(2)}) collective-permute-start(bf16[32,3712]{1,0:T(8,128)(2,1)S(1)} %collective-permute-done.refs_0_), channel_id=1, source_target_pairs={{0,8},{1,9},{2,10},{3,11},{4,12},{5,13},{6,14},{7,15},{8,0},{9,1},... | collective-permute-start | bytes 712712 | tf_op jit(solution)/shard_map/ppermute | solution.py:234
  18.7 13.4 %collective-permute-start.6 = (bf16[32,3712]{1,0:T(8,128)(2,1)S(1)}, bf16[32,3712]{1,0:T(8,128)(2,1)S(1)}, u32[]{:S(2)}, u32[]{:S(2)}) collective-permute-start(bf16[32,3712]{1,0:T(8,128)(2,1)S(1)} %collective-permute-done.4.refs_4_), channel_id=1, source_target_pairs={{0,8},{1,9},{2,10},{3,11},{4,12},{5,13},{6,14},{7,15},{8,0},{9,1},... | collective-permute-start | bytes 712712 | tf_op jit(solution)/shard_map/ppermute | solution.py:234
  20.1 12.1 %collective-permute-start.8 = (bf16[32,3712]{1,0:T(8,128)(2,1)S(1)}, bf16[32,3712]{1,0:T(8,128)(2,1)S(1)}, u32[]{:S(2)}, u32[]{:S(2)}) collective-permute-start(bf16[32,3712]{1,0:T(8,128)(2,1)S(1)} %shard_map.68.refs_8_), channel_id=1, source_target_pairs={{0,4},{1,5},{2,6},{3,7},{4,0},{5,1},{6,2},{7,3},{8,12},{9,13},{10,... | collective-permute-start | bytes 712712 | tf_op jit(solution)/shard_map/ppermute | solution.py:234
  26.9 6.8 %collective-permute-start.13 = (bf16[32,3712]{1,0:T(8,128)(2,1)S(1)}, bf16[32,3712]{1,0:T(8,128)(2,1)S(1)}, u32[]{:S(2)}, u32[]{:S(2)}) collective-permute-start(bf16[32,3712]{1,0:T(8,128)(2,1)S(1)} %collective-permute-done.11.refs_5_), channel_id=1, source_target_pairs={{0,8},{1,9},{2,10},{3,11},{4,12},{5,13},{6,14},{7,15},{8,0},{9,1},... | collective-permute-start | bytes 712712 | tf_op jit(solution)/shard_map/ppermute | solution.py:234
  31.6 2.2 %collective-permute-start.10 = (bf16[32,3712]{1,0:T(8,128)(2,1)S(1)}, bf16[32,3712]{1,0:T(8,128)(2,1)S(1)}, u32[]{:S(2)}, u32[]{:S(2)}) collective-permute-start(bf16[32,3712]{1,0:T(8,128)(2,1)S(1)} %collective-permute-done.9.refs_10_), channel_id=1, source_target_pairs={{0,4},{1,5},{2,6},{3,7},{4,0},{5,1},{6,2},{7,3},{8,12},{9,13},{10,... | collective-permute-start | bytes 712712 | tf_op jit(solution)/shard_map/ppermute | solution.py:234
  31.7 2.6 %collective-permute-start.1 = (bf16[32,3712]{1,0:T(8,128)(2,1)S(1)}, bf16[32,3712]{1,0:T(8,128)(2,1)S(1)}, u32[]{:S(2)}, u32[]{:S(2)}) collective-permute-start(bf16[32,3712]{1,0:T(8,128)(2,1)S(1)} %collective-permute-done.refs_0_), channel_id=1, source_target_pairs={{0,4},{1,5},{2,6},{3,7},{4,0},{5,1},{6,2},{7,3},{8,12},{9,13},{10,... | collective-permute-start | bytes 712712 | tf_op jit(solution)/shard_map/ppermute | solution.py:234
  32.2 2.2 %collective-permute-start.5 = (bf16[32,3712]{1,0:T(8,128)(2,1)S(1)}, bf16[32,3712]{1,0:T(8,128)(2,1)S(1)}, u32[]{:S(2)}, u32[]{:S(2)}) collective-permute-start(bf16[32,3712]{1,0:T(8,128)(2,1)S(1)} %collective-permute-done.4.refs_4_), channel_id=1, source_target_pairs={{0,4},{1,5},{2,6},{3,7},{4,0},{5,1},{6,2},{7,3},{8,12},{9,13},{10,... | collective-permute-start | bytes 712712 | tf_op jit(solution)/shard_map/ppermute | solution.py:234
  32.3 2.1 %collective-permute-start.3 = (bf16[32,3712]{1,0:T(8,128)(2,1)S(1)}, bf16[32,3712]{1,0:T(8,128)(2,1)S(1)}, u32[]{:S(2)}, u32[]{:S(2)}) collective-permute-start(bf16[32,3712]{1,0:T(8,128)(2,1)S(1)} %collective-permute-done.2.refs_2_), channel_id=1, source_target_pairs={{0,4},{1,5},{2,6},{3,7},{4,0},{5,1},{6,2},{7,3},{8,12},{9,13},{10,... | collective-permute-start | bytes 712712 | tf_op jit(solution)/shard_map/ppermute | solution.py:234
  33.8 1.5 %collective-permute-start.7 = (bf16[32,3712]{1,0:T(8,128)(2,1)S(1)}, bf16[32,3712]{1,0:T(8,128)(2,1)S(1)}, u32[]{:S(2)}, u32[]{:S(2)}) collective-permute-start(bf16[32,3712]{1,0:T(8,128)(2,1)S(1)} %collective-permute-done.6.refs_6_), channel_id=1, source_target_pairs={{0,4},{1,5},{2,6},{3,7},{4,0},{5,1},{6,2},{7,3},{8,12},{9,13},{10,... | collective-permute-start | bytes 712712 | tf_op jit(solution)/shard_map/ppermute | solution.py:234
  33.8 2.5 %collective-permute-start.12 = (bf16[32,3712]{1,0:T(8,128)(2,1)S(1)}, bf16[32,3712]{1,0:T(8,128)(2,1)S(1)}, u32[]{:S(2)}, u32[]{:S(2)}) collective-permute-start(bf16[32,3712]{1,0:T(8,128)(2,1)S(1)} %collective-permute-done.11.refs_5_), channel_id=1, source_target_pairs={{0,4},{1,5},{2,6},{3,7},{4,0},{5,1},{6,2},{7,3},{8,12},{9,13},{10,... | collective-permute-start | bytes 712712 | tf_op jit(solution)/shard_map/ppermute | solution.py:234
  34.3 2.0 %collective-permute-start.14 = (bf16[32,3712]{1,0:T(8,128)(2,1)S(1)}, bf16[32,3712]{1,0:T(8,128)(2,1)S(1)}, u32[]{:S(2)}, u32[]{:S(2)}) collective-permute-start(bf16[32,3712]{1,0:T(8,128)(2,1)S(1)} %collective-permute-done.13.refs_7_), channel_id=1, source_target_pairs={{0,4},{1,5},{2,6},{3,7},{4,0},{5,1},{6,2},{7,3},{8,12},{9,13},{10,... | collective-permute-start | bytes 712712 | tf_op jit(solution)/shard_map/ppermute | solution.py:234
  34.4 16.0 %copy-start = (s32[32,8]{0,1:T(8,128)S(1)}, s32[32,8]{0,1:T(8,128)}, u32[]{:S(2)}) copy-start(s32[32,8]{0,1:T(8,128)} %param.6) | copy-start | bytes 3076
  38.8 5.4 %collective-permute-start.15 = (f32[1,128]{1,0:T(1,128)S(1)}, f32[1,128]{1,0:T(1,128)S(1)}, u32[]{:S(2)}, u32[]{:S(2)}) collective-permute-start(f32[1,128]{1,0:T(1,128)S(1)} %get-tuple-element.30), channel_id=1, source_target_pairs={{0,3},{1,2},{2,1},{3,0},{4,7},{5,6},{6,5},{7,4},{8,11},{9,10},{10,... | collective-permute-start | bytes 1544 | tf_op jit(solution)/shard_map/ppermute | solution.py:234
  41.1 3.5 %collective-permute-start.16 = (f32[1,128]{1,0:T(1,128)S(1)}, f32[1,128]{1,0:T(1,128)S(1)}, u32[]{:S(2)}, u32[]{:S(2)}) collective-permute-start(f32[1,128]{1,0:T(1,128)S(1)} %get-tuple-element.31), channel_id=1, source_target_pairs={{0,1},{1,0},{2,3},{3,2},{4,5},{5,4},{6,7},{7,6},{8,9},{9,8},{10,11... | collective-permute-start | bytes 1544 | tf_op jit(solution)/shard_map/ppermute | solution.py:234
  41.1 4.4 %collective-permute-start.17 = (f32[1,128]{1,0:T(1,128)S(1)}, f32[1,128]{1,0:T(1,128)S(1)}, u32[]{:S(2)}, u32[]{:S(2)}) collective-permute-start(f32[1,128]{1,0:T(1,128)S(1)} %get-tuple-element.32), channel_id=1, source_target_pairs={{0,2},{1,3},{2,0},{3,1},{4,6},{5,7},{6,4},{7,5},{8,10},{9,11},{10,... | collective-permute-start | bytes 1544 | tf_op jit(solution)/shard_map/ppermute | solution.py:234
  45.6 2.0 %collective-permute-start.18 = (f32[4,128]{1,0:T(4,128)S(1)}, f32[4,128]{1,0:T(4,128)S(1)}, u32[]{:S(2)}, u32[]{:S(2)}) collective-permute-start(f32[4,128]{1,0:T(4,128)S(1)} %pad_maximum_fusion), channel_id=1, source_target_pairs={{0,4},{1,5},{2,6},{3,7},{4,0},{5,1},{6,2},{7,3},{8,12},{9,13},{10,... | collective-permute-start | bytes 6152 | tf_op jit(solution)/shard_map/ppermute | solution.py:234
  45.7 3.7 %collective-permute-start.19 = (f32[4,128]{1,0:T(4,128)S(1)}, f32[4,128]{1,0:T(4,128)S(1)}, u32[]{:S(2)}, u32[]{:S(2)}) collective-permute-start(f32[4,128]{1,0:T(4,128)S(1)} %pad_maximum_fusion), channel_id=1, source_target_pairs={{0,8},{1,9},{2,10},{3,11},{4,12},{5,13},{6,14},{7,15},{8,0},{9,1},... | collective-permute-start | bytes 6152 | tf_op jit(solution)/shard_map/ppermute | solution.py:234
  47.2 3.0 %collective-permute-start.20 = (f32[4,128]{1,0:T(4,128)S(1)}, f32[4,128]{1,0:T(4,128)S(1)}, u32[]{:S(2)}, u32[]{:S(2)}) collective-permute-start(f32[4,128]{1,0:T(4,128)S(1)} %pad_maximum_fusion), channel_id=1, source_target_pairs={{0,12},{1,13},{2,14},{3,15},{4,8},{5,9},{6,10},{7,11},{8,4},{9,5},... | collective-permute-start | bytes 6152 | tf_op jit(solution)/shard_map/ppermute | solution.py:234
